TPU v7x, 256 devices: a whole 4x4x8 slice. The times are simulated.
256 devices in a mesh: seq: 64 (over z, x_lo, y), tp: 4 (over x_hi, core).
Axes of the slice: x: 4 (x_hi: 2, x_lo: 2; x = x_hi * 2 + x_lo), y: 4, z: 8, core: 2. Of those that a mesh axis runs over, the one named last changes fastest.
Arguments:
- queries: bfloat16 [2, 4096, 4096], P(None, 'seq', 'tp'), may hold values from -8 to 8
- key_projected: bfloat16 [2, 4096, 512], P(None, 'seq', 'tp'), may hold values from -4 to 4
- values: bfloat16 [2, 4096, 512], P(None, 'seq', 'tp'), may hold values from -6 to 6
- segments: int32 [2, 4096], replicated, may hold values from 0 to 3, never falling along the last dimension, each value on 1 to 2048 neighbouring positions
- out_weight: bfloat16 [4096, 4096], P('tp'), may hold values from -0.09375 to 0.09375
Outputs:
- projected: bfloat16 [2, 4096, 4096], P(None, 'seq')
Inputs may be any that keep to these rules, and one draw needn't show every extreme that they name: `segments`: along each sequence the numbers never fall; a segment spans 1 to 2048 positions and one spans exactly 2048.
All inputs are finite; a program needn't handle non-finite values.
Results may differ from a plain program's by a relative error of at most 0.0058.
Values may be sent and summed in bfloat16 or wider, within the bound.
No kernel may reach another device: no remote copies, remote signals or barrier semaphores. Data moves between devices by JAX's collectives and lax.ppermute only.
A program may use at most 64 MiB of HBM per device.

v0:
```python
import math

import jax
import jax.numpy as jnp
from jax import lax
from jax.sharding import PartitionSpec as P


def attend(query_rows, row_pos, key_rows, value_rows, seg_ids, query_size):
    row_count, head_size = query_rows.shape
    seq_len = key_rows.shape[0]
    key_size = min(512, seq_len)
    factor = 1.0 / math.sqrt(head_size)

    def per_block(pieces):
        query_block, query_pos = pieces
        query_seg = seg_ids[query_pos]
        block_reach = (jnp.max(query_pos) + key_size) // key_size

        def scores_at(block_idx):
            offset = block_idx * key_size
            key_block = lax.dynamic_slice_in_dim(key_rows, offset, key_size)
            key_seg = lax.dynamic_slice_in_dim(seg_ids, offset, key_size)
            key_pos = offset + jnp.arange(key_size, dtype=jnp.int32)
            logits = (
                jnp.einsum("qd,kd->qk", query_block, key_block, preferred_element_type=jnp.float32)
                * factor
            )
            allowed = (key_pos[None, :] <= query_pos[:, None]) & (
                key_seg[None, :] == query_seg[:, None]
            )
            return (jnp.where(allowed, logits, -1e30), allowed)

        def sweep_max(block_idx, state_pair):
            row_top, row_sum = state_pair
            masked, allowed = scores_at(block_idx)
            new_top = jnp.maximum(row_top, jnp.max(masked, axis=1))
            kept_exp = jnp.where(allowed, jnp.exp(masked - new_top[:, None]), 0.0)
            return (new_top, row_sum * jnp.exp(row_top - new_top) + jnp.sum(kept_exp, axis=1))

        start_top = jnp.full((query_size,), -1e30, jnp.float32)
        start_sum = jnp.zeros((query_size,), jnp.float32)
        row_top, row_sum = lax.fori_loop(0, block_reach, sweep_max, (start_top, start_sum))

        def sweep_sum(block_idx, context_sum):
            masked, allowed = scores_at(block_idx)
            kept_exp = jnp.where(allowed, jnp.exp(masked - row_top[:, None]), 0.0)
            weights = (kept_exp / row_sum[:, None]).astype(jnp.bfloat16)
            value_block = lax.dynamic_slice_in_dim(value_rows, block_idx * key_size, key_size)
            return context_sum + jnp.dot(weights, value_block, preferred_element_type=jnp.float32)

        context_sum = lax.fori_loop(
            0, block_reach, sweep_sum, jnp.zeros((query_size, head_size), jnp.float32)
        )
        return context_sum.astype(jnp.bfloat16)

    blocks = lax.map(
        per_block,
        (
            query_rows.reshape(row_count // query_size, query_size, head_size),
            row_pos.reshape(row_count // query_size, query_size),
        ),
    )
    return blocks.reshape(row_count, head_size)


def attend_rows(block_rows):

    def applied(query_rows, row_pos, key_rows, value_rows, seg_ids):
        return attend(query_rows, row_pos, key_rows, value_rows, seg_ids, block_rows)

    return jax.vmap(applied, in_axes=(0, None, 0, 0, 0))


def body(queries, key_projected, values, segments, out_weight):
    batches, local_tok, row_width = queries.shape
    head_size = key_projected.shape[2]
    heads_here = row_width // head_size
    key_all, value_all = (
        lax.all_gather(key_projected, "seq", axis=1, tiled=True),
        lax.all_gather(values, "seq", axis=1, tiled=True),
    )
    row_total = local_tok * heads_here
    query_rows = queries.reshape(batches, row_total, head_size)
    row_pos = (
        lax.axis_index("seq") * local_tok + jnp.arange(row_total, dtype=jnp.int32) // heads_here
    )
    attend_all = attend_rows(min(512, row_total))
    context = attend_all(query_rows, row_pos, key_all, value_all, segments)
    merged_heads = context.reshape(batches, local_tok, row_width)
    partial_sum = jnp.einsum(
        "btw,wf->btf", merged_heads, out_weight, preferred_element_type=jnp.float32
    )
    return lax.psum(partial_sum, "tp").astype(jnp.bfloat16)


def solution(mesh):
    in_specs = (
        P(None, "seq", "tp"),
        P(None, "seq", "tp"),
        P(None, "seq", "tp"),
        P(),
        P("tp", None),
    )
    out_specs = P(None, "seq", None)
    return jax.shard_map(body, mesh=mesh, in_specs=in_specs, out_specs=out_specs, check_vma=False)
```

profile of v0, /device:TPU:243, one launch (start us, length us, event | category | flops | bytes accessed | tf_op | source)
XLA Modules:
  0.0 689.6 jit_solution(1515044343568699959)
XLA Ops:
  6.5 0.7 all-gather.3.cloned.1.call-update
  7.3 0.7 all-gather.5.cloned.1.call-update
  9.3 1.4 copy.9
  10.7 1.0 gather_fusion
  12.1 251.0 %all-gather.3.cloned.1.call-done = bf16[2,4096,128]{2,1,0:T(8,128)(2,1)} async-done(((bf16[2,64,128]{2,1,0:T(8,128)(2,1)}), bf16[2,4096,128]{2,1,0:T(8,128)(2,1)}) %all-gather.3.cloned.1.call-update) | async-done | bytes 2097168 | tf_op jit(solution)/shard_map/all_gather | solution.py:80
  263.1 28.0 %while.40 = (s32[]{:T(128)}, f32[2,512]{1,0:T(2,128)S(1)}, f32[2,512]{1,0:T(2,128)S(1)}, s32[]{:T(128)}, s32[2,4096]{1,0:T(2,128)}, /*index=5*/s32[2,512]{1,0:T(...) while((s32[]{:T(128)}, f32[2,512]{1,0:T(2,128)S(1)}, ...), condition=%wide.region_4.5_spmd.clone, body=%wide.region_1.4_spmd.clone.sunk | while | flops 139729920 | bytes 5591251 | solution.py:43
  264.1 1.7 fusion.59
  265.8 0.7 select_reduce_fusion.2
  266.6 0.7 constant_dynamic-slice_fusion.4
  267.6 1.7 fusion.59
  269.3 0.7 select_reduce_fusion.2
  270.1 0.7 constant_dynamic-slice_fusion.4
  271.1 1.7 fusion.59
  272.8 0.7 select_reduce_fusion.2
  273.6 0.7 constant_dynamic-slice_fusion.4
  274.6 1.7 fusion.59
  276.3 0.7 select_reduce_fusion.2
  277.1 0.7 constant_dynamic-slice_fusion.4
  278.1 1.7 fusion.59
  279.8 0.7 select_reduce_fusion.2
  280.6 0.7 constant_dynamic-slice_fusion.4
  281.6 1.7 fusion.59
  283.3 0.7 select_reduce_fusion.2
  284.1 0.7 constant_dynamic-slice_fusion.4
  285.1 1.7 fusion.59
  286.8 0.7 select_reduce_fusion.2
  287.6 0.7 constant_dynamic-slice_fusion.4
  288.6 1.7 fusion.59
  290.3 0.7 select_reduce_fusion.2
  291.1 270.6 %all-gather.5.cloned.1.call-done = bf16[2,4096,128]{2,1,0:T(8,128)(2,1)} async-done(((bf16[2,64,128]{2,1,0:T(8,128)(2,1)}), bf16[2,4096,128]{2,1,0:T(8,128)(2,1)}) %all-gather.5.cloned.1.call-update) | async-done | bytes 2097168 | tf_op jit(solution)/shard_map/all_gather | solution.py:81
  561.8 27.9 %while.41 = (s32[]{:T(128)}, f32[2,512,128]{2,1,0:T(8,128)S(1)}, s32[]{:T(128)}, s32[2,4096]{1,0:T(2,128)}, s32[2,512]{1,0:T(2,128)S(1)}, /*index=5*/bf16[2,4096...) while((s32[]{:T(128)}, f32[2,512,128]{2,1,0:T(8,128)S(1)}, ...), condition=%wide.region_6.7_spmd.clone, body=%wide.region_5.6_spmd.clone.sunk | while | flops 273028096 | bytes 2393311 | solution.py:52
  561.8 0.7 constant_dynamic-slice_fusion.5
  562.8 2.5 fusion.64
  566.3 2.5 fusion.64
  568.8 0.7 constant_dynamic-slice_fusion.5
  569.8 2.5 fusion.64
  572.2 0.7 constant_dynamic-slice_fusion.5
  573.2 2.5 fusion.64
  575.7 0.7 constant_dynamic-slice_fusion.5
  576.7 2.5 fusion.64
  579.2 0.7 constant_dynamic-slice_fusion.5
  580.2 2.5 fusion.64
  582.7 0.7 constant_dynamic-slice_fusion.5
  583.7 2.5 fusion.64
  586.2 0.7 constant_dynamic-slice_fusion.5
  587.2 2.5 fusion.64
  589.8 4.6 fusion.37
  594.4 88.3 %all-reduce.1 = bf16[2,64,4096]{2,1,0:T(8,128)(2,1)} all-reduce(f32[2,64,4096]{2,1,0:T(8,128)S(1)} %fusion.37), channel_id=1, replica_groups=mesh['seq'=64,'tp'=4] {'tp'}, use_global_device_ids=true, to_apply=%region_7.8 | all-reduce | flops 524288 | bytes 3145728 | tf_op jit(solution)/shard_map/psum | solution.py:94
  (88 shorter events, 7.4 us)
Async XLA Ops:
  6.5 5.4 copy-start
  6.5 256.5 %all-gather.3.cloned.1.call-start = ((), (), s32[]{:S(2)}) async-start(), calls=%async_computation | async-start | bytes 2129920 | tf_op jit(solution)/shard_map/all_gather | solution.py:80
  7.3 554.5 %all-gather.5.cloned.1.call-start = ((), (), s32[]{:S(2)}) async-start(), calls=%async_computation.1 | async-start | bytes 2129920 | tf_op jit(solution)/shard_map/all_gather | solution.py:81
Sparse Core Ops, SparseCore 0:
  9.2 253.8 all-gather.2
  264.9 296.8 all-gather.4
where the time goes:
time: 691 us; the launch traced here: 690 us
  waiting for transfers between devices  523 us (76%)
  blocking collectives  88.3 us (13%)
  matrix products  38 us (5%)
  between operations  14.2 us (2%)
  local copies, waits for them, and re-layouts  13.9 us (2%)
  other arithmetic  11.2 us (2%)
    all_gather x1, waiting for transfers between devices, body(): lax.all_gather(values, 'seq', axis=1, tiled=True)  271 us
    all_gather x1, waiting for transfers between devices, body(): lax.all_gather(key_projected, 'seq', axis=1, tiled=True)  251 us
    psum x1, blocking collectives, body(): return lax.psum(partial_sum, 'tp').astype(jnp.bfloat16)  88.3 us
    dot_general x8, matrix products, sweep_sum(): jnp.dot(weights, value_block, preferred_element_type=jnp.float32)  19.6 us
  transfers between devices with their start and end apart: 2, of which 2 were waited for; matrix products, arithmetic and copies ran while one was open for 4% of the time, Pallas kernels for 0%

commit v1 on v0

v1 whole, which is shorter than its diff:
```python
import functools
import math

import jax
import jax.numpy as jnp
from jax import lax
from jax.experimental import pallas as pl
from jax.experimental.pallas import tpu as pltpu
from jax.sharding import PartitionSpec as P

NZ, NX, NY, NH, NC = 8, 2, 4, 2, 2
AXES = ("seq", "tp")
MASKED = -1e30
NEAR, FAR = (0, 1), (2, 3, 4)


def shift(array, move):
    pairs = []
    for z in range(NZ):
        for x in range(NX):
            for y in range(NY):
                for h in range(NH):
                    for c in range(NC):
                        to = move(z, x, y, h, c)
                        if to is not None:
                            flat = lambda a, b, d, e, f: (((a * NX + b) * NY + d) * NH + e) * NC + f
                            pairs.append((flat(z, x, y, h, c), flat(*to)))
    return lax.ppermute(array, AXES, pairs)


def swap_x(array):
    return shift(array, lambda z, x, y, h, c: (z, 1 - x, y, h, c))


def swap_core(array):
    return shift(array, lambda z, x, y, h, c: (z, x, y, h, 1 - c))


def swap_high(array):
    return shift(array, lambda z, x, y, h, c: (z, x, y, 1 - h, c))


def swap_both(array):
    return shift(array, lambda z, x, y, h, c: (z, 1 - x, y, 1 - h, c))


def shift_z(array, by):
    return shift(array, lambda z, x, y, h, c: (z + by, x, y, h, c) if z + by < NZ else None)


def shift_y(array, by):
    return shift(array, lambda z, x, y, h, c: (z, x, (y + by) % NY, h, c))


def row_limits(info, rows, block):
    z, x, y = info[0], info[1], info[2]
    row = lax.broadcasted_iota(jnp.int32, (rows, 1), 0)
    layer = block * NX * NY
    own = z * layer + x * (block * NY) + y * block
    other = z * layer + (1 - x) * (block * NY) + y * block
    last = jnp.where(row < block, own + row, other + row - block)
    first = jnp.zeros_like(last)
    for at in range(4):
        start = info[4 + at]
        first = jnp.where(start <= last, jnp.maximum(first, start), first)
    return first, last


def key_positions(info, layer_back, column, rows, block):
    z, x = info[0], info[1]
    lane = lax.broadcasted_iota(jnp.int32, (1, rows), 1)
    layer = block * NX * NY
    base = (z - layer_back) * layer + column * block
    own, other = base + x * (block * NY), base + (1 - x) * (block * NY)
    return jnp.where(lane < block, own + lane, other + lane - block)


def bias_of(info, first, last, layers, rows, block):
    parts = []
    for back in (0, 1, 3, 2):
        column = lax.rem(info[2] + NY - back, NY)
        tiles = []
        for layer_back in layers:
            at = key_positions(info, layer_back, column, rows, block)
            tiles.append(jnp.where((at >= first) & (at <= last), 0.0, MASKED))
        parts.append(jnp.concatenate(tiles, axis=1))
    return parts


def attend_tiles(query, kv_refs, bias, top, scale):
    scores = []
    for ref, part in zip(kv_refs, bias):
        keys = ref[0].reshape(-1, query.shape[1])
        raw = lax.dot_general(query, keys, (((1,), (1,)), ((), ())), preferred_element_type=jnp.float32)
        scores.append(raw + part)
    highest = functools.reduce(jnp.maximum, [jnp.max(s, axis=1, keepdims=True) for s in scores])
    if top is not None:
        highest = jnp.maximum(highest, top)
    total, mixed = 0.0, 0.0
    for ref, s in zip(kv_refs, scores):
        kept = jnp.exp2((s - highest) * scale)
        total = total + jnp.sum(kept, axis=1, keepdims=True)
        rows = ref[1].reshape(-1, query.shape[1])
        mixed = mixed + jnp.dot(kept.astype(jnp.bfloat16), rows, preferred_element_type=jnp.float32)
    return highest, total, mixed


def head_query(own_ref, other_ref, head, size):
    at = slice(head * size, (head + 1) * size)
    return jnp.concatenate([own_ref[:, at], other_ref[:, at]], axis=0)


def near_kernel(heads, size, block, info, own_ref, other_ref, k0, k1, k2, k3, mixed_ref, stat_ref):
    scale = math.log2(math.e) / math.sqrt(size)
    rows = 2 * block
    first, last = row_limits(info, rows, block)
    bias = bias_of(info, first, last, NEAR, rows, block)
    lane = lax.broadcasted_iota(jnp.int32, (rows, 128), 1)
    stats = jnp.zeros((rows, 128), jnp.float32)
    for head in range(heads):
        query = head_query(own_ref, other_ref, head, size)
        highest, total, mixed = attend_tiles(query, (k0, k1, k2, k3), bias, None, scale)
        mixed_ref[:, head * size:(head + 1) * size] = mixed
        stats = jnp.where(lane == head, highest, stats)
        stats = jnp.where(lane == heads + head, total, stats)
    stat_ref[...] = stats


def far_kernel(heads, size, block, info, own_ref, other_ref, k0, k1, k2, k3, mixed_ref, stat_ref, weight_hbm,
               keep_ref, give_ref, weight, context, sem):
    copy = pltpu.make_async_copy(weight_hbm, weight, sem)
    copy.start()
    scale = math.log2(math.e) / math.sqrt(size)
    rows = 2 * block
    first, last = row_limits(info, rows, block)
    bias = bias_of(info, first, last, FAR, rows, block)
    stats = stat_ref[...]
    for head in range(heads):
        at = slice(head * size, (head + 1) * size)
        query = head_query(own_ref, other_ref, head, size)
        old_top, old_total = stats[:, head:head + 1], stats[:, heads + head:heads + head + 1]
        highest, total, mixed = attend_tiles(query, (k0, k1, k2, k3), bias, old_top, scale)
        fade = jnp.exp2((old_top - highest) * scale)
        mixed = mixed + mixed_ref[:, at] * fade
        total = total + old_total * fade
        context[:, at] = (mixed / total).astype(jnp.bfloat16)
    copy.wait()
    half = keep_ref.shape[1]
    core = info[3]
    mine = pl.ds(pl.multiple_of(core * half, 128), half)
    theirs = pl.ds(pl.multiple_of((1 - core) * half, 128), half)
    give_ref[...] = jnp.dot(context[...], weight[:, theirs], preferred_element_type=jnp.float32).astype(jnp.bfloat16)
    keep_ref[...] = jnp.dot(context[...], weight[:, mine], preferred_element_type=jnp.float32)


def body(queries, key_projected, values, segments, out_weight):
    _, block, width = queries.shape
    size = key_projected.shape[2]
    heads = width // size
    features = out_weight.shape[1]
    rows = 2 * block
    seq, tp = lax.axis_index("seq"), lax.axis_index("tp")
    z, x, y = seq // (NX * NY), (seq // NY) % NX, seq % NY
    high, core = tp // NC, tp % NC
    batch = x ^ high

    pair = jnp.stack([key_projected, values], axis=1)
    pick = lambda a, i: lax.dynamic_index_in_dim(a, i, 0, keepdims=False)
    unit = jnp.concatenate([pick(pair, batch), swap_x(pick(pair, 1 - batch))], axis=1)
    own_q = pick(queries, batch)
    other_q = swap_x(pick(queries, 1 - batch))

    seg = pick(segments, batch)
    starts = jnp.sum((seg[None, :] < jnp.arange(4, dtype=jnp.int32)[:, None]).astype(jnp.int32), axis=1)
    info = jnp.concatenate([jnp.stack([z, x, y, core]).astype(jnp.int32), starts])

    near = jnp.stack([unit, shift_z(unit, 1)], axis=1)
    near_all = [near] + [shift_y(near, by) for by in (1, 3, 2)]
    far = jnp.concatenate([shift_z(near, 2), shift_z(unit, 4)[:, None]], axis=1)
    far_all = [far] + [shift_y(far, by) for by in (1, 3, 2)]

    smem = pl.BlockSpec(memory_space=pltpu.SMEM)
    vmem = pl.BlockSpec(memory_space=pltpu.VMEM)
    mixed, stats = pl.pallas_call(
        functools.partial(near_kernel, heads, size, block),
        out_shape=(
            jax.ShapeDtypeStruct((rows, width), jnp.float32),
            jax.ShapeDtypeStruct((rows, 128), jnp.float32),
        ),
        in_specs=[smem] + [vmem] * 6,
        out_specs=(vmem, vmem),
        compiler_params=pltpu.CompilerParams(vmem_limit_bytes=32 * 1024 * 1024),
        cost_estimate=pl.CostEstimate(flops=4 * rows * width * 8 * rows, bytes_accessed=2 << 20, transcendentals=heads * rows * 8 * rows),
    )(info, own_q, other_q, *near_all)
    keep, give = pl.pallas_call(
        functools.partial(far_kernel, heads, size, block),
        out_shape=(
            jax.ShapeDtypeStruct((rows, features // 2), jnp.float32),
            jax.ShapeDtypeStruct((rows, features // 2), jnp.bfloat16),
        ),
        in_specs=[smem] + [vmem] * 8 + [pl.BlockSpec(memory_space=pl.ANY)],
        out_specs=(vmem, vmem),
        scratch_shapes=[
            pltpu.VMEM(out_weight.shape, jnp.bfloat16),
            pltpu.VMEM((rows, width), jnp.bfloat16),
            pltpu.SemaphoreType.DMA,
        ],
        compiler_params=pltpu.CompilerParams(vmem_limit_bytes=40 * 1024 * 1024),
    )(info, own_q, other_q, *far_all, mixed, stats, out_weight)

    summed = keep + swap_core(give).astype(jnp.float32)
    final = (summed[:block] + swap_both(summed[block:].astype(jnp.bfloat16)).astype(jnp.float32)).astype(jnp.bfloat16)
    other = swap_high(final)
    final_far, other_far = swap_core(final), swap_core(other)
    left = jnp.where(core == 0, jnp.stack([final, other]), jnp.stack([final_far, other_far]))
    right = jnp.where(core == 0, jnp.stack([final_far, other_far]), jnp.stack([final, other]))
    whole = jnp.concatenate([left, right], axis=2)
    return jnp.where(batch == 0, whole, whole[::-1])


def solution(mesh):
    in_specs = (
        P(None, "seq", "tp"),
        P(None, "seq", "tp"),
        P(None, "seq", "tp"),
        P(),
        P("tp", None),
    )
    return jax.shard_map(body, mesh=mesh, in_specs=in_specs, out_specs=P(None, "seq", None), check_vma=False)
```

time: 691 us -> 80 us (0.12)
  the two profiles are of different devices: /device:TPU:243 before, /device:TPU:1 now
where the time goes in v1:
time: 80 us; the launch traced here: 79.7 us
  starting transfers between devices  38.1 us (48%)
  waiting for transfers between devices  23.5 us (29%)
  Pallas kernels  11 us (14%)
  local copies, waits for them, and re-layouts  4.55 us (6%)
  other arithmetic  2.52 us (3%)
    ppermute x16, starting transfers between devices, shift(): return lax.ppermute(array, AXES, pairs)  38.1 us
    ppermute x16, waiting for transfers between devices, shift(): return lax.ppermute(array, AXES, pairs)  23.5 us
    pallas_call x1, Pallas kernels, body(): pl.pallas_call(functools.partial(far_kernel, heads, size, block), out_sha...  7.39 us
    pallas_call x1, Pallas kernels, body(): pl.pallas_call(functools.partial(near_kernel, heads, size, block), out_sh...  3.56 us
    unnamed x4, local copies, waits for them, and re-layouts  3.39 us
  transfers between devices with their start and end apart: 16, of which 10 were waited for; matrix products, arithmetic and copies ran while one was open for 2% of the time, Pallas kernels for 4%

profile of v1, /device:TPU:1, one launch (start us, length us, event | category | flops | bytes accessed | tf_op | source)
XLA Modules:
  0.0 79.7 jit_solution(4871027508042721122)
XLA Ops:
  0.0 0.0 copy-start
  0.0 0.8 fusion.4
  0.8 2.1 %collective-permute-start.1 = (bf16[2,64,128]{2,1,0:T(8,128)(2,1)S(1)}, bf16[2,64,128]{2,1,0:T(8,128)(2,1)S(1)}, u32[]{:S(2)}, u32[]{:S(2)}) collective-permute-start(bf16[2,64,128]{2,1,0:T(8,128)(2,1)S(1)} %get-tuple-element.20), channel_id=1, source_target_pairs={{0,16},{1,17},{2,18},{3,19},{4,20},{5,21},{6,22},{7,23},{8,24},{9,... | collective-permute-start | bytes 98312 | tf_op jit(solution)/shard_map/ppermute | solution.py:28
  2.9 1.3 %collective-permute-done.1 = bf16[2,64,128]{2,1,0:T(8,128)(2,1)S(1)} collective-permute-done((bf16[2,64,128]{2,1,0:T(8,128)(2,1)S(1)}, bf16[2,64,128]{2,1,0:T(8,128)(2,1)S(1)}, u32[]{:S(2)}, u32[]{:S(2)}) %collective-permute-start.1) | collective-permute-done | bytes 32800 | tf_op jit(solution)/shard_map/ppermute | solution.py:28
  4.2 3.8 %collective-permute-start.2 = (bf16[2,128,128]{2,1,0:T(8,128)(2,1)S(1)}, bf16[2,128,128]{2,1,0:T(8,128)(2,1)S(1)}, u32[]{:S(2)}, u32[]{:S(2)}) collective-permute-start(bf16[2,128,128]{2,1,0:T(8,128)(2,1)S(1)} %get-tuple-element.18), channel_id=1, source_target_pairs={{0,32},{1,33},{2,34},{3,35},{4,36},{5,37},{6,38},{7,39},{8,40},{9,... | collective-permute-start | bytes 196616 | tf_op jit(solution)/shard_map/ppermute | solution.py:28
  8.0 1.3 %collective-permute-done.2 = bf16[2,128,128]{2,1,0:T(8,128)(2,1)S(1)} collective-permute-done((bf16[2,128,128]{2,1,0:T(8,128)(2,1)S(1)}, bf16[2,128,128]{2,1,0:T(8,128)(2,1)S(1)}, u32[]{:S(2)}, u32[]{:S(2)}) %collective-permute-start.2) | collective-permute-done | bytes 65568 | tf_op jit(solution)/shard_map/ppermute | solution.py:28
  9.4 5.0 %collective-permute-start.3 = (bf16[2,2,128,128]{3,2,0,1:T(8,128)(2,1)S(1)}, bf16[2,2,128,128]{3,2,0,1:T(8,128)(2,1)S(1)}, u32[]{:S(2)}, u32[]{:S(2)}) collective-permute-start(bf16[2,2,128,128]{3,2,0,1:T(8,128)(2,1)S(1)} %pad_maximum_fusion.4), channel_id=1, source_target_pairs={{0,64},{1,65},{2,66},{3,67},{4,68},{5,69},{6,70},{7,71},{8,72},{9,... | collective-permute-start | bytes 393224 | tf_op jit(solution)/shard_map/ppermute | solution.py:28
  14.4 7.0 %collective-permute-start.4 = (bf16[2,128,128]{2,1,0:T(8,128)(2,1)S(1)}, bf16[2,128,128]{2,1,0:T(8,128)(2,1)S(1)}, u32[]{:S(2)}, u32[]{:S(2)}) collective-permute-start(bf16[2,128,128]{2,1,0:T(8,128)(2,1)S(1)} %get-tuple-element.18), channel_id=1, source_target_pairs={{0,128},{1,129},{2,130},{3,131},{4,132},{5,133},{6,134},{7,135},{8... | collective-permute-start | bytes 196616 | tf_op jit(solution)/shard_map/ppermute | solution.py:28
  21.5 1.0 %dynamic-slice_bitcast_fusion = (bf16[64,1024]{1,0:T(8,128)(2,1)S(1)}, bf16[64,1024]{1,0:T(8,128)(2,1)S(1)}) fusion(bf16[2,64,1024]{2,1,0:T(8,128)(2,1)} %param.5, s32[]{:T(128)S(6)} %select_n.66, s32[]{:T(128)S(6)} %select_n.65), kind=kLoop, calls=%fused_computation.12 | loop fusion | bytes 524296 | tf_op jit(solution)/shard_map/jit(dynamic_index_in_dim)/squeeze | solution.py:168
  22.5 1.3 %collective-permute-start = (bf16[64,1024]{1,0:T(8,128)(2,1)S(1)}, bf16[64,1024]{1,0:T(8,128)(2,1)S(1)}, u32[]{:S(2)}, u32[]{:S(2)}) collective-permute-start(bf16[64,1024]{1,0:T(8,128)(2,1)S(1)} %get-tuple-element.15), channel_id=1, source_target_pairs={{0,16},{1,17},{2,18},{3,19},{4,20},{5,21},{6,22},{7,23},{8,24},{9,... | collective-permute-start | bytes 393224 | tf_op jit(solution)/shard_map/ppermute | solution.py:28
  23.8 2.9 %collective-permute-start.10 = (bf16[2,2,128,128]{3,2,0,1:T(8,128)(2,1)S(1)}, bf16[2,2,128,128]{3,2,0,1:T(8,128)(2,1)S(1)}, u32[]{:S(2)}, u32[]{:S(2)}) collective-permute-start(bf16[2,2,128,128]{3,2,0,1:T(8,128)(2,1)S(1)} %pad_maximum_fusion.4), channel_id=1, source_target_pairs={{0,8},{1,9},{2,10},{3,11},{4,12},{5,13},{6,14},{7,15},{8,0},{9,1},... | collective-permute-start | bytes 393224 | tf_op jit(solution)/shard_map/ppermute | solution.py:28
  26.7 0.8 collective-permute-start.9
  27.5 0.0 collective-permute-done.4
  27.5 0.7 collective-permute-start.8
  28.2 0.0 collective-permute-done.3
  28.2 0.8 %collective-permute-start.7 = (bf16[2,3,128,128]{3,2,1,0:T(8,128)(2,1)S(1)}, bf16[2,3,128,128]{3,2,1,0:T(8,128)(2,1)S(1)}, u32[]{:S(2)}, u32[]{:S(2)}) collective-permute-start(bf16[2,3,128,128]{3,2,1,0:T(8,128)(2,1)S(1)} %pad_maximum_fusion.3.k0), channel_id=1, source_target_pairs={{0,8},{1,9},{2,10},{3,11},{4,12},{5,13},{6,14},{7,15},{8,0},{9,1},... | collective-permute-start | bytes 589832 | tf_op jit(solution)/shard_map/ppermute | solution.py:28
  29.0 0.1 collective-permute-done.10
  29.1 2.8 %collective-permute-start.6 = (bf16[2,3,128,128]{3,2,1,0:T(8,128)(2,1)S(1)}, bf16[2,3,128,128]{3,2,1,0:T(8,128)(2,1)S(1)}, u32[]{:S(2)}, u32[]{:S(2)}) collective-permute-start(bf16[2,3,128,128]{3,2,1,0:T(8,128)(2,1)S(1)} %pad_maximum_fusion.3.k0), channel_id=1, source_target_pairs={{0,12},{1,13},{2,14},{3,15},{4,0},{5,1},{6,2},{7,3},{8,4},{9,5},{1... | collective-permute-start | bytes 589832 | tf_op jit(solution)/shard_map/ppermute | solution.py:28
  31.9 0.0 collective-permute-done.9
  31.9 0.0 collective-permute-start.5
  31.9 0.0 copy-done
  32.0 0.1 convert_reduce_fusion
  32.1 0.1 concatenate.12.info
  32.3 3.3 %collective-permute-done.8 = bf16[2,2,128,128]{3,2,0,1:T(8,128)(2,1)S(1)} collective-permute-done((bf16[2,2,128,128]{3,2,0,1:T(8,128)(2,1)S(1)}, bf16[2,2,128,128]{3,2,0,1:T(8,128)(2,1)S(1)}, u32[]{:S(2)}, u32[]{:S(2)}) %collective-permute-start.8) | collective-permute-done | bytes 131104 | tf_op jit(solution)/shard_map/ppermute | solution.py:28
  35.6 0.0 collective-permute-done.other_ref
  35.6 3.6 %shard_map.55 = (f32[128,1024]{1,0:T(8,128)S(1)}, f32[128,128]{1,0:T(8,128)S(1)}) custom-call(s32[8]{0:T(128)S(1)} %concatenate.12.info, bf16[64,1024]{1,0:T(8,128)(2,1)S(1)} %get-tuple-element.16.own_ref, bf16[64,1024]{1,0:T(8,128)(2,1)S(1)} %collective-permute-done.other_ref, bf16[2,2,128,128]{3,2,1,0:T(8,128)(2,1)S(1)} %copy.12.k0, ...), custom_call_target="tpu_custom_call" | custom-call | flops 536870912 | bytes 2097152 | tf_op jit(solution)/shard_map/pallas_call | solution.py:184
  39.1 0.0 collective-permute-done.7.k3
  39.2 0.9 %collective-permute-done.6.k2 = bf16[2,3,128,128]{3,2,1,0:T(8,128)(2,1)S(1)} collective-permute-done((bf16[2,3,128,128]{3,2,1,0:T(8,128)(2,1)S(1)}, bf16[2,3,128,128]{3,2,1,0:T(8,128)(2,1)S(1)}, u32[]{:S(2)}, u32[]{:S(2)}) %collective-permute-start.6) | collective-permute-done | bytes 196640 | tf_op jit(solution)/shard_map/ppermute | solution.py:28
  40.1 1.5 %collective-permute-done.5.k1 = bf16[2,3,128,128]{3,2,1,0:T(8,128)(2,1)S(1)} collective-permute-done((bf16[2,3,128,128]{3,2,1,0:T(8,128)(2,1)S(1)}, bf16[2,3,128,128]{3,2,1,0:T(8,128)(2,1)S(1)}, u32[]{:S(2)}, u32[]{:S(2)}) %collective-permute-start.5) | collective-permute-done | bytes 196640 | tf_op jit(solution)/shard_map/ppermute | solution.py:28
  41.6 0.0 copy-start.1
  41.6 3.4 %copy-done.1 = bf16[1024,4096]{1,0:T(8,128)(2,1)S(1)} copy-done((bf16[1024,4096]{1,0:T(8,128)(2,1)S(1)}, bf16[1024,4096]{1,0:T(8,128)(2,1)}, u32[]{:S(2)}) %copy-start.1) | copy-done | bytes 8388632
  45.0 7.4 %shard_map.56 = (f32[128,2048]{1,0:T(8,128)S(1)}, bf16[128,2048]{1,0:T(8,128)(2,1)S(1)}) custom-call(s32[8]{0:T(128)S(1)} %concatenate.12.info, bf16[64,1024]{1,0:T(8,128)(2,1)S(1)} %get-tuple-element.16.own_ref, bf16[64,1024]{1,0:T(8,128)(2,1)S(1)} %collective-permute-done.other_ref, bf16[2,3,128,128]{3,2,1,0:T(8,128)(2,1)S(1)} %pad_maximum_fusion.3.k0, ...), custom_call_target="tpu_custom_call" | custom-call | tf_op jit(solution)/shard_map/pallas_call | solution.py:195
  52.4 3.9 %collective-permute-start.11 = (bf16[128,2048]{1,0:T(8,128)(2,1)S(1)}, bf16[128,2048]{1,0:T(8,128)(2,1)S(1)}, u32[]{:S(2)}, u32[]{:S(2)}) collective-permute-start(bf16[128,2048]{1,0:T(8,128)(2,1)S(1)} %get-tuple-element.12), channel_id=1, source_target_pairs={{0,1},{1,0},{2,3},{3,2},{4,5},{5,4},{6,7},{7,6},{8,9},{9,8},{10,11... | collective-permute-start | bytes 1572872 | tf_op jit(solution)/shard_map/ppermute | solution.py:28
  56.3 1.5 %collective-permute-done.11 = bf16[128,2048]{1,0:T(8,128)(2,1)S(1)} collective-permute-done((bf16[128,2048]{1,0:T(8,128)(2,1)S(1)}, bf16[128,2048]{1,0:T(8,128)(2,1)S(1)}, u32[]{:S(2)}, u32[]{:S(2)}) %collective-permute-start.11) | collective-permute-done | bytes 524320 | tf_op jit(solution)/shard_map/ppermute | solution.py:28
  57.9 0.1 convert_add_fusion
  58.0 1.9 %collective-permute-start.12 = (bf16[64,2048]{1,0:T(8,128)(2,1)S(1)}, bf16[64,2048]{1,0:T(8,128)(2,1)S(1)}, u32[]{:S(2)}, u32[]{:S(2)}) collective-permute-start(bf16[64,2048]{1,0:T(8,128)(2,1)S(1)} %slice.15), channel_id=1, source_target_pairs={{0,18},{1,19},{2,16},{3,17},{4,22},{5,23},{6,20},{7,21},{8,26},{9,... | collective-permute-start | bytes 786440 | tf_op jit(solution)/shard_map/ppermute | solution.py:28
  59.9 6.9 %collective-permute-done.12 = bf16[64,2048]{1,0:T(8,128)(2,1)S(1)} collective-permute-done((bf16[64,2048]{1,0:T(8,128)(2,1)S(1)}, bf16[64,2048]{1,0:T(8,128)(2,1)S(1)}, u32[]{:S(2)}, u32[]{:S(2)}) %collective-permute-start.12) | collective-permute-done | bytes 262176 | tf_op jit(solution)/shard_map/ppermute | solution.py:28
  66.9 1.3 %collective-permute-start.13 = (bf16[64,2048]{1,0:T(8,128)(2,1)S(1)}, bf16[64,2048]{1,0:T(8,128)(2,1)S(1)}, u32[]{:S(2)}, u32[]{:S(2)}) collective-permute-start(bf16[64,2048]{1,0:T(8,128)(2,1)S(1)} %fusion), channel_id=1, source_target_pairs={{0,2},{1,3},{2,0},{3,1},{4,6},{5,7},{6,4},{7,5},{8,10},{9,11},{10,... | collective-permute-start | bytes 786440 | tf_op jit(solution)/shard_map/ppermute | solution.py:28
  68.2 1.5 %collective-permute-start.14 = (bf16[64,2048]{1,0:T(8,128)(2,1)S(1)}, bf16[64,2048]{1,0:T(8,128)(2,1)S(1)}, u32[]{:S(2)}, u32[]{:S(2)}) collective-permute-start(bf16[64,2048]{1,0:T(8,128)(2,1)S(1)} %fusion), channel_id=1, source_target_pairs={{0,1},{1,0},{2,3},{3,2},{4,5},{5,4},{6,7},{7,6},{8,9},{9,8},{10,11... | collective-permute-start | bytes 786440 | tf_op jit(solution)/shard_map/ppermute | solution.py:28
  69.7 5.4 %collective-permute-done.13 = bf16[64,2048]{1,0:T(8,128)(2,1)S(1)} collective-permute-done((bf16[64,2048]{1,0:T(8,128)(2,1)S(1)}, bf16[64,2048]{1,0:T(8,128)(2,1)S(1)}, u32[]{:S(2)}, u32[]{:S(2)}) %collective-permute-start.13) | collective-permute-done | bytes 262176 | tf_op jit(solution)/shard_map/ppermute | solution.py:28
  75.1 2.1 %collective-permute-start.15 = (bf16[64,2048]{1,0:T(8,128)(2,1)S(1)}, bf16[64,2048]{1,0:T(8,128)(2,1)S(1)}, u32[]{:S(2)}, u32[]{:S(2)}) collective-permute-start(bf16[64,2048]{1,0:T(8,128)(2,1)S(1)} %collective-permute-done.13), channel_id=1, source_target_pairs={{0,1},{1,0},{2,3},{3,2},{4,5},{5,4},{6,7},{7,6},{8,9},{9,8},{10,11... | collective-permute-start | bytes 786440 | tf_op jit(solution)/shard_map/ppermute | solution.py:28
  77.2 0.0 collective-permute-done.14
  77.2 1.2 %collective-permute-done.15 = bf16[64,2048]{1,0:T(8,128)(2,1)S(1)} collective-permute-done((bf16[64,2048]{1,0:T(8,128)(2,1)S(1)}, bf16[64,2048]{1,0:T(8,128)(2,1)S(1)}, u32[]{:S(2)}, u32[]{:S(2)}) %collective-permute-start.15) | collective-permute-done | bytes 262176 | tf_op jit(solution)/shard_map/ppermute | solution.py:28
  78.3 0.1 broadcast_select_fusion.1
  78.4 0.1 pad_maximum_fusion
  78.5 1.2 %reverse_select_fusion = bf16[2,64,4096]{2,1,0:T(8,128)(2,1)} fusion(bf16[2,64,4096]{2,1,0:T(8,128)(2,1)S(1)} %pad_maximum_fusion, pred[]{:T(512)S(6)} %eq.11), kind=kLoop, calls=%fused_computation | loop fusion | flops 524288 | bytes 2097153 | tf_op jit(solution)/shard_map/jit(_where)/select_n | solution.py:218
  (10 shorter events, 0.2 us)
Async XLA Ops:
  0.0 31.9 %copy-start = (s32[2,4096]{1,0:T(2,128)S(1)}, s32[2,4096]{1,0:T(2,128)}, u32[]{:S(2)}) copy-start(s32[2,4096]{1,0:T(2,128)} %param.8) | copy-start | bytes 98308
  0.8 3.4 %collective-permute-start.1 = (bf16[2,64,128]{2,1,0:T(8,128)(2,1)S(1)}, bf16[2,64,128]{2,1,0:T(8,128)(2,1)S(1)}, u32[]{:S(2)}, u32[]{:S(2)}) collective-permute-start(bf16[2,64,128]{2,1,0:T(8,128)(2,1)S(1)} %get-tuple-element.20), channel_id=1, source_target_pairs={{0,16},{1,17},{2,18},{3,19},{4,20},{5,21},{6,22},{7,23},{8,24},{9,... | collective-permute-start | bytes 98312 | tf_op jit(solution)/shard_map/ppermute | solution.py:28
  4.2 5.1 %collective-permute-start.2 = (bf16[2,128,128]{2,1,0:T(8,128)(2,1)S(1)}, bf16[2,128,128]{2,1,0:T(8,128)(2,1)S(1)}, u32[]{:S(2)}, u32[]{:S(2)}) collective-permute-start(bf16[2,128,128]{2,1,0:T(8,128)(2,1)S(1)} %get-tuple-element.18), channel_id=1, source_target_pairs={{0,32},{1,33},{2,34},{3,35},{4,36},{5,37},{6,38},{7,39},{8,40},{9,... | collective-permute-start | bytes 196616 | tf_op jit(solution)/shard_map/ppermute | solution.py:28
  9.4 18.8 %collective-permute-start.3 = (bf16[2,2,128,128]{3,2,0,1:T(8,128)(2,1)S(1)}, bf16[2,2,128,128]{3,2,0,1:T(8,128)(2,1)S(1)}, u32[]{:S(2)}, u32[]{:S(2)}) collective-permute-start(bf16[2,2,128,128]{3,2,0,1:T(8,128)(2,1)S(1)} %pad_maximum_fusion.4), channel_id=1, source_target_pairs={{0,64},{1,65},{2,66},{3,67},{4,68},{5,69},{6,70},{7,71},{8,72},{9,... | collective-permute-start | bytes 393224 | tf_op jit(solution)/shard_map/ppermute | solution.py:28
  14.4 13.0 %collective-permute-start.4 = (bf16[2,128,128]{2,1,0:T(8,128)(2,1)S(1)}, bf16[2,128,128]{2,1,0:T(8,128)(2,1)S(1)}, u32[]{:S(2)}, u32[]{:S(2)}) collective-permute-start(bf16[2,128,128]{2,1,0:T(8,128)(2,1)S(1)} %get-tuple-element.18), channel_id=1, source_target_pairs={{0,128},{1,129},{2,130},{3,131},{4,132},{5,133},{6,134},{7,135},{8... | collective-permute-start | bytes 196616 | tf_op jit(solution)/shard_map/ppermute | solution.py:28
  22.5 13.1 %collective-permute-start = (bf16[64,1024]{1,0:T(8,128)(2,1)S(1)}, bf16[64,1024]{1,0:T(8,128)(2,1)S(1)}, u32[]{:S(2)}, u32[]{:S(2)}) collective-permute-start(bf16[64,1024]{1,0:T(8,128)(2,1)S(1)} %get-tuple-element.15), channel_id=1, source_target_pairs={{0,16},{1,17},{2,18},{3,19},{4,20},{5,21},{6,22},{7,23},{8,24},{9,... | collective-permute-start | bytes 393224 | tf_op jit(solution)/shard_map/ppermute | solution.py:28
  23.8 5.3 %collective-permute-start.10 = (bf16[2,2,128,128]{3,2,0,1:T(8,128)(2,1)S(1)}, bf16[2,2,128,128]{3,2,0,1:T(8,128)(2,1)S(1)}, u32[]{:S(2)}, u32[]{:S(2)}) collective-permute-start(bf16[2,2,128,128]{3,2,0,1:T(8,128)(2,1)S(1)} %pad_maximum_fusion.4), channel_id=1, source_target_pairs={{0,8},{1,9},{2,10},{3,11},{4,12},{5,13},{6,14},{7,15},{8,0},{9,1},... | collective-permute-start | bytes 393224 | tf_op jit(solution)/shard_map/ppermute | solution.py:28
  26.7 5.2 %collective-permute-start.9 = (bf16[2,2,128,128]{3,2,0,1:T(8,128)(2,1)S(1)}, bf16[2,2,128,128]{3,2,0,1:T(8,128)(2,1)S(1)}, u32[]{:S(2)}, u32[]{:S(2)}) collective-permute-start(bf16[2,2,128,128]{3,2,0,1:T(8,128)(2,1)S(1)} %pad_maximum_fusion.4), channel_id=1, source_target_pairs={{0,12},{1,13},{2,14},{3,15},{4,0},{5,1},{6,2},{7,3},{8,4},{9,5},{1... | collective-permute-start | bytes 393224 | tf_op jit(solution)/shard_map/ppermute | solution.py:28
  27.5 8.1 %collective-permute-start.8 = (bf16[2,2,128,128]{3,2,0,1:T(8,128)(2,1)S(1)}, bf16[2,2,128,128]{3,2,0,1:T(8,128)(2,1)S(1)}, u32[]{:S(2)}, u32[]{:S(2)}) collective-permute-start(bf16[2,2,128,128]{3,2,0,1:T(8,128)(2,1)S(1)} %pad_maximum_fusion.4), channel_id=1, source_target_pairs={{0,4},{1,5},{2,6},{3,7},{4,8},{5,9},{6,10},{7,11},{8,12},{9,13},{1... | collective-permute-start | bytes 393224 | tf_op jit(solution)/shard_map/ppermute | solution.py:28
  28.2 11.0 %collective-permute-start.7 = (bf16[2,3,128,128]{3,2,1,0:T(8,128)(2,1)S(1)}, bf16[2,3,128,128]{3,2,1,0:T(8,128)(2,1)S(1)}, u32[]{:S(2)}, u32[]{:S(2)}) collective-permute-start(bf16[2,3,128,128]{3,2,1,0:T(8,128)(2,1)S(1)} %pad_maximum_fusion.3.k0), channel_id=1, source_target_pairs={{0,8},{1,9},{2,10},{3,11},{4,12},{5,13},{6,14},{7,15},{8,0},{9,1},... | collective-permute-start | bytes 589832 | tf_op jit(solution)/shard_map/ppermute | solution.py:28
  29.1 11.0 %collective-permute-start.6 = (bf16[2,3,128,128]{3,2,1,0:T(8,128)(2,1)S(1)}, bf16[2,3,128,128]{3,2,1,0:T(8,128)(2,1)S(1)}, u32[]{:S(2)}, u32[]{:S(2)}) collective-permute-start(bf16[2,3,128,128]{3,2,1,0:T(8,128)(2,1)S(1)} %pad_maximum_fusion.3.k0), channel_id=1, source_target_pairs={{0,12},{1,13},{2,14},{3,15},{4,0},{5,1},{6,2},{7,3},{8,4},{9,5},{1... | collective-permute-start | bytes 589832 | tf_op jit(solution)/shard_map/ppermute | solution.py:28
  31.9 9.7 %collective-permute-start.5 = (bf16[2,3,128,128]{3,2,1,0:T(8,128)(2,1)S(1)}, bf16[2,3,128,128]{3,2,1,0:T(8,128)(2,1)S(1)}, u32[]{:S(2)}, u32[]{:S(2)}) collective-permute-start(bf16[2,3,128,128]{3,2,1,0:T(8,128)(2,1)S(1)} %pad_maximum_fusion.3.k0), channel_id=1, source_target_pairs={{0,4},{1,5},{2,6},{3,7},{4,8},{5,9},{6,10},{7,11},{8,12},{9,13},{1... | collective-permute-start | bytes 589832 | tf_op jit(solution)/shard_map/ppermute | solution.py:28
  41.6 3.4 %copy-start.1 = (bf16[1024,4096]{1,0:T(8,128)(2,1)S(1)}, bf16[1024,4096]{1,0:T(8,128)(2,1)}, u32[]{:S(2)}) copy-start(bf16[1024,4096]{1,0:T(8,128)(2,1)} %weight_hbm.1) | copy-start | bytes 25165828
  52.4 5.4 %collective-permute-start.11 = (bf16[128,2048]{1,0:T(8,128)(2,1)S(1)}, bf16[128,2048]{1,0:T(8,128)(2,1)S(1)}, u32[]{:S(2)}, u32[]{:S(2)}) collective-permute-start(bf16[128,2048]{1,0:T(8,128)(2,1)S(1)} %get-tuple-element.12), channel_id=1, source_target_pairs={{0,1},{1,0},{2,3},{3,2},{4,5},{5,4},{6,7},{7,6},{8,9},{9,8},{10,11... | collective-permute-start | bytes 1572872 | tf_op jit(solution)/shard_map/ppermute | solution.py:28
  58.0 8.8 %collective-permute-start.12 = (bf16[64,2048]{1,0:T(8,128)(2,1)S(1)}, bf16[64,2048]{1,0:T(8,128)(2,1)S(1)}, u32[]{:S(2)}, u32[]{:S(2)}) collective-permute-start(bf16[64,2048]{1,0:T(8,128)(2,1)S(1)} %slice.15), channel_id=1, source_target_pairs={{0,18},{1,19},{2,16},{3,17},{4,22},{5,23},{6,20},{7,21},{8,26},{9,... | collective-permute-start | bytes 786440 | tf_op jit(solution)/shard_map/ppermute | solution.py:28
  66.9 8.2 %collective-permute-start.13 = (bf16[64,2048]{1,0:T(8,128)(2,1)S(1)}, bf16[64,2048]{1,0:T(8,128)(2,1)S(1)}, u32[]{:S(2)}, u32[]{:S(2)}) collective-permute-start(bf16[64,2048]{1,0:T(8,128)(2,1)S(1)} %fusion), channel_id=1, source_target_pairs={{0,2},{1,3},{2,0},{3,1},{4,6},{5,7},{6,4},{7,5},{8,10},{9,11},{10,... | collective-permute-start | bytes 786440 | tf_op jit(solution)/shard_map/ppermute | solution.py:28
  68.2 9.0 %collective-permute-start.14 = (bf16[64,2048]{1,0:T(8,128)(2,1)S(1)}, bf16[64,2048]{1,0:T(8,128)(2,1)S(1)}, u32[]{:S(2)}, u32[]{:S(2)}) collective-permute-start(bf16[64,2048]{1,0:T(8,128)(2,1)S(1)} %fusion), channel_id=1, source_target_pairs={{0,1},{1,0},{2,3},{3,2},{4,5},{5,4},{6,7},{7,6},{8,9},{9,8},{10,11... | collective-permute-start | bytes 786440 | tf_op jit(solution)/shard_map/ppermute | solution.py:28
  75.1 3.3 %collective-permute-start.15 = (bf16[64,2048]{1,0:T(8,128)(2,1)S(1)}, bf16[64,2048]{1,0:T(8,128)(2,1)S(1)}, u32[]{:S(2)}, u32[]{:S(2)}) collective-permute-start(bf16[64,2048]{1,0:T(8,128)(2,1)S(1)} %collective-permute-done.13), channel_id=1, source_target_pairs={{0,1},{1,0},{2,3},{3,2},{4,5},{5,4},{6,7},{7,6},{8,9},{9,8},{10,11... | collective-permute-start | bytes 786440 | tf_op jit(solution)/shard_map/ppermute | solution.py:28

commit v2 on v1

v2 whole, which is shorter than its diff:
```python
import functools
import math

import jax
import jax.numpy as jnp
from jax import lax
from jax.experimental import pallas as pl
from jax.experimental.pallas import tpu as pltpu
from jax.sharding import PartitionSpec as P

NZ, NX, NY, NH, NC = 8, 2, 4, 2, 2
AXES = ("seq", "tp")
MASKED = -1e30
NEAR, FAR = (0, 1), (2, 3, 4)
GROUP = 2


def shift(array, move):
    pairs = []
    for z in range(NZ):
        for x in range(NX):
            for y in range(NY):
                for h in range(NH):
                    for c in range(NC):
                        flat = lambda a, b, d, e, f: (((a * NX + b) * NY + d) * NH + e) * NC + f
                        pairs.append((flat(z, x, y, h, c), flat(*move(z, x, y, h, c))))
    return lax.ppermute(array, AXES, pairs)


def swap_x(array):
    return shift(array, lambda z, x, y, h, c: (z, 1 - x, y, h, c))


def swap_core(array):
    return shift(array, lambda z, x, y, h, c: (z, x, y, h, 1 - c))


def swap_high(array):
    return shift(array, lambda z, x, y, h, c: (z, x, y, 1 - h, c))


def swap_both(array):
    return shift(array, lambda z, x, y, h, c: (z, 1 - x, y, 1 - h, c))


def shift_z(array, by):
    return shift(array, lambda z, x, y, h, c: ((z + by) % NZ, x, y, h, c))


def shift_y(array, by):
    return shift(array, lambda z, x, y, h, c: (z, x, (y + by) % NY, h, c))


def row_limits(info, rows, block):
    z, x, y = info[0], info[1], info[2]
    row = lax.broadcasted_iota(jnp.int32, (rows, 1), 0)
    layer = block * NX * NY
    own = z * layer + x * (block * NY) + y * block
    other = z * layer + (1 - x) * (block * NY) + y * block
    last = jnp.where(row < block, own + row, other + row - block)
    first = jnp.zeros_like(last)
    for at in range(4):
        start = info[4 + at]
        first = jnp.where(start <= last, jnp.maximum(first, start), first)
    return first, last


def key_positions(info, layer_back, column, rows, block):
    z, x = info[0], info[1]
    lane = lax.broadcasted_iota(jnp.int32, (1, rows), 1)
    layer = block * NX * NY
    base = (z - layer_back) * layer + column * block
    own, other = base + x * (block * NY), base + (1 - x) * (block * NY)
    return jnp.where(lane < block, own + lane, other + lane - block)


def bias_of(info, first, last, layers, rows, block):
    parts = []
    for back in (0, 1, 3, 2):
        column = lax.rem(info[2] + NY - back, NY)
        tiles = []
        for layer_back in layers:
            at = key_positions(info, layer_back, column, rows, block)
            tiles.append(jnp.where((at >= first) & (at <= last), 0.0, MASKED))
        parts.append(jnp.concatenate(tiles, axis=1))
    return parts


def attend_group(queries, kv_refs, bias, top, scale, heads):
    size = queries.shape[1]
    scores = []
    for ref, part in zip(kv_refs, bias):
        keys = ref[0].reshape(-1, size)
        raw = lax.dot_general(queries, keys, (((1,), (1,)), ((), ())), preferred_element_type=jnp.float32)
        scores.append((raw.reshape(heads, -1, raw.shape[1]) + part[None]).reshape(raw.shape))
    highest = functools.reduce(jnp.maximum, [jnp.max(s, axis=1, keepdims=True) for s in scores])
    if top is not None:
        highest = jnp.maximum(highest, top)
    offset = highest * scale
    total, mixed = 0.0, 0.0
    for ref, s in zip(kv_refs, scores):
        kept = jnp.exp2(s * scale - offset)
        total = total + jnp.sum(kept, axis=1, keepdims=True)
        mixed = mixed + jnp.dot(kept.astype(jnp.bfloat16), ref[1].reshape(-1, size), preferred_element_type=jnp.float32)
    return highest, total, mixed


def group_queries(own_ref, other_ref, heads, size):
    return jnp.concatenate([ref[:, h * size:(h + 1) * size] for h in heads for ref in (own_ref, other_ref)], axis=0)


def load_columns(info, own_half, weight_hbm, weight_ref, sem):
    half = weight_ref.shape[1]
    which = info[3] if own_half else 1 - info[3]
    return pltpu.make_async_copy(weight_hbm.at[:, pl.ds(pl.multiple_of(which * half, half), half)], weight_ref, sem)


def near_kernel(heads, size, block, info, own_ref, other_ref, k0, k1, k2, k3, weight_hbm, mixed_ref, stat_ref, weight_ref, sem):
    copy = load_columns(info, False, weight_hbm, weight_ref, sem)
    copy.start()
    scale = math.log2(math.e) / math.sqrt(size)
    rows = 2 * block
    first, last = row_limits(info, rows, block)
    bias = bias_of(info, first, last, NEAR, rows, block)
    lane = lax.broadcasted_iota(jnp.int32, (rows, 128), 1)
    stats = jnp.zeros((rows, 128), jnp.float32)
    for start in range(0, heads, GROUP):
        group = range(start, start + GROUP)
        queries = group_queries(own_ref, other_ref, group, size)
        highest, total, mixed = attend_group(queries, (k0, k1, k2, k3), bias, None, scale, GROUP)
        for i, head in enumerate(group):
            part = slice(i * rows, (i + 1) * rows)
            mixed_ref[:, head * size:(head + 1) * size] = mixed[part]
            stats = jnp.where(lane == head, highest[part], stats)
            stats = jnp.where(lane == heads + head, total[part], stats)
    stat_ref[...] = stats
    copy.wait()


def far_kernel(heads, size, block, info, own_ref, other_ref, k0, k1, k2, k3, mixed_ref, stat_ref, weight_hbm, context_ref, weight_ref, sem):
    copy = load_columns(info, True, weight_hbm, weight_ref, sem)
    copy.start()
    scale = math.log2(math.e) / math.sqrt(size)
    rows = 2 * block
    first, last = row_limits(info, rows, block)
    bias = bias_of(info, first, last, FAR, rows, block)
    stats = stat_ref[...]
    for start in range(0, heads, GROUP):
        group = range(start, start + GROUP)
        queries = group_queries(own_ref, other_ref, group, size)
        old_top = jnp.concatenate([stats[:, h:h + 1] for h in group], axis=0)
        highest, total, mixed = attend_group(queries, (k0, k1, k2, k3), bias, old_top, scale, GROUP)
        fade = jnp.exp2((old_top - highest) * scale)
        for i, head in enumerate(group):
            part, at = slice(i * rows, (i + 1) * rows), slice(head * size, (head + 1) * size)
            whole = total[part] + stats[:, heads + head:heads + head + 1] * fade[part]
            context_ref[:, at] = ((mixed[part] + mixed_ref[:, at] * fade[part]) / whole).astype(jnp.bfloat16)
    copy.wait()


def project_kernel(context_ref, weight_ref, out_ref):
    out_ref[...] = jnp.dot(context_ref[...], weight_ref[...], preferred_element_type=jnp.float32).astype(out_ref.dtype)


def body(queries, key_projected, values, segments, out_weight):
    _, block, width = queries.shape
    size = key_projected.shape[2]
    heads = width // size
    features = out_weight.shape[1]
    rows = 2 * block
    seq, tp = lax.axis_index("seq"), lax.axis_index("tp")
    z, x, y = seq // (NX * NY), (seq // NY) % NX, seq % NY
    high, core = tp // NC, tp % NC
    batch = x ^ high
    pick = lambda a, i, axis: lax.dynamic_index_in_dim(a, i, axis, keepdims=False)

    pair = jnp.stack([key_projected, values], axis=1)
    unit = jnp.concatenate([pick(pair, batch, 0), swap_x(pick(pair, 1 - batch, 0))], axis=1)
    near = jnp.stack([unit, shift_z(unit, 1)], axis=1)
    far = jnp.stack([shift_z(unit, by) for by in (2, 3, 4)], axis=1)
    near_all = [near] + [shift_y(near, by) for by in (1, 3, 2)]
    far_all = [far] + [shift_y(far, by) for by in (1, 3, 2)]
    own_q = pick(queries, batch, 0)
    other_q = swap_x(pick(queries, 1 - batch, 0))

    seg = pick(segments, batch, 0)
    starts = jnp.sum((seg[None, :] < jnp.arange(4, dtype=jnp.int32)[:, None]).astype(jnp.int32), axis=1)
    info = jnp.concatenate([jnp.stack([z, x, y, core]).astype(jnp.int32), starts])

    smem = pl.BlockSpec(memory_space=pltpu.SMEM)
    vmem = pl.BlockSpec(memory_space=pltpu.VMEM)
    hbm = pl.BlockSpec(memory_space=pltpu.HBM)
    limit = pltpu.CompilerParams(vmem_limit_bytes=24 * 1024 * 1024)
    mixed, stats, weight_given = pl.pallas_call(
        functools.partial(near_kernel, heads, size, block),
        out_shape=(
            jax.ShapeDtypeStruct((rows, width), jnp.float32),
            jax.ShapeDtypeStruct((rows, 128), jnp.float32),
            jax.ShapeDtypeStruct((width, features // 2), jnp.bfloat16),
        ),
        in_specs=[smem] + [vmem] * 6 + [hbm],
        out_specs=(vmem, vmem, vmem),
        scratch_shapes=[pltpu.SemaphoreType.DMA],
        compiler_params=limit,
    )(info, own_q, other_q, *near_all, out_weight)
    context, weight_kept = pl.pallas_call(
        functools.partial(far_kernel, heads, size, block),
        out_shape=(
            jax.ShapeDtypeStruct((rows, width), jnp.bfloat16),
            jax.ShapeDtypeStruct((width, features // 2), jnp.bfloat16),
        ),
        in_specs=[smem] + [vmem] * 8 + [hbm],
        out_specs=(vmem, vmem),
        scratch_shapes=[pltpu.SemaphoreType.DMA],
        compiler_params=limit,
    )(info, own_q, other_q, *far_all, mixed, stats, out_weight)

    def project(weight, dtype):
        return pl.pallas_call(
            project_kernel,
            out_shape=jax.ShapeDtypeStruct((rows, features // 2), dtype),
            in_specs=[vmem, vmem],
            out_specs=vmem,
            compiler_params=limit,
        )(context, weight)

    given = swap_core(project(weight_given, jnp.bfloat16))
    summed = project(weight_kept, jnp.float32) + given.astype(jnp.float32)
    final = (summed[:block] + swap_both(summed[block:].astype(jnp.bfloat16)).astype(jnp.float32)).astype(jnp.bfloat16)
    other = swap_high(final)
    final_far, other_far = swap_core(final), swap_core(other)
    left = jnp.where(core == 0, jnp.stack([final, other]), jnp.stack([final_far, other_far]))
    right = jnp.where(core == 0, jnp.stack([final_far, other_far]), jnp.stack([final, other]))
    whole = jnp.concatenate([left, right], axis=2)
    return jnp.where(batch == 0, whole, whole[::-1])


def solution(mesh):
    in_specs = (
        P(None, "seq", "tp"),
        P(None, "seq", "tp"),
        P(None, "seq", "tp"),
        P(),
        P("tp", None),
    )
    return jax.shard_map(body, mesh=mesh, in_specs=in_specs, out_specs=P(None, "seq", None), check_vma=False)
```

time: 80 us -> 69.9 us (0.87)
  waiting for transfers between devices: 23.5 us -> 17.3 us
  starting transfers between devices: 38.1 us -> 34.8 us
    ppermute x16 -> x17, waiting for transfers between devices: 23.5 us -> 17.3 us  [shift(): return lax.ppermute(array, AXES, pairs)]
    ppermute x16 -> x17, starting transfers between devices: 38.1 us -> 34.8 us  [shift(): return lax.ppermute(array, AXES, pairs)]
    pallas_call x1, Pallas kernels: 7.39 us -> 5.05 us  [body(): pl.pallas_call(functools.partial(far_kernel, heads, size, block), out_sha...]
    pallas_call x0 -> x2, Pallas kernels: none -> 1.45 us  [project(): pl.pallas_call(project_kernel, out_shape=jax.ShapeDtypeStruct((rows, feat...]
    unnamed x4 -> x6, local copies, waits for them, and re-layouts: 3.39 us -> 3.38 us
  transfers between devices with their start and end apart: 16 -> 17, of which waited for: 10 -> 7; matrix products, arithmetic and copies ran while one was open for 2% -> 2% of each run, Pallas kernels for 4% -> 7%
where the time goes in v2:
time: 69.9 us; the launch traced here: 69.7 us
  starting transfers between devices  34.8 us (50%)
  waiting for transfers between devices  17.3 us (25%)
  Pallas kernels  10.3 us (15%)
  local copies, waits for them, and re-layouts  4.54 us (6%)
  other arithmetic  2.54 us (4%)
    ppermute x17, starting transfers between devices, shift(): return lax.ppermute(array, AXES, pairs)  34.8 us
    ppermute x17, waiting for transfers between devices, shift(): return lax.ppermute(array, AXES, pairs)  17.3 us
    pallas_call x1, Pallas kernels, body(): pl.pallas_call(functools.partial(far_kernel, heads, size, block), out_sha...  5.05 us
    pallas_call x1, Pallas kernels, body(): pl.pallas_call(functools.partial(near_kernel, heads, size, block), out_sh...  3.84 us
    unnamed x6, local copies, waits for them, and re-layouts  3.38 us
    pallas_call x2, Pallas kernels, project(): pl.pallas_call(project_kernel, out_shape=jax.ShapeDtypeStruct((rows, feat...  1.45 us
  transfers between devices with their start and end apart: 17, of which 7 were waited for; matrix products, arithmetic and copies ran while one was open for 2% of the time, Pallas kernels for 7%

profile of v2, /device:TPU:1, one launch (start us, length us, event | category | flops | bytes accessed | tf_op | source)
XLA Modules:
  0.0 69.7 jit_solution(14789664844474797338)
XLA Ops:
  0.0 0.8 %fusion.4 = (bf16[2,64,128]{2,1,0:T(8,128)(2,1)S(1)}, bf16[2,64,128]{2,1,0:T(8,128)(2,1)S(1)}) fusion(s32[]{:T(128)S(6)} %select_n.65, bf16[2,1,64,128]{3,2,0,1:T(8,128)(2,1)} %bitcast.38, bf16[2,1,64,128]{3,2,0,1:T(8,128)(2,1)} %bitcast.39, s32[]{:T(128)S(6)} %select_n.66), kind=kLoop, calls=%fused_computation.24 | loop fusion | flops 32768 | bytes 131080 | tf_op jit(solution)/shard_map/jit(dynamic_index_in_dim)/squeeze | solution.py:175
  0.8 2.1 %collective-permute-start.1 = (bf16[2,64,128]{2,1,0:T(8,128)(2,1)S(1)}, bf16[2,64,128]{2,1,0:T(8,128)(2,1)S(1)}, u32[]{:S(2)}, u32[]{:S(2)}) collective-permute-start(bf16[2,64,128]{2,1,0:T(8,128)(2,1)S(1)} %get-tuple-element.22), channel_id=1, source_target_pairs={{0,16},{1,17},{2,18},{3,19},{4,20},{5,21},{6,22},{7,23},{8,24},{9,... | collective-permute-start | bytes 98312 | tf_op jit(solution)/shard_map/ppermute | solution.py:27
  2.9 1.3 %collective-permute-done.1 = bf16[2,64,128]{2,1,0:T(8,128)(2,1)S(1)} collective-permute-done((bf16[2,64,128]{2,1,0:T(8,128)(2,1)S(1)}, bf16[2,64,128]{2,1,0:T(8,128)(2,1)S(1)}, u32[]{:S(2)}, u32[]{:S(2)}) %collective-permute-start.1) | collective-permute-done | bytes 32800 | tf_op jit(solution)/shard_map/ppermute | solution.py:27
  4.2 2.0 %collective-permute-start.8 = (bf16[2,128,128]{2,1,0:T(8,128)(2,1)S(1)}, bf16[2,128,128]{2,1,0:T(8,128)(2,1)S(1)}, u32[]{:S(2)}, u32[]{:S(2)}) collective-permute-start(bf16[2,128,128]{2,1,0:T(8,128)(2,1)S(1)} %get-tuple-element.20), channel_id=1, source_target_pairs={{0,32},{1,33},{2,34},{3,35},{4,36},{5,37},{6,38},{7,39},{8,40},{9,... | collective-permute-start | bytes 196616 | tf_op jit(solution)/shard_map/ppermute | solution.py:27
  6.2 6.0 %collective-permute-start.4 = (bf16[2,128,128]{2,1,0:T(8,128)(2,1)S(1)}, bf16[2,128,128]{2,1,0:T(8,128)(2,1)S(1)}, u32[]{:S(2)}, u32[]{:S(2)}) collective-permute-start(bf16[2,128,128]{2,1,0:T(8,128)(2,1)S(1)} %get-tuple-element.20), channel_id=1, source_target_pairs={{0,128},{1,129},{2,130},{3,131},{4,132},{5,133},{6,134},{7,135},{8... | collective-permute-start | bytes 196616 | tf_op jit(solution)/shard_map/ppermute | solution.py:27
  12.2 1.0 %collective-permute-start.3 = (bf16[2,128,128]{2,1,0:T(8,128)(2,1)S(1)}, bf16[2,128,128]{2,1,0:T(8,128)(2,1)S(1)}, u32[]{:S(2)}, u32[]{:S(2)}) collective-permute-start(bf16[2,128,128]{2,1,0:T(8,128)(2,1)S(1)} %get-tuple-element.20), channel_id=1, source_target_pairs={{0,96},{1,97},{2,98},{3,99},{4,100},{5,101},{6,102},{7,103},{8,104... | collective-permute-start | bytes 196616 | tf_op jit(solution)/shard_map/ppermute | solution.py:27
  13.2 0.2 collective-permute-start.2
  13.4 0.0 collective-permute-done.8
  13.4 3.0 %collective-permute-start.11 = (bf16[2,2,128,128]{3,2,0,1:T(8,128)(2,1)S(1)}, bf16[2,2,128,128]{3,2,0,1:T(8,128)(2,1)S(1)}, u32[]{:S(2)}, u32[]{:S(2)}) collective-permute-start(bf16[2,2,128,128]{3,2,0,1:T(8,128)(2,1)S(1)} %pad_maximum_fusion.4), channel_id=1, source_target_pairs={{0,8},{1,9},{2,10},{3,11},{4,12},{5,13},{6,14},{7,15},{8,0},{9,1},... | collective-permute-start | bytes 393224 | tf_op jit(solution)/shard_map/ppermute | solution.py:27
  16.4 0.8 %collective-permute-start.10 = (bf16[2,2,128,128]{3,2,0,1:T(8,128)(2,1)S(1)}, bf16[2,2,128,128]{3,2,0,1:T(8,128)(2,1)S(1)}, u32[]{:S(2)}, u32[]{:S(2)}) collective-permute-start(bf16[2,2,128,128]{3,2,0,1:T(8,128)(2,1)S(1)} %pad_maximum_fusion.4), channel_id=1, source_target_pairs={{0,12},{1,13},{2,14},{3,15},{4,0},{5,1},{6,2},{7,3},{8,4},{9,5},{1... | collective-permute-start | bytes 393224 | tf_op jit(solution)/shard_map/ppermute | solution.py:27
  17.2 1.0 %dynamic-slice_bitcast_fusion = (bf16[64,1024]{1,0:T(8,128)(2,1)S(1)}, bf16[64,1024]{1,0:T(8,128)(2,1)S(1)}) fusion(bf16[2,64,1024]{2,1,0:T(8,128)(2,1)} %param.5, s32[]{:T(128)S(6)} %select_n.66, s32[]{:T(128)S(6)} %select_n.65), kind=kLoop, calls=%fused_computation.12 | loop fusion | bytes 524296 | tf_op jit(solution)/shard_map/jit(dynamic_index_in_dim)/squeeze | solution.py:175
  18.2 0.0 collective-permute-done.4
  18.2 1.3 %collective-permute-start = (bf16[64,1024]{1,0:T(8,128)(2,1)S(1)}, bf16[64,1024]{1,0:T(8,128)(2,1)S(1)}, u32[]{:S(2)}, u32[]{:S(2)}) collective-permute-start(bf16[64,1024]{1,0:T(8,128)(2,1)S(1)} %get-tuple-element.17), channel_id=1, source_target_pairs={{0,16},{1,17},{2,18},{3,19},{4,20},{5,21},{6,22},{7,23},{8,24},{9,... | collective-permute-start | bytes 393224 | tf_op jit(solution)/shard_map/ppermute | solution.py:27
  19.5 1.5 %collective-permute-done.3 = bf16[2,128,128]{2,1,0:T(8,128)(2,1)S(1)} collective-permute-done((bf16[2,128,128]{2,1,0:T(8,128)(2,1)S(1)}, bf16[2,128,128]{2,1,0:T(8,128)(2,1)S(1)}, u32[]{:S(2)}, u32[]{:S(2)}) %collective-permute-start.3) | collective-permute-done | bytes 65568 | tf_op jit(solution)/shard_map/ppermute | solution.py:27
  21.0 1.3 %collective-permute-start.9 = (bf16[2,2,128,128]{3,2,0,1:T(8,128)(2,1)S(1)}, bf16[2,2,128,128]{3,2,0,1:T(8,128)(2,1)S(1)}, u32[]{:S(2)}, u32[]{:S(2)}) collective-permute-start(bf16[2,2,128,128]{3,2,0,1:T(8,128)(2,1)S(1)} %pad_maximum_fusion.4), channel_id=1, source_target_pairs={{0,4},{1,5},{2,6},{3,7},{4,8},{5,9},{6,10},{7,11},{8,12},{9,13},{1... | collective-permute-start | bytes 393224 | tf_op jit(solution)/shard_map/ppermute | solution.py:27
  22.3 0.0 collective-permute-done.2
  22.3 2.7 %collective-permute-start.7 = (bf16[2,3,128,128]{3,2,1,0:T(8,128)(2,1)S(1)}, bf16[2,3,128,128]{3,2,1,0:T(8,128)(2,1)S(1)}, u32[]{:S(2)}, u32[]{:S(2)}) collective-permute-start(bf16[2,3,128,128]{3,2,1,0:T(8,128)(2,1)S(1)} %pad_maximum_fusion.3.k0), channel_id=1, source_target_pairs={{0,8},{1,9},{2,10},{3,11},{4,12},{5,13},{6,14},{7,15},{8,0},{9,1},... | collective-permute-start | bytes 589832 | tf_op jit(solution)/shard_map/ppermute | solution.py:27
  25.0 0.0 collective-permute-done.11
  25.0 1.1 %collective-permute-start.6 = (bf16[2,3,128,128]{3,2,1,0:T(8,128)(2,1)S(1)}, bf16[2,3,128,128]{3,2,1,0:T(8,128)(2,1)S(1)}, u32[]{:S(2)}, u32[]{:S(2)}) collective-permute-start(bf16[2,3,128,128]{3,2,1,0:T(8,128)(2,1)S(1)} %pad_maximum_fusion.3.k0), channel_id=1, source_target_pairs={{0,12},{1,13},{2,14},{3,15},{4,0},{5,1},{6,2},{7,3},{8,4},{9,5},{1... | collective-permute-start | bytes 589832 | tf_op jit(solution)/shard_map/ppermute | solution.py:27
  26.1 0.0 collective-permute-done.10
  26.1 0.4 collective-permute-start.5
  26.5 0.1 convert_reduce_fusion
  26.7 0.1 concatenate.9.info
  26.8 0.0 collective-permute-done.9
  26.9 0.0 collective-permute-done.other_ref
  26.9 0.0 copy-start.1
  26.9 3.4 %copy-done.1 = bf16[1024,4096]{1,0:T(8,128)(2,1)S(1)} copy-done((bf16[1024,4096]{1,0:T(8,128)(2,1)S(1)}, bf16[1024,4096]{1,0:T(8,128)(2,1)}, u32[]{:S(2)}) %copy-start.1) | copy-done | bytes 8388632
  30.3 3.8 %shard_map.55 = (f32[128,1024]{1,0:T(8,128)S(1)}, f32[128,128]{1,0:T(8,128)S(1)}, bf16[1024,2048]{1,0:T(8,128)(2,1)S(1)}) custom-call(s32[8]{0:T(128)S(1)} %concatenate.9.info, bf16[64,1024]{1,0:T(8,128)(2,1)S(1)} %get-tuple-element.18.own_ref, bf16[64,1024]{1,0:T(8,128)(2,1)S(1)} %collective-permute-done.other_ref, bf16[2,2,128,128]{3,2,1,0:T(8,128)(2,1)S(1)} %copy.14.k0, ...), custom_call_target="tpu_custom_call" | custom-call | tf_op jit(solution)/shard_map/pallas_call | solution.py:194
  34.1 0.0 collective-permute-done.6.k2
  34.1 1.2 %collective-permute-done.5.k1 = bf16[2,3,128,128]{3,2,1,0:T(8,128)(2,1)S(1)} collective-permute-done((bf16[2,3,128,128]{3,2,1,0:T(8,128)(2,1)S(1)}, bf16[2,3,128,128]{3,2,1,0:T(8,128)(2,1)S(1)}, u32[]{:S(2)}, u32[]{:S(2)}) %collective-permute-start.5) | collective-permute-done | bytes 196640 | tf_op jit(solution)/shard_map/ppermute | solution.py:27
  35.3 5.1 %shard_map.56 = (bf16[128,1024]{1,0:T(8,128)(2,1)S(1)}, bf16[1024,2048]{1,0:T(8,128)(2,1)S(1)}) custom-call(s32[8]{0:T(128)S(1)} %concatenate.9.info, bf16[64,1024]{1,0:T(8,128)(2,1)S(1)} %get-tuple-element.18.own_ref, bf16[64,1024]{1,0:T(8,128)(2,1)S(1)} %collective-permute-done.other_ref, bf16[2,3,128,128]{3,2,1,0:T(8,128)(2,1)S(1)} %pad_maximum_fusion.3.k0, ...), custom_call_target="tpu_custom_call" | custom-call | tf_op jit(solution)/shard_map/pallas_call | solution.py:206
  40.4 0.7 %shard_map.58 = bf16[128,2048]{1,0:T(8,128)(2,1)S(1)} custom-call(bf16[128,1024]{1,0:T(8,128)(2,1)S(1)} %get-tuple-element.12.context_ref, bf16[1024,2048]{1,0:T(8,128)(2,1)S(1)} %get-tuple-element.14.weight_ref), custom_call_target="tpu_custom_call" | custom-call | tf_op jit(solution)/shard_map/pallas_call | solution.py:219
  41.1 5.1 %collective-permute-start.12 = (bf16[128,2048]{1,0:T(8,128)(2,1)S(1)}, bf16[128,2048]{1,0:T(8,128)(2,1)S(1)}, u32[]{:S(2)}, u32[]{:S(2)}) collective-permute-start(bf16[128,2048]{1,0:T(8,128)(2,1)S(1)} %shard_map.58), channel_id=1, source_target_pairs={{0,1},{1,0},{2,3},{3,2},{4,5},{5,4},{6,7},{7,6},{8,9},{9,8},{10,11... | collective-permute-start | bytes 1572872 | tf_op jit(solution)/shard_map/ppermute | solution.py:27
  46.2 0.7 %shard_map.57 = f32[128,2048]{1,0:T(8,128)S(1)} custom-call(bf16[128,1024]{1,0:T(8,128)(2,1)S(1)} %get-tuple-element.12.context_ref, bf16[1024,2048]{1,0:T(8,128)(2,1)S(1)} %get-tuple-element.13.weight_ref), custom_call_target="tpu_custom_call" | custom-call | tf_op jit(solution)/shard_map/pallas_call | solution.py:219
  47.0 0.8 %collective-permute-done.12 = bf16[128,2048]{1,0:T(8,128)(2,1)S(1)} collective-permute-done((bf16[128,2048]{1,0:T(8,128)(2,1)S(1)}, bf16[128,2048]{1,0:T(8,128)(2,1)S(1)}, u32[]{:S(2)}, u32[]{:S(2)}) %collective-permute-start.12) | collective-permute-done | bytes 524320 | tf_op jit(solution)/shard_map/ppermute | solution.py:27
  47.8 0.1 convert_add_fusion
  47.9 2.6 %collective-permute-start.13 = (bf16[64,2048]{1,0:T(8,128)(2,1)S(1)}, bf16[64,2048]{1,0:T(8,128)(2,1)S(1)}, u32[]{:S(2)}, u32[]{:S(2)}) collective-permute-start(bf16[64,2048]{1,0:T(8,128)(2,1)S(1)} %slice.15), channel_id=1, source_target_pairs={{0,18},{1,19},{2,16},{3,17},{4,22},{5,23},{6,20},{7,21},{8,26},{9,... | collective-permute-start | bytes 786440 | tf_op jit(solution)/shard_map/ppermute | solution.py:27
  50.5 6.3 %collective-permute-done.13 = bf16[64,2048]{1,0:T(8,128)(2,1)S(1)} collective-permute-done((bf16[64,2048]{1,0:T(8,128)(2,1)S(1)}, bf16[64,2048]{1,0:T(8,128)(2,1)S(1)}, u32[]{:S(2)}, u32[]{:S(2)}) %collective-permute-start.13) | collective-permute-done | bytes 262176 | tf_op jit(solution)/shard_map/ppermute | solution.py:27
  56.7 0.1 fusion
  56.8 1.6 %collective-permute-start.14 = (bf16[64,2048]{1,0:T(8,128)(2,1)S(1)}, bf16[64,2048]{1,0:T(8,128)(2,1)S(1)}, u32[]{:S(2)}, u32[]{:S(2)}) collective-permute-start(bf16[64,2048]{1,0:T(8,128)(2,1)S(1)} %fusion), channel_id=1, source_target_pairs={{0,2},{1,3},{2,0},{3,1},{4,6},{5,7},{6,4},{7,5},{8,10},{9,11},{10,... | collective-permute-start | bytes 786440 | tf_op jit(solution)/shard_map/ppermute | solution.py:27
  58.4 1.5 %collective-permute-start.15 = (bf16[64,2048]{1,0:T(8,128)(2,1)S(1)}, bf16[64,2048]{1,0:T(8,128)(2,1)S(1)}, u32[]{:S(2)}, u32[]{:S(2)}) collective-permute-start(bf16[64,2048]{1,0:T(8,128)(2,1)S(1)} %fusion), channel_id=1, source_target_pairs={{0,1},{1,0},{2,3},{3,2},{4,5},{5,4},{6,7},{7,6},{8,9},{9,8},{10,11... | collective-permute-start | bytes 786440 | tf_op jit(solution)/shard_map/ppermute | solution.py:27
  59.9 5.1 %collective-permute-done.14 = bf16[64,2048]{1,0:T(8,128)(2,1)S(1)} collective-permute-done((bf16[64,2048]{1,0:T(8,128)(2,1)S(1)}, bf16[64,2048]{1,0:T(8,128)(2,1)S(1)}, u32[]{:S(2)}, u32[]{:S(2)}) %collective-permute-start.14) | collective-permute-done | bytes 262176 | tf_op jit(solution)/shard_map/ppermute | solution.py:27
  65.0 2.1 %collective-permute-start.16 = (bf16[64,2048]{1,0:T(8,128)(2,1)S(1)}, bf16[64,2048]{1,0:T(8,128)(2,1)S(1)}, u32[]{:S(2)}, u32[]{:S(2)}) collective-permute-start(bf16[64,2048]{1,0:T(8,128)(2,1)S(1)} %collective-permute-done.14), channel_id=1, source_target_pairs={{0,1},{1,0},{2,3},{3,2},{4,5},{5,4},{6,7},{7,6},{8,9},{9,8},{10,11... | collective-permute-start | bytes 786440 | tf_op jit(solution)/shard_map/ppermute | solution.py:27
  67.1 0.0 collective-permute-done.15
  67.1 1.2 %collective-permute-done.16 = bf16[64,2048]{1,0:T(8,128)(2,1)S(1)} collective-permute-done((bf16[64,2048]{1,0:T(8,128)(2,1)S(1)}, bf16[64,2048]{1,0:T(8,128)(2,1)S(1)}, u32[]{:S(2)}, u32[]{:S(2)}) %collective-permute-start.16) | collective-permute-done | bytes 262176 | tf_op jit(solution)/shard_map/ppermute | solution.py:27
  68.3 0.1 broadcast_select_fusion.1
  68.4 0.1 pad_maximum_fusion
  68.5 1.2 %reverse_select_fusion = bf16[2,64,4096]{2,1,0:T(8,128)(2,1)} fusion(bf16[2,64,4096]{2,1,0:T(8,128)(2,1)S(1)} %pad_maximum_fusion, pred[]{:T(512)S(6)} %eq.11), kind=kLoop, calls=%fused_computation | loop fusion | flops 524288 | bytes 2097153 | tf_op jit(solution)/shard_map/jit(_where)/select_n | solution.py:235
  (14 shorter events, 0.2 us)
Async XLA Ops:
  0.0 26.5 %copy-start = (s32[2,4096]{1,0:T(2,128)S(1)}, s32[2,4096]{1,0:T(2,128)}, u32[]{:S(2)}) copy-start(s32[2,4096]{1,0:T(2,128)} %param.8) | copy-start | bytes 98308
  0.8 3.4 %collective-permute-start.1 = (bf16[2,64,128]{2,1,0:T(8,128)(2,1)S(1)}, bf16[2,64,128]{2,1,0:T(8,128)(2,1)S(1)}, u32[]{:S(2)}, u32[]{:S(2)}) collective-permute-start(bf16[2,64,128]{2,1,0:T(8,128)(2,1)S(1)} %get-tuple-element.22), channel_id=1, source_target_pairs={{0,16},{1,17},{2,18},{3,19},{4,20},{5,21},{6,22},{7,23},{8,24},{9,... | collective-permute-start | bytes 98312 | tf_op jit(solution)/shard_map/ppermute | solution.py:27
  4.2 9.2 %collective-permute-start.8 = (bf16[2,128,128]{2,1,0:T(8,128)(2,1)S(1)}, bf16[2,128,128]{2,1,0:T(8,128)(2,1)S(1)}, u32[]{:S(2)}, u32[]{:S(2)}) collective-permute-start(bf16[2,128,128]{2,1,0:T(8,128)(2,1)S(1)} %get-tuple-element.20), channel_id=1, source_target_pairs={{0,32},{1,33},{2,34},{3,35},{4,36},{5,37},{6,38},{7,39},{8,40},{9,... | collective-permute-start | bytes 196616 | tf_op jit(solution)/shard_map/ppermute | solution.py:27
  6.2 12.0 %collective-permute-start.4 = (bf16[2,128,128]{2,1,0:T(8,128)(2,1)S(1)}, bf16[2,128,128]{2,1,0:T(8,128)(2,1)S(1)}, u32[]{:S(2)}, u32[]{:S(2)}) collective-permute-start(bf16[2,128,128]{2,1,0:T(8,128)(2,1)S(1)} %get-tuple-element.20), channel_id=1, source_target_pairs={{0,128},{1,129},{2,130},{3,131},{4,132},{5,133},{6,134},{7,135},{8... | collective-permute-start | bytes 196616 | tf_op jit(solution)/shard_map/ppermute | solution.py:27
  12.2 8.8 %collective-permute-start.3 = (bf16[2,128,128]{2,1,0:T(8,128)(2,1)S(1)}, bf16[2,128,128]{2,1,0:T(8,128)(2,1)S(1)}, u32[]{:S(2)}, u32[]{:S(2)}) collective-permute-start(bf16[2,128,128]{2,1,0:T(8,128)(2,1)S(1)} %get-tuple-element.20), channel_id=1, source_target_pairs={{0,96},{1,97},{2,98},{3,99},{4,100},{5,101},{6,102},{7,103},{8,104... | collective-permute-start | bytes 196616 | tf_op jit(solution)/shard_map/ppermute | solution.py:27
  13.2 9.1 %collective-permute-start.2 = (bf16[2,128,128]{2,1,0:T(8,128)(2,1)S(1)}, bf16[2,128,128]{2,1,0:T(8,128)(2,1)S(1)}, u32[]{:S(2)}, u32[]{:S(2)}) collective-permute-start(bf16[2,128,128]{2,1,0:T(8,128)(2,1)S(1)} %get-tuple-element.20), channel_id=1, source_target_pairs={{0,64},{1,65},{2,66},{3,67},{4,68},{5,69},{6,70},{7,71},{8,72},{9,... | collective-permute-start | bytes 196616 | tf_op jit(solution)/shard_map/ppermute | solution.py:27
  13.4 11.6 %collective-permute-start.11 = (bf16[2,2,128,128]{3,2,0,1:T(8,128)(2,1)S(1)}, bf16[2,2,128,128]{3,2,0,1:T(8,128)(2,1)S(1)}, u32[]{:S(2)}, u32[]{:S(2)}) collective-permute-start(bf16[2,2,128,128]{3,2,0,1:T(8,128)(2,1)S(1)} %pad_maximum_fusion.4), channel_id=1, source_target_pairs={{0,8},{1,9},{2,10},{3,11},{4,12},{5,13},{6,14},{7,15},{8,0},{9,1},... | collective-permute-start | bytes 393224 | tf_op jit(solution)/shard_map/ppermute | solution.py:27
  16.4 9.7 %collective-permute-start.10 = (bf16[2,2,128,128]{3,2,0,1:T(8,128)(2,1)S(1)}, bf16[2,2,128,128]{3,2,0,1:T(8,128)(2,1)S(1)}, u32[]{:S(2)}, u32[]{:S(2)}) collective-permute-start(bf16[2,2,128,128]{3,2,0,1:T(8,128)(2,1)S(1)} %pad_maximum_fusion.4), channel_id=1, source_target_pairs={{0,12},{1,13},{2,14},{3,15},{4,0},{5,1},{6,2},{7,3},{8,4},{9,5},{1... | collective-permute-start | bytes 393224 | tf_op jit(solution)/shard_map/ppermute | solution.py:27
  18.2 8.7 %collective-permute-start = (bf16[64,1024]{1,0:T(8,128)(2,1)S(1)}, bf16[64,1024]{1,0:T(8,128)(2,1)S(1)}, u32[]{:S(2)}, u32[]{:S(2)}) collective-permute-start(bf16[64,1024]{1,0:T(8,128)(2,1)S(1)} %get-tuple-element.17), channel_id=1, source_target_pairs={{0,16},{1,17},{2,18},{3,19},{4,20},{5,21},{6,22},{7,23},{8,24},{9,... | collective-permute-start | bytes 393224 | tf_op jit(solution)/shard_map/ppermute | solution.py:27
  21.0 5.9 %collective-permute-start.9 = (bf16[2,2,128,128]{3,2,0,1:T(8,128)(2,1)S(1)}, bf16[2,2,128,128]{3,2,0,1:T(8,128)(2,1)S(1)}, u32[]{:S(2)}, u32[]{:S(2)}) collective-permute-start(bf16[2,2,128,128]{3,2,0,1:T(8,128)(2,1)S(1)} %pad_maximum_fusion.4), channel_id=1, source_target_pairs={{0,4},{1,5},{2,6},{3,7},{4,8},{5,9},{6,10},{7,11},{8,12},{9,13},{1... | collective-permute-start | bytes 393224 | tf_op jit(solution)/shard_map/ppermute | solution.py:27
  22.3 11.8 %collective-permute-start.7 = (bf16[2,3,128,128]{3,2,1,0:T(8,128)(2,1)S(1)}, bf16[2,3,128,128]{3,2,1,0:T(8,128)(2,1)S(1)}, u32[]{:S(2)}, u32[]{:S(2)}) collective-permute-start(bf16[2,3,128,128]{3,2,1,0:T(8,128)(2,1)S(1)} %pad_maximum_fusion.3.k0), channel_id=1, source_target_pairs={{0,8},{1,9},{2,10},{3,11},{4,12},{5,13},{6,14},{7,15},{8,0},{9,1},... | collective-permute-start | bytes 589832 | tf_op jit(solution)/shard_map/ppermute | solution.py:27
  25.0 9.1 %collective-permute-start.6 = (bf16[2,3,128,128]{3,2,1,0:T(8,128)(2,1)S(1)}, bf16[2,3,128,128]{3,2,1,0:T(8,128)(2,1)S(1)}, u32[]{:S(2)}, u32[]{:S(2)}) collective-permute-start(bf16[2,3,128,128]{3,2,1,0:T(8,128)(2,1)S(1)} %pad_maximum_fusion.3.k0), channel_id=1, source_target_pairs={{0,12},{1,13},{2,14},{3,15},{4,0},{5,1},{6,2},{7,3},{8,4},{9,5},{1... | collective-permute-start | bytes 589832 | tf_op jit(solution)/shard_map/ppermute | solution.py:27
  26.1 9.2 %collective-permute-start.5 = (bf16[2,3,128,128]{3,2,1,0:T(8,128)(2,1)S(1)}, bf16[2,3,128,128]{3,2,1,0:T(8,128)(2,1)S(1)}, u32[]{:S(2)}, u32[]{:S(2)}) collective-permute-start(bf16[2,3,128,128]{3,2,1,0:T(8,128)(2,1)S(1)} %pad_maximum_fusion.3.k0), channel_id=1, source_target_pairs={{0,4},{1,5},{2,6},{3,7},{4,8},{5,9},{6,10},{7,11},{8,12},{9,13},{1... | collective-permute-start | bytes 589832 | tf_op jit(solution)/shard_map/ppermute | solution.py:27
  26.9 3.4 %copy-start.1 = (bf16[1024,4096]{1,0:T(8,128)(2,1)S(1)}, bf16[1024,4096]{1,0:T(8,128)(2,1)}, u32[]{:S(2)}) copy-start(bf16[1024,4096]{1,0:T(8,128)(2,1)} %weight_hbm.3) | copy-start | bytes 25165828
  30.3 5.1 %copy-start.2 = (bf16[1024,4096]{1,0:T(8,128)(2,1)S(1)}, bf16[1024,4096]{1,0:T(8,128)(2,1)}, u32[]{:S(2)}) copy-start(bf16[1024,4096]{1,0:T(8,128)(2,1)} %weight_hbm.3) | copy-start | bytes 25165828
  41.1 6.7 %collective-permute-start.12 = (bf16[128,2048]{1,0:T(8,128)(2,1)S(1)}, bf16[128,2048]{1,0:T(8,128)(2,1)S(1)}, u32[]{:S(2)}, u32[]{:S(2)}) collective-permute-start(bf16[128,2048]{1,0:T(8,128)(2,1)S(1)} %shard_map.58), channel_id=1, source_target_pairs={{0,1},{1,0},{2,3},{3,2},{4,5},{5,4},{6,7},{7,6},{8,9},{9,8},{10,11... | collective-permute-start | bytes 1572872 | tf_op jit(solution)/shard_map/ppermute | solution.py:27
  47.9 8.8 %collective-permute-start.13 = (bf16[64,2048]{1,0:T(8,128)(2,1)S(1)}, bf16[64,2048]{1,0:T(8,128)(2,1)S(1)}, u32[]{:S(2)}, u32[]{:S(2)}) collective-permute-start(bf16[64,2048]{1,0:T(8,128)(2,1)S(1)} %slice.15), channel_id=1, source_target_pairs={{0,18},{1,19},{2,16},{3,17},{4,22},{5,23},{6,20},{7,21},{8,26},{9,... | collective-permute-start | bytes 786440 | tf_op jit(solution)/shard_map/ppermute | solution.py:27
  56.8 8.2 %collective-permute-start.14 = (bf16[64,2048]{1,0:T(8,128)(2,1)S(1)}, bf16[64,2048]{1,0:T(8,128)(2,1)S(1)}, u32[]{:S(2)}, u32[]{:S(2)}) collective-permute-start(bf16[64,2048]{1,0:T(8,128)(2,1)S(1)} %fusion), channel_id=1, source_target_pairs={{0,2},{1,3},{2,0},{3,1},{4,6},{5,7},{6,4},{7,5},{8,10},{9,11},{10,... | collective-permute-start | bytes 786440 | tf_op jit(solution)/shard_map/ppermute | solution.py:27
  58.4 8.7 %collective-permute-start.15 = (bf16[64,2048]{1,0:T(8,128)(2,1)S(1)}, bf16[64,2048]{1,0:T(8,128)(2,1)S(1)}, u32[]{:S(2)}, u32[]{:S(2)}) collective-permute-start(bf16[64,2048]{1,0:T(8,128)(2,1)S(1)} %fusion), channel_id=1, source_target_pairs={{0,1},{1,0},{2,3},{3,2},{4,5},{5,4},{6,7},{7,6},{8,9},{9,8},{10,11... | collective-permute-start | bytes 786440 | tf_op jit(solution)/shard_map/ppermute | solution.py:27
  65.0 3.3 %collective-permute-start.16 = (bf16[64,2048]{1,0:T(8,128)(2,1)S(1)}, bf16[64,2048]{1,0:T(8,128)(2,1)S(1)}, u32[]{:S(2)}, u32[]{:S(2)}) collective-permute-start(bf16[64,2048]{1,0:T(8,128)(2,1)S(1)} %collective-permute-done.14), channel_id=1, source_target_pairs={{0,1},{1,0},{2,3},{3,2},{4,5},{5,4},{6,7},{7,6},{8,9},{9,8},{10,11... | collective-permute-start | bytes 786440 | tf_op jit(solution)/shard_map/ppermute | solution.py:27

commit v3 on v1

v3 whole, which is shorter than its diff:
```python
import functools
import math

import jax
import jax.numpy as jnp
from jax import lax
from jax.experimental import pallas as pl
from jax.experimental.pallas import tpu as pltpu
from jax.sharding import PartitionSpec as P

NZ, NX, NY, NH, NC = 8, 2, 4, 2, 2
AXES = ("seq", "tp")
MASKED = -1e30
NEAR, FAR = (0, 1, 2), (3, 4)
COLUMNS_BACK = (0, 1, 3, 2)
GROUP = 4
PIECES = 1
LONG = pl.CostEstimate(flops=4 << 30, bytes_accessed=16 << 20, transcendentals=4 << 20)
LIMIT = pltpu.CompilerParams(vmem_limit_bytes=24 * 1024 * 1024)
SMEM = pl.BlockSpec(memory_space=pltpu.SMEM)
VMEM = pl.BlockSpec(memory_space=pltpu.VMEM)
HBM = pl.BlockSpec(memory_space=pl.ANY)


def shift(array, move):
    flat = lambda z, x, y, h, c: (((z * NX + x) * NY + y) * NH + h) * NC + c
    devices = [
        (z, x, y, h, c)
        for z in range(NZ) for x in range(NX) for y in range(NY) for h in range(NH) for c in range(NC)
    ]
    return lax.ppermute(array, AXES, [(flat(*d), flat(*move(*d))) for d in devices])


def swap_x(array):
    return shift(array, lambda z, x, y, h, c: (z, 1 - x, y, h, c))


def swap_core(array):
    return shift(array, lambda z, x, y, h, c: (z, x, y, h, 1 - c))


def swap_high(array):
    return shift(array, lambda z, x, y, h, c: (z, x, y, 1 - h, c))


def swap_both(array):
    return shift(array, lambda z, x, y, h, c: (z, 1 - x, y, 1 - h, c))


def shift_z(array, by):
    return shift(array, lambda z, x, y, h, c: ((z + by) % NZ, x, y, h, c))


def shift_y(array, by):
    return shift(array, lambda z, x, y, h, c: (z, x, (y + by) % NY, h, c))


def row_limits(info, which, block):
    z, x, y = info[0], info[1], info[2]
    base = (z * NX + (1 - x if which else x)) * (NY * block) + y * block
    last = base + lax.broadcasted_iota(jnp.int32, (block, 1), 0)
    first = jnp.zeros_like(last)
    for at in range(4):
        start = info[4 + at]
        first = jnp.where(start <= last, jnp.maximum(first, start), first)
    return first, last


def bias_of(info, which, layers, block):
    z, x, y = info[0], info[1], info[2]
    first, last = row_limits(info, which, block)
    lane = lax.broadcasted_iota(jnp.int32, (1, 2 * block), 1)
    own, other = x * (NY * block), (1 - x) * (NY * block)
    within = jnp.where(lane < block, own + lane, other + lane - block)
    parts = []
    for back in COLUMNS_BACK:
        column = lax.rem(y + NY - back, NY) * block
        tiles = []
        for layer_back in layers:
            at = within + ((z - layer_back) * (NX * NY * block) + column)
            tiles.append(jnp.where((at >= first) & (at <= last), 0.0, MASKED))
        parts.append(jnp.concatenate(tiles, axis=1))
    return parts


def attend_group(queries, kv_refs, bias, top, scale):
    size = queries.shape[1]
    scores = []
    for ref, part in zip(kv_refs, bias):
        keys = ref[0].reshape(-1, size)
        raw = lax.dot_general(queries, keys, (((1,), (1,)), ((), ())), preferred_element_type=jnp.float32)
        scores.append((raw.reshape(GROUP, -1, raw.shape[1]) + part[None]).reshape(raw.shape))
    highest = functools.reduce(jnp.maximum, [jnp.max(s, axis=1, keepdims=True) for s in scores])
    if top is not None:
        highest = jnp.maximum(highest, top)
    offset = highest * scale
    total, mixed = 0.0, 0.0
    for ref, s in zip(kv_refs, scores):
        kept = jnp.exp2(s * scale - offset)
        total = total + jnp.sum(kept, axis=1, keepdims=True)
        mixed = mixed + jnp.dot(kept.astype(jnp.bfloat16), ref[1].reshape(-1, size), preferred_element_type=jnp.float32)
    return highest, total, mixed


def near_kernel(heads, size, block, info, own_ref, other_ref, k0, k1, k2, k3, mixed_ref, stat_ref):
    scale = math.log2(math.e) / math.sqrt(size)
    lane = lax.broadcasted_iota(jnp.int32, (block, 128), 1)
    for which, query_ref in enumerate((own_ref, other_ref)):
        bias = bias_of(info, which, NEAR, block)
        stats = jnp.zeros((block, 128), jnp.float32)
        for start in range(0, heads, GROUP):
            group = range(start, start + GROUP)
            queries = jnp.concatenate([query_ref[:, h * size:(h + 1) * size] for h in group], axis=0)
            highest, total, mixed = attend_group(queries, (k0, k1, k2, k3), bias, None, scale)
            for i, head in enumerate(group):
                part = slice(i * block, (i + 1) * block)
                mixed_ref[which, :, head * size:(head + 1) * size] = mixed[part]
                stats = jnp.where(lane == head, highest[part], stats)
                stats = jnp.where(lane == heads + head, total[part], stats)
        stat_ref[which] = stats


def far_block(heads, size, block, which, info, query_ref, kv_refs, mixed_ref, stat_ref, context_ref):
    scale = math.log2(math.e) / math.sqrt(size)
    bias = bias_of(info, which, FAR, block)
    stats = stat_ref[which]
    for start in range(0, heads, GROUP):
        group = range(start, start + GROUP)
        queries = jnp.concatenate([query_ref[:, h * size:(h + 1) * size] for h in group], axis=0)
        old_top = jnp.concatenate([stats[:, h:h + 1] for h in group], axis=0)
        highest, total, mixed = attend_group(queries, kv_refs, bias, old_top, scale)
        fade = jnp.exp2((old_top - highest) * scale)
        for i, head in enumerate(group):
            part, at = slice(i * block, (i + 1) * block), slice(head * size, (head + 1) * size)
            whole = total[part] + stats[:, heads + head:heads + head + 1] * fade[part]
            context_ref[:, at] = ((mixed[part] + mixed_ref[which, :, at] * fade[part]) / whole).astype(jnp.bfloat16)


def far_kernel(heads, size, block, info, query_ref, k0, k1, k2, k3, mixed_ref, stat_ref, context_ref):
    far_block(heads, size, block, 1, info, query_ref, (k0, k1, k2, k3), mixed_ref, stat_ref, context_ref)


def project(core, own_half, context_ref, weight_ref, out_ref, pieces=1, piece=0):
    width = out_ref.shape[1]
    which = core if own_half else 1 - core
    columns = pl.ds(pl.multiple_of((which * pieces + piece) * width, width), width)
    out_ref[...] = jnp.dot(context_ref[...], weight_ref[:, columns], preferred_element_type=jnp.float32).astype(out_ref.dtype)


def project_kernel(own_half, info, context_ref, weight_ref, out_ref):
    project(info[3], own_half, context_ref, weight_ref, out_ref)


def far_project_kernel(heads, size, block, info, query_ref, k0, k1, k2, k3, mixed_ref, stat_ref, weight_ref, give0_ref, give1_ref, keep_ref, context_ref):
    far_block(heads, size, block, 0, info, query_ref, (k0, k1, k2, k3), mixed_ref, stat_ref, context_ref)
    project(info[3], False, context_ref, weight_ref, give0_ref, 2, 0)
    project(info[3], False, context_ref, weight_ref, give1_ref, 2, 1)
    project(info[3], True, context_ref, weight_ref, keep_ref)


def place_kernel(pieces, info, *refs):
    parts, out_ref, sems = refs[:4 * pieces], refs[-2], refs[-1]
    batch, core = info[8], info[3]
    width = parts[0].shape[1]
    copies = []
    for i, part in enumerate(parts):
        row = 1 - batch if (i // pieces) % 2 else batch
        half = 1 - core if i // pieces >= 2 else core
        at = pl.multiple_of(half * (pieces * width) + (i % pieces) * width, 128)
        copies.append(pltpu.make_async_copy(part, out_ref.at[row, :, pl.ds(at, width)], sems.at[i]))
    for copy in copies:
        copy.start()
    for copy in copies:
        copy.wait()


def body(queries, key_projected, values, segments, out_weight):
    batches, block, width = queries.shape
    size = key_projected.shape[2]
    heads = width // size
    features = out_weight.shape[1]
    seq, tp = lax.axis_index("seq"), lax.axis_index("tp")
    z, x, y = seq // (NX * NY), (seq // NY) % NX, seq % NY
    high, core = tp // NC, tp % NC
    batch = x ^ high
    pick = lambda a, i: lax.dynamic_index_in_dim(a, i, 0, keepdims=False)

    pair = jnp.stack([key_projected, values], axis=1)
    unit = jnp.concatenate([pick(pair, batch), swap_x(pick(pair, 1 - batch))], axis=1)
    back = {0: unit}
    for by in (1, 2, 3, 4):
        back[by] = shift_z(unit, by)
    near = jnp.stack([back[layer] for layer in NEAR], axis=1)
    far = jnp.stack([back[layer] for layer in FAR], axis=1)
    near_all = [near] + [shift_y(near, by) for by in COLUMNS_BACK[1:]]
    far_all = [far] + [shift_y(far, by) for by in COLUMNS_BACK[1:]]
    own_q = pick(queries, batch)
    other_q = swap_x(pick(queries, 1 - batch))

    seg = pick(segments, batch)
    starts = jnp.sum((seg[None, :] < jnp.arange(4, dtype=jnp.int32)[:, None]).astype(jnp.int32), axis=1)
    info = jnp.concatenate([jnp.stack([z, x, y, core]).astype(jnp.int32), starts, batch[None].astype(jnp.int32)])

    mixed, stats = pl.pallas_call(
        functools.partial(near_kernel, heads, size, block),
        out_shape=(
            jax.ShapeDtypeStruct((2, block, width), jnp.float32),
            jax.ShapeDtypeStruct((2, block, 128), jnp.float32),
        ),
        in_specs=[SMEM] + [VMEM] * 6,
        out_specs=(VMEM, VMEM),
        compiler_params=LIMIT,
        cost_estimate=LONG,
    )(info, own_q, other_q, *near_all)

    other_context = pl.pallas_call(
        functools.partial(far_kernel, heads, size, block),
        out_shape=jax.ShapeDtypeStruct((block, width), jnp.bfloat16),
        in_specs=[SMEM] + [VMEM] * 7,
        out_specs=VMEM,
        compiler_params=LIMIT,
        cost_estimate=LONG,
    )(info, other_q, *far_all, mixed, stats)

    def projected(own_half, dtype):
        return pl.pallas_call(
            functools.partial(project_kernel, own_half),
            out_shape=jax.ShapeDtypeStruct((block, features // 2), dtype),
            in_specs=[SMEM, VMEM, VMEM],
            out_specs=VMEM,
            compiler_params=LIMIT,
        )(info, other_context, out_weight)

    def cut(array):
        return jnp.split(array, PIECES, axis=1)

    given = swap_core(projected(False, jnp.bfloat16))
    sent = (projected(True, jnp.float32) + given.astype(jnp.float32)).astype(jnp.bfloat16)
    sent, own_q = lax.optimization_barrier((sent, own_q))
    arrived = [swap_both(piece) for piece in cut(sent)]
    given0, given1, kept = pl.pallas_call(
        functools.partial(far_project_kernel, heads, size, block),
        out_shape=(
            jax.ShapeDtypeStruct((block, features // 4), jnp.bfloat16),
            jax.ShapeDtypeStruct((block, features // 4), jnp.bfloat16),
            jax.ShapeDtypeStruct((block, features // 2), jnp.float32),
        ),
        in_specs=[SMEM] + [VMEM] * 8,
        out_specs=(VMEM, VMEM, VMEM),
        scratch_shapes=[pltpu.VMEM((block, width), jnp.bfloat16)],
        compiler_params=LIMIT,
    )(info, own_q, *far_all, mixed, stats, out_weight)
    given = jnp.concatenate([swap_core(given0), swap_core(given1)], axis=1)
    summed = kept + given.astype(jnp.float32)

    final = [(s + a.astype(jnp.float32)).astype(jnp.bfloat16) for s, a in zip(cut(summed), arrived)]
    other = [swap_high(f) for f in final]

    parts = final + other + [swap_core(f) for f in final] + [swap_core(o) for o in other]
    return pl.pallas_call(
        functools.partial(place_kernel, PIECES),
        out_shape=jax.ShapeDtypeStruct((batches, block, features), jnp.bfloat16),
        in_specs=[SMEM] + [VMEM] * len(parts),
        out_specs=HBM,
        scratch_shapes=[pltpu.SemaphoreType.DMA((len(parts),))],
        compiler_params=LIMIT,
    )(info, *parts)


def solution(mesh):
    in_specs = (
        P(None, "seq", "tp"),
        P(None, "seq", "tp"),
        P(None, "seq", "tp"),
        P(),
        P("tp", None),
    )
    return jax.shard_map(body, mesh=mesh, in_specs=in_specs, out_specs=P(None, "seq", None), check_vma=False)
```

time: 80 us -> 64.3 us (0.80)
  waiting for transfers between devices: 23.5 us -> 13.4 us
  starting transfers between devices: 38.1 us -> 33.2 us
  Pallas kernels: 11 us -> 14.1 us
  local copies, waits for them, and re-layouts: 4.55 us -> 1.56 us
  other arithmetic: 2.52 us -> 1.13 us
    ppermute x16 -> x19, waiting for transfers between devices: 23.5 us -> 13.4 us  [shift(): lax.ppermute(array, AXES, [(flat(*d), flat(*move(*d))) for d in devices])]
    pallas_call x0 -> x4, Pallas kernels: none -> 8.57 us  [the longest x1 4.27 us: body(): pl.pallas_call(functools.partial(far_project_kernel, heads, size, block),...]
    pallas_call x1, Pallas kernels: 7.39 us -> 1.93 us  [body(): pl.pallas_call(functools.partial(far_kernel, heads, size, block), out_sha...]
    ppermute x16 -> x19, starting transfers between devices: 38.1 us -> 33.2 us  [shift(): lax.ppermute(array, AXES, [(flat(*d), flat(*move(*d))) for d in devices])]
    unnamed x4 -> x6, local copies, waits for them, and re-layouts: 3.39 us -> 0.42 us
    select_n x2 -> x0, other arithmetic: 1.29 us -> none  [the longest x1 1.2 us: body(): return jnp.where(batch == 0, whole, whole[::-1])]
  transfers between devices with their start and end apart: 16 -> 19, of which waited for: 10 -> 10; matrix products, arithmetic and copies ran while one was open for 2% -> 2% of each run, Pallas kernels for 4% -> 15%
where the time goes in v3:
time: 64.3 us; the launch traced here: 63.8 us
  starting transfers between devices  33.2 us (52%)
  Pallas kernels  14.1 us (22%)
  waiting for transfers between devices  13.4 us (21%)
  local copies, waits for them, and re-layouts  1.56 us (2%)
  other arithmetic  1.13 us (2%)
    ppermute x19, starting transfers between devices, shift(): lax.ppermute(array, AXES, [(flat(*d), flat(*move(*d))) for d in devices])  33.2 us
    ppermute x19, waiting for transfers between devices, shift(): lax.ppermute(array, AXES, [(flat(*d), flat(*move(*d))) for d in devices])  13.4 us
    pallas_call x1, Pallas kernels, body(): pl.pallas_call(functools.partial(far_project_kernel, heads, size, block),...  4.27 us
    pallas_call x1, Pallas kernels, body(): pl.pallas_call(functools.partial(near_kernel, heads, size, block), out_sh...  3.61 us
    pallas_call x2, Pallas kernels, projected(): pl.pallas_call(functools.partial(project_kernel, own_half), out_shape=jax...  2.76 us
    pallas_call x1, Pallas kernels, body(): pl.pallas_call(functools.partial(far_kernel, heads, size, block), out_sha...  1.93 us
    pallas_call x1, Pallas kernels, body(): pl.pallas_call(functools.partial(place_kernel, PIECES), out_shape=jax.Sha...  1.54 us
  transfers between devices with their start and end apart: 19, of which 10 were waited for; matrix products, arithmetic and copies ran while one was open for 2% of the time, Pallas kernels for 15%

profile of v3, /device:TPU:1, one launch (start us, length us, event | category | flops | bytes accessed | tf_op | source)
XLA Modules:
  0.0 63.8 jit_solution(9617606390399606694)
XLA Ops:
  0.0 0.8 %fusion.3 = (bf16[2,64,128]{2,1,0:T(8,128)(2,1)S(1)}, bf16[2,64,128]{2,1,0:T(8,128)(2,1)S(1)}) fusion(s32[]{:T(128)S(6)} %select_n.43, bf16[2,1,64,128]{3,2,0,1:T(8,128)(2,1)} %bitcast.31, bf16[2,1,64,128]{3,2,0,1:T(8,128)(2,1)} %bitcast.32, s32[]{:T(128)S(6)} %select_n.44), kind=kLoop, calls=%fused_computation.16 | loop fusion | flops 32768 | bytes 131080 | tf_op jit(solution)/shard_map/jit(dynamic_index_in_dim)/squeeze | solution.py:186
  0.8 2.1 %collective-permute-start.1 = (bf16[2,64,128]{2,1,0:T(8,128)(2,1)S(1)}, bf16[2,64,128]{2,1,0:T(8,128)(2,1)S(1)}, u32[]{:S(2)}, u32[]{:S(2)}) collective-permute-start(bf16[2,64,128]{2,1,0:T(8,128)(2,1)S(1)} %get-tuple-element.24), channel_id=1, source_target_pairs={{0,16},{1,17},{2,18},{3,19},{4,20},{5,21},{6,22},{7,23},{8,24},{9,... | collective-permute-start | bytes 98312 | tf_op jit(solution)/shard_map/ppermute | solution.py:31
  2.9 1.0 %dynamic-slice_bitcast_fusion = (bf16[64,1024]{1,0:T(8,128)(2,1)S(1)}, bf16[64,1024]{1,0:T(8,128)(2,1)S(1)}) fusion(bf16[2,64,1024]{2,1,0:T(8,128)(2,1)} %param.5, s32[]{:T(128)S(6)} %select_n.43, s32[]{:T(128)S(6)} %select_n.44), kind=kLoop, calls=%fused_computation.4 | loop fusion | bytes 524296 | tf_op jit(solution)/shard_map/jit(dynamic_index_in_dim)/squeeze | solution.py:186
  3.9 0.1 collective-permute-start
  4.0 0.2 collective-permute-done.1
  4.2 2.0 %collective-permute-start.7 = (bf16[2,128,128]{2,1,0:T(8,128)(2,1)S(1)}, bf16[2,128,128]{2,1,0:T(8,128)(2,1)S(1)}, u32[]{:S(2)}, u32[]{:S(2)}) collective-permute-start(bf16[2,128,128]{2,1,0:T(8,128)(2,1)S(1)} %get-tuple-element.22), channel_id=1, source_target_pairs={{0,32},{1,33},{2,34},{3,35},{4,36},{5,37},{6,38},{7,39},{8,40},{9,... | collective-permute-start | bytes 196616 | tf_op jit(solution)/shard_map/ppermute | solution.py:31
  6.2 3.0 %collective-permute-start.8 = (bf16[2,128,128]{2,1,0:T(8,128)(2,1)S(1)}, bf16[2,128,128]{2,1,0:T(8,128)(2,1)S(1)}, u32[]{:S(2)}, u32[]{:S(2)}) collective-permute-start(bf16[2,128,128]{2,1,0:T(8,128)(2,1)S(1)} %get-tuple-element.22), channel_id=1, source_target_pairs={{0,64},{1,65},{2,66},{3,67},{4,68},{5,69},{6,70},{7,71},{8,72},{9,... | collective-permute-start | bytes 196616 | tf_op jit(solution)/shard_map/ppermute | solution.py:31
  9.2 4.3 %collective-permute-start.3 = (bf16[2,128,128]{2,1,0:T(8,128)(2,1)S(1)}, bf16[2,128,128]{2,1,0:T(8,128)(2,1)S(1)}, u32[]{:S(2)}, u32[]{:S(2)}) collective-permute-start(bf16[2,128,128]{2,1,0:T(8,128)(2,1)S(1)} %get-tuple-element.22), channel_id=1, source_target_pairs={{0,128},{1,129},{2,130},{3,131},{4,132},{5,133},{6,134},{7,135},{8... | collective-permute-start | bytes 196616 | tf_op jit(solution)/shard_map/ppermute | solution.py:31
  13.5 0.0 collective-permute-start.2
  13.5 0.0 collective-permute-done.7
  13.5 0.9 %collective-permute-done.8 = bf16[2,128,128]{2,1,0:T(8,128)(2,1)S(1)} collective-permute-done((bf16[2,128,128]{2,1,0:T(8,128)(2,1)S(1)}, bf16[2,128,128]{2,1,0:T(8,128)(2,1)S(1)}, u32[]{:S(2)}, u32[]{:S(2)}) %collective-permute-start.8) | collective-permute-done | bytes 65568 | tf_op jit(solution)/shard_map/ppermute | solution.py:31
  14.4 3.0 %collective-permute-start.11 = (bf16[2,3,128,128]{3,2,0,1:T(8,128)(2,1)S(1)}, bf16[2,3,128,128]{3,2,0,1:T(8,128)(2,1)S(1)}, u32[]{:S(2)}, u32[]{:S(2)}) collective-permute-start(bf16[2,3,128,128]{3,2,0,1:T(8,128)(2,1)S(1)} %pad_maximum_fusion), channel_id=1, source_target_pairs={{0,8},{1,9},{2,10},{3,11},{4,12},{5,13},{6,14},{7,15},{8,0},{9,1},... | collective-permute-start | bytes 589832 | tf_op jit(solution)/shard_map/ppermute | solution.py:31
  17.4 0.8 %collective-permute-start.10 = (bf16[2,3,128,128]{3,2,0,1:T(8,128)(2,1)S(1)}, bf16[2,3,128,128]{3,2,0,1:T(8,128)(2,1)S(1)}, u32[]{:S(2)}, u32[]{:S(2)}) collective-permute-start(bf16[2,3,128,128]{3,2,0,1:T(8,128)(2,1)S(1)} %pad_maximum_fusion), channel_id=1, source_target_pairs={{0,12},{1,13},{2,14},{3,15},{4,0},{5,1},{6,2},{7,3},{8,4},{9,5},{1... | collective-permute-start | bytes 589832 | tf_op jit(solution)/shard_map/ppermute | solution.py:31
  18.2 0.0 collective-permute-done.3
  18.2 0.8 %collective-permute-start.9 = (bf16[2,3,128,128]{3,2,0,1:T(8,128)(2,1)S(1)}, bf16[2,3,128,128]{3,2,0,1:T(8,128)(2,1)S(1)}, u32[]{:S(2)}, u32[]{:S(2)}) collective-permute-start(bf16[2,3,128,128]{3,2,0,1:T(8,128)(2,1)S(1)} %pad_maximum_fusion), channel_id=1, source_target_pairs={{0,4},{1,5},{2,6},{3,7},{4,8},{5,9},{6,10},{7,11},{8,12},{9,13},{1... | collective-permute-start | bytes 589832 | tf_op jit(solution)/shard_map/ppermute | solution.py:31
  19.0 0.1 convert_reduce_fusion
  19.2 0.1 concatenate.9.info
  19.3 2.5 %collective-permute-done.2 = bf16[2,128,128]{2,1,0:T(8,128)(2,1)S(1)} collective-permute-done((bf16[2,128,128]{2,1,0:T(8,128)(2,1)S(1)}, bf16[2,128,128]{2,1,0:T(8,128)(2,1)S(1)}, u32[]{:S(2)}, u32[]{:S(2)}) %collective-permute-start.2) | collective-permute-done | bytes 65568 | tf_op jit(solution)/shard_map/ppermute | solution.py:31
  21.8 3.0 %collective-permute-start.6 = (bf16[2,2,128,128]{3,2,1,0:T(8,128)(2,1)S(1)}, bf16[2,2,128,128]{3,2,1,0:T(8,128)(2,1)S(1)}, u32[]{:S(2)}, u32[]{:S(2)}) collective-permute-start(bf16[2,2,128,128]{3,2,1,0:T(8,128)(2,1)S(1)} %pad_maximum_fusion.1.k0), channel_id=1, source_target_pairs={{0,8},{1,9},{2,10},{3,11},{4,12},{5,13},{6,14},{7,15},{8,0},{9,1},... | collective-permute-start | bytes 393224 | tf_op jit(solution)/shard_map/ppermute | solution.py:31
  24.8 0.8 %collective-permute-start.5 = (bf16[2,2,128,128]{3,2,1,0:T(8,128)(2,1)S(1)}, bf16[2,2,128,128]{3,2,1,0:T(8,128)(2,1)S(1)}, u32[]{:S(2)}, u32[]{:S(2)}) collective-permute-start(bf16[2,2,128,128]{3,2,1,0:T(8,128)(2,1)S(1)} %pad_maximum_fusion.1.k0), channel_id=1, source_target_pairs={{0,12},{1,13},{2,14},{3,15},{4,0},{5,1},{6,2},{7,3},{8,4},{9,5},{1... | collective-permute-start | bytes 393224 | tf_op jit(solution)/shard_map/ppermute | solution.py:31
  25.6 0.0 collective-permute-done.10
  25.6 0.9 %collective-permute-start.4 = (bf16[2,2,128,128]{3,2,1,0:T(8,128)(2,1)S(1)}, bf16[2,2,128,128]{3,2,1,0:T(8,128)(2,1)S(1)}, u32[]{:S(2)}, u32[]{:S(2)}) collective-permute-start(bf16[2,2,128,128]{3,2,1,0:T(8,128)(2,1)S(1)} %pad_maximum_fusion.1.k0), channel_id=1, source_target_pairs={{0,4},{1,5},{2,6},{3,7},{4,8},{5,9},{6,10},{7,11},{8,12},{9,13},{1... | collective-permute-start | bytes 393224 | tf_op jit(solution)/shard_map/ppermute | solution.py:31
  26.6 0.0 collective-permute-done.9
  26.6 0.0 collective-permute-done.other_ref.query_ref
  26.6 3.6 %shard_map.55 = (f32[2,64,1024]{2,1,0:T(8,128)S(1)}, f32[2,64,128]{2,1,0:T(8,128)S(1)}) custom-call(s32[9]{0:T(128)S(1)} %concatenate.9.info, bf16[64,1024]{1,0:T(8,128)(2,1)S(1)} %get-tuple-element.14.own_ref.query_ref, bf16[64,1024]{1,0:T(8,128)(2,1)S(1)} %collective-permute-done.other_ref.query_ref, bf16[2,3,128,128]{3,2,1,0:T(8,128)(2,1)S(1)} %copy.12.k0, ...), custom_call_target="tpu_custom_call" | custom-call | flops 4294967296 | bytes 16777216 | tf_op jit(solution)/shard_map/pallas_call | solution.py:204
  30.2 0.0 slice-start
  30.3 0.5 collective-permute-done.5.k2
  30.7 1.0 %collective-permute-done.4.k1 = bf16[2,2,128,128]{3,2,1,0:T(8,128)(2,1)S(1)} collective-permute-done((bf16[2,2,128,128]{3,2,1,0:T(8,128)(2,1)S(1)}, bf16[2,2,128,128]{3,2,1,0:T(8,128)(2,1)S(1)}, u32[]{:S(2)}, u32[]{:S(2)}) %collective-permute-start.4) | collective-permute-done | bytes 131104 | tf_op jit(solution)/shard_map/ppermute | solution.py:31
  31.8 1.9 %shard_map.56.context_ref = bf16[64,1024]{1,0:T(8,128)(2,1)S(1)} custom-call(s32[9]{0:T(128)S(1)} %concatenate.9.info, bf16[64,1024]{1,0:T(8,128)(2,1)S(1)} %collective-permute-done.other_ref.query_ref, bf16[2,2,128,128]{3,2,1,0:T(8,128)(2,1)S(1)} %pad_maximum_fusion.1.k0, bf16[2,2,128,128]{3,2,1,0:T(8,128)(2,1)S(1)} %collective-permute-done.4.k1, ...), custom_call_target="tpu_custom_call" | custom-call | flops 4294967296 | bytes 16777216 | tf_op jit(solution)/shard_map/pallas_call | solution.py:216
  33.7 0.4 slice-done.1
  34.1 1.4 %shard_map.58 = bf16[64,2048]{1,0:T(8,128)(2,1)S(1)} custom-call(s32[9]{0:T(128)S(1)} %concatenate.9.info, bf16[64,1024]{1,0:T(8,128)(2,1)S(1)} %shard_map.56.context_ref, bf16[1024,4096]{1,0:T(8,128)(2,1)S(1)} %bitcast.25), custom_call_target="tpu_custom_call" | custom-call | tf_op jit(solution)/shard_map/pallas_call | solution.py:226
  35.5 4.5 %collective-permute-start.12 = (bf16[64,2048]{1,0:T(8,128)(2,1)S(1)}, bf16[64,2048]{1,0:T(8,128)(2,1)S(1)}, u32[]{:S(2)}, u32[]{:S(2)}) collective-permute-start(bf16[64,2048]{1,0:T(8,128)(2,1)S(1)} %shard_map.58), channel_id=1, source_target_pairs={{0,1},{1,0},{2,3},{3,2},{4,5},{5,4},{6,7},{7,6},{8,9},{9,8},{10,11... | collective-permute-start | bytes 786440 | tf_op jit(solution)/shard_map/ppermute | solution.py:31
  40.0 1.4 %shard_map.57 = f32[64,2048]{1,0:T(8,128)S(1)} custom-call(s32[9]{0:T(128)S(1)} %concatenate.9.info, bf16[64,1024]{1,0:T(8,128)(2,1)S(1)} %shard_map.56.context_ref, bf16[1024,4096]{1,0:T(8,128)(2,1)S(1)} %bitcast.25), custom_call_target="tpu_custom_call" | custom-call | tf_op jit(solution)/shard_map/pallas_call | solution.py:226
  41.4 2.6 %collective-permute-start.15 = (bf16[64,2048]{1,0:T(8,128)(2,1)S(1)}, bf16[64,2048]{1,0:T(8,128)(2,1)S(1)}, u32[]{:S(2)}, u32[]{:S(2)}) collective-permute-start(bf16[64,2048]{1,0:T(8,128)(2,1)S(1)} %add_convert_fusion.1), channel_id=1, source_target_pairs={{0,18},{1,19},{2,16},{3,17},{4,22},{5,23},{6,20},{7,21},{8,26},{9,... | collective-permute-start | bytes 786440 | tf_op jit(solution)/shard_map/ppermute | solution.py:31
  44.0 4.3 %shard_map.59 = (bf16[64,1024]{1,0:T(8,128)(2,1)S(1)}, bf16[64,1024]{1,0:T(8,128)(2,1)S(1)}, f32[64,2048]{1,0:T(8,128)S(1)}) custom-call(s32[9]{0:T(128)S(1)} %concatenate.9.info, bf16[64,1024]{1,0:T(8,128)(2,1)S(1)} %get-tuple-element.14.own_ref.query_ref, bf16[2,2,128,128]{3,2,1,0:T(8,128)(2,1)S(1)} %pad_maximum_fusion.1.k0, ...), custom_call_target="tpu_custom_call" | custom-call | tf_op jit(solution)/shard_map/pallas_call | solution.py:241
  48.3 0.5 collective-permute-start.13
  48.8 0.1 collective-permute-start.14
  48.9 0.9 %collective-permute-done.13 = bf16[64,1024]{1,0:T(8,128)(2,1)S(1)} collective-permute-done((bf16[64,1024]{1,0:T(8,128)(2,1)S(1)}, bf16[64,1024]{1,0:T(8,128)(2,1)S(1)}, u32[]{:S(2)}, u32[]{:S(2)}) %collective-permute-start.13) | collective-permute-done | bytes 131104 | tf_op jit(solution)/shard_map/ppermute | solution.py:31
  49.8 0.4 collective-permute-done.14
  50.1 0.3 collective-permute-done.15
  50.5 0.1 add_convert_fusion.refs_0_
  50.6 1.6 %collective-permute-start.16 = (bf16[64,2048]{1,0:T(8,128)(2,1)S(1)}, bf16[64,2048]{1,0:T(8,128)(2,1)S(1)}, u32[]{:S(2)}, u32[]{:S(2)}) collective-permute-start(bf16[64,2048]{1,0:T(8,128)(2,1)S(1)} %add_convert_fusion.refs_0_), channel_id=1, source_target_pairs={{0,2},{1,3},{2,0},{3,1},{4,6},{5,7},{6,4},{7,5},{8,10},{9,11},{10,... | collective-permute-start | bytes 786440 | tf_op jit(solution)/shard_map/ppermute | solution.py:31
  52.2 1.2 %collective-permute-start.17 = (bf16[64,2048]{1,0:T(8,128)(2,1)S(1)}, bf16[64,2048]{1,0:T(8,128)(2,1)S(1)}, u32[]{:S(2)}, u32[]{:S(2)}) collective-permute-start(bf16[64,2048]{1,0:T(8,128)(2,1)S(1)} %add_convert_fusion.refs_0_), channel_id=1, source_target_pairs={{0,1},{1,0},{2,3},{3,2},{4,5},{5,4},{6,7},{7,6},{8,9},{9,8},{10,11... | collective-permute-start | bytes 786440 | tf_op jit(solution)/shard_map/ppermute | solution.py:31
  53.4 5.6 %collective-permute-done.16.refs_1_ = bf16[64,2048]{1,0:T(8,128)(2,1)S(1)} collective-permute-done((bf16[64,2048]{1,0:T(8,128)(2,1)S(1)}, bf16[64,2048]{1,0:T(8,128)(2,1)S(1)}, u32[]{:S(2)}, u32[]{:S(2)}) %collective-permute-start.16) | collective-permute-done | bytes 262176 | tf_op jit(solution)/shard_map/ppermute | solution.py:31
  59.0 1.9 %collective-permute-start.18 = (bf16[64,2048]{1,0:T(8,128)(2,1)S(1)}, bf16[64,2048]{1,0:T(8,128)(2,1)S(1)}, u32[]{:S(2)}, u32[]{:S(2)}) collective-permute-start(bf16[64,2048]{1,0:T(8,128)(2,1)S(1)} %collective-permute-done.16.refs_1_), channel_id=1, source_target_pairs={{0,1},{1,0},{2,3},{3,2},{4,5},{5,4},{6,7},{7,6},{8,9},{9,8},{10,11... | collective-permute-start | bytes 786440 | tf_op jit(solution)/shard_map/ppermute | solution.py:31
  60.9 0.0 collective-permute-done.17.refs_2_
  60.9 1.2 %collective-permute-done.18.refs_3_ = bf16[64,2048]{1,0:T(8,128)(2,1)S(1)} collective-permute-done((bf16[64,2048]{1,0:T(8,128)(2,1)S(1)}, bf16[64,2048]{1,0:T(8,128)(2,1)S(1)}, u32[]{:S(2)}, u32[]{:S(2)}) %collective-permute-start.18) | collective-permute-done | bytes 262176 | tf_op jit(solution)/shard_map/ppermute | solution.py:31
  62.1 1.5 %shard_map.60 = bf16[2,64,4096]{2,1,0:T(8,128)(2,1)} custom-call(s32[9]{0:T(128)S(1)} %concatenate.9.info, bf16[64,2048]{1,0:T(8,128)(2,1)S(1)} %add_convert_fusion.refs_0_, bf16[64,2048]{1,0:T(8,128)(2,1)S(1)} %collective-permute-done.16.refs_1_, bf16[64,2048]{1,0:T(8,128)(2,1)S(1)} %collective-permute-done.17.refs_2_, ...), custom_call_target="tpu_custom_call" | custom-call | tf_op jit(solution)/shard_map/pallas_call | solution.py:260
  (17 shorter events, 0.2 us)
Async XLA Ops:
  0.0 9.2 %copy-start = (s32[2,4096]{1,0:T(2,128)S(1)}, s32[2,4096]{1,0:T(2,128)}, u32[]{:S(2)}) copy-start(s32[2,4096]{1,0:T(2,128)} %param.8) | copy-start | bytes 98308
  0.8 3.4 %collective-permute-start.1 = (bf16[2,64,128]{2,1,0:T(8,128)(2,1)S(1)}, bf16[2,64,128]{2,1,0:T(8,128)(2,1)S(1)}, u32[]{:S(2)}, u32[]{:S(2)}) collective-permute-start(bf16[2,64,128]{2,1,0:T(8,128)(2,1)S(1)} %get-tuple-element.24), channel_id=1, source_target_pairs={{0,16},{1,17},{2,18},{3,19},{4,20},{5,21},{6,22},{7,23},{8,24},{9,... | collective-permute-start | bytes 98312 | tf_op jit(solution)/shard_map/ppermute | solution.py:31
  3.9 22.7 %collective-permute-start = (bf16[64,1024]{1,0:T(8,128)(2,1)S(1)}, bf16[64,1024]{1,0:T(8,128)(2,1)S(1)}, u32[]{:S(2)}, u32[]{:S(2)}) collective-permute-start(bf16[64,1024]{1,0:T(8,128)(2,1)S(1)} %get-tuple-element.20), channel_id=1, source_target_pairs={{0,16},{1,17},{2,18},{3,19},{4,20},{5,21},{6,22},{7,23},{8,24},{9,... | collective-permute-start | bytes 393224 | tf_op jit(solution)/shard_map/ppermute | solution.py:31
  4.2 9.3 %collective-permute-start.7 = (bf16[2,128,128]{2,1,0:T(8,128)(2,1)S(1)}, bf16[2,128,128]{2,1,0:T(8,128)(2,1)S(1)}, u32[]{:S(2)}, u32[]{:S(2)}) collective-permute-start(bf16[2,128,128]{2,1,0:T(8,128)(2,1)S(1)} %get-tuple-element.22), channel_id=1, source_target_pairs={{0,32},{1,33},{2,34},{3,35},{4,36},{5,37},{6,38},{7,39},{8,40},{9,... | collective-permute-start | bytes 196616 | tf_op jit(solution)/shard_map/ppermute | solution.py:31
  6.2 8.2 %collective-permute-start.8 = (bf16[2,128,128]{2,1,0:T(8,128)(2,1)S(1)}, bf16[2,128,128]{2,1,0:T(8,128)(2,1)S(1)}, u32[]{:S(2)}, u32[]{:S(2)}) collective-permute-start(bf16[2,128,128]{2,1,0:T(8,128)(2,1)S(1)} %get-tuple-element.22), channel_id=1, source_target_pairs={{0,64},{1,65},{2,66},{3,67},{4,68},{5,69},{6,70},{7,71},{8,72},{9,... | collective-permute-start | bytes 196616 | tf_op jit(solution)/shard_map/ppermute | solution.py:31
  9.2 9.0 %collective-permute-start.3 = (bf16[2,128,128]{2,1,0:T(8,128)(2,1)S(1)}, bf16[2,128,128]{2,1,0:T(8,128)(2,1)S(1)}, u32[]{:S(2)}, u32[]{:S(2)}) collective-permute-start(bf16[2,128,128]{2,1,0:T(8,128)(2,1)S(1)} %get-tuple-element.22), channel_id=1, source_target_pairs={{0,128},{1,129},{2,130},{3,131},{4,132},{5,133},{6,134},{7,135},{8... | collective-permute-start | bytes 196616 | tf_op jit(solution)/shard_map/ppermute | solution.py:31
  13.5 8.3 %collective-permute-start.2 = (bf16[2,128,128]{2,1,0:T(8,128)(2,1)S(1)}, bf16[2,128,128]{2,1,0:T(8,128)(2,1)S(1)}, u32[]{:S(2)}, u32[]{:S(2)}) collective-permute-start(bf16[2,128,128]{2,1,0:T(8,128)(2,1)S(1)} %get-tuple-element.22), channel_id=1, source_target_pairs={{0,96},{1,97},{2,98},{3,99},{4,100},{5,101},{6,102},{7,103},{8,104... | collective-permute-start | bytes 196616 | tf_op jit(solution)/shard_map/ppermute | solution.py:31
  14.4 10.4 %collective-permute-start.11 = (bf16[2,3,128,128]{3,2,0,1:T(8,128)(2,1)S(1)}, bf16[2,3,128,128]{3,2,0,1:T(8,128)(2,1)S(1)}, u32[]{:S(2)}, u32[]{:S(2)}) collective-permute-start(bf16[2,3,128,128]{3,2,0,1:T(8,128)(2,1)S(1)} %pad_maximum_fusion), channel_id=1, source_target_pairs={{0,8},{1,9},{2,10},{3,11},{4,12},{5,13},{6,14},{7,15},{8,0},{9,1},... | collective-permute-start | bytes 589832 | tf_op jit(solution)/shard_map/ppermute | solution.py:31
  17.4 8.2 %collective-permute-start.10 = (bf16[2,3,128,128]{3,2,0,1:T(8,128)(2,1)S(1)}, bf16[2,3,128,128]{3,2,0,1:T(8,128)(2,1)S(1)}, u32[]{:S(2)}, u32[]{:S(2)}) collective-permute-start(bf16[2,3,128,128]{3,2,0,1:T(8,128)(2,1)S(1)} %pad_maximum_fusion), channel_id=1, source_target_pairs={{0,12},{1,13},{2,14},{3,15},{4,0},{5,1},{6,2},{7,3},{8,4},{9,5},{1... | collective-permute-start | bytes 589832 | tf_op jit(solution)/shard_map/ppermute | solution.py:31
  18.2 8.4 %collective-permute-start.9 = (bf16[2,3,128,128]{3,2,0,1:T(8,128)(2,1)S(1)}, bf16[2,3,128,128]{3,2,0,1:T(8,128)(2,1)S(1)}, u32[]{:S(2)}, u32[]{:S(2)}) collective-permute-start(bf16[2,3,128,128]{3,2,0,1:T(8,128)(2,1)S(1)} %pad_maximum_fusion), channel_id=1, source_target_pairs={{0,4},{1,5},{2,6},{3,7},{4,8},{5,9},{6,10},{7,11},{8,12},{9,13},{1... | collective-permute-start | bytes 589832 | tf_op jit(solution)/shard_map/ppermute | solution.py:31
  21.8 8.4 %collective-permute-start.6 = (bf16[2,2,128,128]{3,2,1,0:T(8,128)(2,1)S(1)}, bf16[2,2,128,128]{3,2,1,0:T(8,128)(2,1)S(1)}, u32[]{:S(2)}, u32[]{:S(2)}) collective-permute-start(bf16[2,2,128,128]{3,2,1,0:T(8,128)(2,1)S(1)} %pad_maximum_fusion.1.k0), channel_id=1, source_target_pairs={{0,8},{1,9},{2,10},{3,11},{4,12},{5,13},{6,14},{7,15},{8,0},{9,1},... | collective-permute-start | bytes 393224 | tf_op jit(solution)/shard_map/ppermute | solution.py:31
  24.8 5.9 %collective-permute-start.5 = (bf16[2,2,128,128]{3,2,1,0:T(8,128)(2,1)S(1)}, bf16[2,2,128,128]{3,2,1,0:T(8,128)(2,1)S(1)}, u32[]{:S(2)}, u32[]{:S(2)}) collective-permute-start(bf16[2,2,128,128]{3,2,1,0:T(8,128)(2,1)S(1)} %pad_maximum_fusion.1.k0), channel_id=1, source_target_pairs={{0,12},{1,13},{2,14},{3,15},{4,0},{5,1},{6,2},{7,3},{8,4},{9,5},{1... | collective-permute-start | bytes 393224 | tf_op jit(solution)/shard_map/ppermute | solution.py:31
  25.6 6.1 %collective-permute-start.4 = (bf16[2,2,128,128]{3,2,1,0:T(8,128)(2,1)S(1)}, bf16[2,2,128,128]{3,2,1,0:T(8,128)(2,1)S(1)}, u32[]{:S(2)}, u32[]{:S(2)}) collective-permute-start(bf16[2,2,128,128]{3,2,1,0:T(8,128)(2,1)S(1)} %pad_maximum_fusion.1.k0), channel_id=1, source_target_pairs={{0,4},{1,5},{2,6},{3,7},{4,8},{5,9},{6,10},{7,11},{8,12},{9,13},{1... | collective-permute-start | bytes 393224 | tf_op jit(solution)/shard_map/ppermute | solution.py:31
  30.2 3.5 %slice-start = ((s8[8388608]{0:T(1024)(128)(4,1)}), s8[4194304]{0:T(1024)(128)(4,1)S(1)}, s32[]{:S(2)}) async-start(s8[8388608]{0:T(1024)(128)(4,1)} %bitcast.24), calls=%async_computation | async-start | bytes 8388608
  31.8 2.4 %slice-start.1 = ((s8[8388608]{0:T(1024)(128)(4,1)}), s8[4194304]{0:T(1024)(128)(4,1)S(1)}, s32[]{:S(2)}) async-start(s8[8388608]{0:T(1024)(128)(4,1)} %bitcast.24), calls=%async_computation.1 | async-start | bytes 8388608
  35.5 5.9 %collective-permute-start.12 = (bf16[64,2048]{1,0:T(8,128)(2,1)S(1)}, bf16[64,2048]{1,0:T(8,128)(2,1)S(1)}, u32[]{:S(2)}, u32[]{:S(2)}) collective-permute-start(bf16[64,2048]{1,0:T(8,128)(2,1)S(1)} %shard_map.58), channel_id=1, source_target_pairs={{0,1},{1,0},{2,3},{3,2},{4,5},{5,4},{6,7},{7,6},{8,9},{9,8},{10,11... | collective-permute-start | bytes 786440 | tf_op jit(solution)/shard_map/ppermute | solution.py:31
  41.4 9.1 %collective-permute-start.15 = (bf16[64,2048]{1,0:T(8,128)(2,1)S(1)}, bf16[64,2048]{1,0:T(8,128)(2,1)S(1)}, u32[]{:S(2)}, u32[]{:S(2)}) collective-permute-start(bf16[64,2048]{1,0:T(8,128)(2,1)S(1)} %add_convert_fusion.1), channel_id=1, source_target_pairs={{0,18},{1,19},{2,16},{3,17},{4,22},{5,23},{6,20},{7,21},{8,26},{9,... | collective-permute-start | bytes 786440 | tf_op jit(solution)/shard_map/ppermute | solution.py:31
  48.3 1.5 %collective-permute-start.13 = (bf16[64,1024]{1,0:T(8,128)(2,1)S(1)}, bf16[64,1024]{1,0:T(8,128)(2,1)S(1)}, u32[]{:S(2)}, u32[]{:S(2)}) collective-permute-start(bf16[64,1024]{1,0:T(8,128)(2,1)S(1)} %get-tuple-element.16), channel_id=1, source_target_pairs={{0,1},{1,0},{2,3},{3,2},{4,5},{5,4},{6,7},{7,6},{8,9},{9,8},{10,11... | collective-permute-start | bytes 393224 | tf_op jit(solution)/shard_map/ppermute | solution.py:31
  48.8 1.3 %collective-permute-start.14 = (bf16[64,1024]{1,0:T(8,128)(2,1)S(1)}, bf16[64,1024]{1,0:T(8,128)(2,1)S(1)}, u32[]{:S(2)}, u32[]{:S(2)}) collective-permute-start(bf16[64,1024]{1,0:T(8,128)(2,1)S(1)} %get-tuple-element.17), channel_id=1, source_target_pairs={{0,1},{1,0},{2,3},{3,2},{4,5},{5,4},{6,7},{7,6},{8,9},{9,8},{10,11... | collective-permute-start | bytes 393224 | tf_op jit(solution)/shard_map/ppermute | solution.py:31
  50.6 8.4 %collective-permute-start.16 = (bf16[64,2048]{1,0:T(8,128)(2,1)S(1)}, bf16[64,2048]{1,0:T(8,128)(2,1)S(1)}, u32[]{:S(2)}, u32[]{:S(2)}) collective-permute-start(bf16[64,2048]{1,0:T(8,128)(2,1)S(1)} %add_convert_fusion.refs_0_), channel_id=1, source_target_pairs={{0,2},{1,3},{2,0},{3,1},{4,6},{5,7},{6,4},{7,5},{8,10},{9,11},{10,... | collective-permute-start | bytes 786440 | tf_op jit(solution)/shard_map/ppermute | solution.py:31
  52.2 8.7 %collective-permute-start.17 = (bf16[64,2048]{1,0:T(8,128)(2,1)S(1)}, bf16[64,2048]{1,0:T(8,128)(2,1)S(1)}, u32[]{:S(2)}, u32[]{:S(2)}) collective-permute-start(bf16[64,2048]{1,0:T(8,128)(2,1)S(1)} %add_convert_fusion.refs_0_), channel_id=1, source_target_pairs={{0,1},{1,0},{2,3},{3,2},{4,5},{5,4},{6,7},{7,6},{8,9},{9,8},{10,11... | collective-permute-start | bytes 786440 | tf_op jit(solution)/shard_map/ppermute | solution.py:31
  59.0 3.0 %collective-permute-start.18 = (bf16[64,2048]{1,0:T(8,128)(2,1)S(1)}, bf16[64,2048]{1,0:T(8,128)(2,1)S(1)}, u32[]{:S(2)}, u32[]{:S(2)}) collective-permute-start(bf16[64,2048]{1,0:T(8,128)(2,1)S(1)} %collective-permute-done.16.refs_1_), channel_id=1, source_target_pairs={{0,1},{1,0},{2,3},{3,2},{4,5},{5,4},{6,7},{7,6},{8,9},{9,8},{10,11... | collective-permute-start | bytes 786440 | tf_op jit(solution)/shard_map/ppermute | solution.py:31

commit v4 on v3

--- a/solution.py
+++ b/solution.py
@@ -15,7 +15,7 @@
 COLUMNS_BACK = (0, 1, 3, 2)
 GROUP = 4
 PIECES = 1
-LONG = pl.CostEstimate(flops=4 << 30, bytes_accessed=16 << 20, transcendentals=4 << 20)
+LONG = pl.CostEstimate(flops=16 << 30, bytes_accessed=16 << 20, transcendentals=4 << 20)
 LIMIT = pltpu.CompilerParams(vmem_limit_bytes=24 * 1024 * 1024)
 SMEM = pl.BlockSpec(memory_space=pltpu.SMEM)
 VMEM = pl.BlockSpec(memory_space=pltpu.VMEM)

time: 64.3 us -> 63.6 us (0.989)
  starting transfers between devices: 33.2 us -> 32.5 us
    ppermute x19, starting transfers between devices: 33.2 us -> 32.5 us  [shift(): lax.ppermute(array, AXES, [(flat(*d), flat(*move(*d))) for d in devices])]
where the time goes in v4:
time: 63.6 us; the launch traced here: 62.9 us
  starting transfers between devices  32.5 us (51%)
  Pallas kernels  14.1 us (22%)
  waiting for transfers between devices  13.4 us (21%)
  local copies, waits for them, and re-layouts  1.4 us (2%)
  other arithmetic  1.13 us (2%)
    ppermute x19, starting transfers between devices, shift(): lax.ppermute(array, AXES, [(flat(*d), flat(*move(*d))) for d in devices])  32.5 us
    ppermute x19, waiting for transfers between devices, shift(): lax.ppermute(array, AXES, [(flat(*d), flat(*move(*d))) for d in devices])  13.4 us
    pallas_call x1, Pallas kernels, body(): pl.pallas_call(functools.partial(far_project_kernel, heads, size, block),...  4.27 us
    pallas_call x1, Pallas kernels, body(): pl.pallas_call(functools.partial(near_kernel, heads, size, block), out_sh...  3.61 us
    pallas_call x2, Pallas kernels, projected(): pl.pallas_call(functools.partial(project_kernel, own_half), out_shape=jax...  2.76 us
    pallas_call x1, Pallas kernels, body(): pl.pallas_call(functools.partial(far_kernel, heads, size, block), out_sha...  1.93 us
    pallas_call x1, Pallas kernels, body(): pl.pallas_call(functools.partial(place_kernel, PIECES), out_shape=jax.Sha...  1.54 us
  transfers between devices with their start and end apart: 19, of which 10 were waited for; matrix products, arithmetic and copies ran while one was open for 2% of the time, Pallas kernels for 15%

profile of v4, /device:TPU:1, one launch (start us, length us, event | category | flops | bytes accessed | tf_op | source)
XLA Modules:
  0.0 62.9 jit_solution(7217118500035645860)
XLA Ops:
  0.0 0.8 %fusion.3 = (bf16[2,64,128]{2,1,0:T(8,128)(2,1)S(1)}, bf16[2,64,128]{2,1,0:T(8,128)(2,1)S(1)}) fusion(s32[]{:T(128)S(6)} %select_n.43, bf16[2,1,64,128]{3,2,0,1:T(8,128)(2,1)} %bitcast.31, bf16[2,1,64,128]{3,2,0,1:T(8,128)(2,1)} %bitcast.32, s32[]{:T(128)S(6)} %select_n.44), kind=kLoop, calls=%fused_computation.16 | loop fusion | flops 32768 | bytes 131080 | tf_op jit(solution)/shard_map/jit(dynamic_index_in_dim)/squeeze | solution.py:186
  0.8 2.1 %collective-permute-start.1 = (bf16[2,64,128]{2,1,0:T(8,128)(2,1)S(1)}, bf16[2,64,128]{2,1,0:T(8,128)(2,1)S(1)}, u32[]{:S(2)}, u32[]{:S(2)}) collective-permute-start(bf16[2,64,128]{2,1,0:T(8,128)(2,1)S(1)} %get-tuple-element.24), channel_id=1, source_target_pairs={{0,16},{1,17},{2,18},{3,19},{4,20},{5,21},{6,22},{7,23},{8,24},{9,... | collective-permute-start | bytes 98312 | tf_op jit(solution)/shard_map/ppermute | solution.py:31
  2.9 1.0 %dynamic-slice_bitcast_fusion = (bf16[64,1024]{1,0:T(8,128)(2,1)S(1)}, bf16[64,1024]{1,0:T(8,128)(2,1)S(1)}) fusion(bf16[2,64,1024]{2,1,0:T(8,128)(2,1)} %param.5, s32[]{:T(128)S(6)} %select_n.43, s32[]{:T(128)S(6)} %select_n.44), kind=kLoop, calls=%fused_computation.4 | loop fusion | bytes 524296 | tf_op jit(solution)/shard_map/jit(dynamic_index_in_dim)/squeeze | solution.py:186
  3.9 0.1 collective-permute-start
  4.0 0.2 collective-permute-done.1
  4.2 2.0 %collective-permute-start.7 = (bf16[2,128,128]{2,1,0:T(8,128)(2,1)S(1)}, bf16[2,128,128]{2,1,0:T(8,128)(2,1)S(1)}, u32[]{:S(2)}, u32[]{:S(2)}) collective-permute-start(bf16[2,128,128]{2,1,0:T(8,128)(2,1)S(1)} %get-tuple-element.22), channel_id=1, source_target_pairs={{0,32},{1,33},{2,34},{3,35},{4,36},{5,37},{6,38},{7,39},{8,40},{9,... | collective-permute-start | bytes 196616 | tf_op jit(solution)/shard_map/ppermute | solution.py:31
  6.2 3.0 %collective-permute-start.8 = (bf16[2,128,128]{2,1,0:T(8,128)(2,1)S(1)}, bf16[2,128,128]{2,1,0:T(8,128)(2,1)S(1)}, u32[]{:S(2)}, u32[]{:S(2)}) collective-permute-start(bf16[2,128,128]{2,1,0:T(8,128)(2,1)S(1)} %get-tuple-element.22), channel_id=1, source_target_pairs={{0,64},{1,65},{2,66},{3,67},{4,68},{5,69},{6,70},{7,71},{8,72},{9,... | collective-permute-start | bytes 196616 | tf_op jit(solution)/shard_map/ppermute | solution.py:31
  9.2 4.3 %collective-permute-start.3 = (bf16[2,128,128]{2,1,0:T(8,128)(2,1)S(1)}, bf16[2,128,128]{2,1,0:T(8,128)(2,1)S(1)}, u32[]{:S(2)}, u32[]{:S(2)}) collective-permute-start(bf16[2,128,128]{2,1,0:T(8,128)(2,1)S(1)} %get-tuple-element.22), channel_id=1, source_target_pairs={{0,128},{1,129},{2,130},{3,131},{4,132},{5,133},{6,134},{7,135},{8... | collective-permute-start | bytes 196616 | tf_op jit(solution)/shard_map/ppermute | solution.py:31
  13.5 0.0 collective-permute-start.2
  13.5 0.0 collective-permute-done.7
  13.5 0.9 %collective-permute-done.8 = bf16[2,128,128]{2,1,0:T(8,128)(2,1)S(1)} collective-permute-done((bf16[2,128,128]{2,1,0:T(8,128)(2,1)S(1)}, bf16[2,128,128]{2,1,0:T(8,128)(2,1)S(1)}, u32[]{:S(2)}, u32[]{:S(2)}) %collective-permute-start.8) | collective-permute-done | bytes 65568 | tf_op jit(solution)/shard_map/ppermute | solution.py:31
  14.4 3.0 %collective-permute-start.11 = (bf16[2,3,128,128]{3,2,0,1:T(8,128)(2,1)S(1)}, bf16[2,3,128,128]{3,2,0,1:T(8,128)(2,1)S(1)}, u32[]{:S(2)}, u32[]{:S(2)}) collective-permute-start(bf16[2,3,128,128]{3,2,0,1:T(8,128)(2,1)S(1)} %pad_maximum_fusion), channel_id=1, source_target_pairs={{0,8},{1,9},{2,10},{3,11},{4,12},{5,13},{6,14},{7,15},{8,0},{9,1},... | collective-permute-start | bytes 589832 | tf_op jit(solution)/shard_map/ppermute | solution.py:31
  17.4 0.8 %collective-permute-start.10 = (bf16[2,3,128,128]{3,2,0,1:T(8,128)(2,1)S(1)}, bf16[2,3,128,128]{3,2,0,1:T(8,128)(2,1)S(1)}, u32[]{:S(2)}, u32[]{:S(2)}) collective-permute-start(bf16[2,3,128,128]{3,2,0,1:T(8,128)(2,1)S(1)} %pad_maximum_fusion), channel_id=1, source_target_pairs={{0,12},{1,13},{2,14},{3,15},{4,0},{5,1},{6,2},{7,3},{8,4},{9,5},{1... | collective-permute-start | bytes 589832 | tf_op jit(solution)/shard_map/ppermute | solution.py:31
  18.2 0.0 collective-permute-done.3
  18.2 0.8 %collective-permute-start.9 = (bf16[2,3,128,128]{3,2,0,1:T(8,128)(2,1)S(1)}, bf16[2,3,128,128]{3,2,0,1:T(8,128)(2,1)S(1)}, u32[]{:S(2)}, u32[]{:S(2)}) collective-permute-start(bf16[2,3,128,128]{3,2,0,1:T(8,128)(2,1)S(1)} %pad_maximum_fusion), channel_id=1, source_target_pairs={{0,4},{1,5},{2,6},{3,7},{4,8},{5,9},{6,10},{7,11},{8,12},{9,13},{1... | collective-permute-start | bytes 589832 | tf_op jit(solution)/shard_map/ppermute | solution.py:31
  19.0 0.1 convert_reduce_fusion
  19.2 0.1 concatenate.9.info
  19.3 2.5 %collective-permute-done.2 = bf16[2,128,128]{2,1,0:T(8,128)(2,1)S(1)} collective-permute-done((bf16[2,128,128]{2,1,0:T(8,128)(2,1)S(1)}, bf16[2,128,128]{2,1,0:T(8,128)(2,1)S(1)}, u32[]{:S(2)}, u32[]{:S(2)}) %collective-permute-start.2) | collective-permute-done | bytes 65568 | tf_op jit(solution)/shard_map/ppermute | solution.py:31
  21.8 3.0 %collective-permute-start.6 = (bf16[2,2,128,128]{3,2,1,0:T(8,128)(2,1)S(1)}, bf16[2,2,128,128]{3,2,1,0:T(8,128)(2,1)S(1)}, u32[]{:S(2)}, u32[]{:S(2)}) collective-permute-start(bf16[2,2,128,128]{3,2,1,0:T(8,128)(2,1)S(1)} %pad_maximum_fusion.1.k0), channel_id=1, source_target_pairs={{0,8},{1,9},{2,10},{3,11},{4,12},{5,13},{6,14},{7,15},{8,0},{9,1},... | collective-permute-start | bytes 393224 | tf_op jit(solution)/shard_map/ppermute | solution.py:31
  24.8 0.0 collective-permute-done.11
  24.8 0.8 %collective-permute-start.5 = (bf16[2,2,128,128]{3,2,1,0:T(8,128)(2,1)S(1)}, bf16[2,2,128,128]{3,2,1,0:T(8,128)(2,1)S(1)}, u32[]{:S(2)}, u32[]{:S(2)}) collective-permute-start(bf16[2,2,128,128]{3,2,1,0:T(8,128)(2,1)S(1)} %pad_maximum_fusion.1.k0), channel_id=1, source_target_pairs={{0,12},{1,13},{2,14},{3,15},{4,0},{5,1},{6,2},{7,3},{8,4},{9,5},{1... | collective-permute-start | bytes 393224 | tf_op jit(solution)/shard_map/ppermute | solution.py:31
  25.6 0.0 collective-permute-done.10
  25.6 0.9 %collective-permute-start.4 = (bf16[2,2,128,128]{3,2,1,0:T(8,128)(2,1)S(1)}, bf16[2,2,128,128]{3,2,1,0:T(8,128)(2,1)S(1)}, u32[]{:S(2)}, u32[]{:S(2)}) collective-permute-start(bf16[2,2,128,128]{3,2,1,0:T(8,128)(2,1)S(1)} %pad_maximum_fusion.1.k0), channel_id=1, source_target_pairs={{0,4},{1,5},{2,6},{3,7},{4,8},{5,9},{6,10},{7,11},{8,12},{9,13},{1... | collective-permute-start | bytes 393224 | tf_op jit(solution)/shard_map/ppermute | solution.py:31
  26.6 0.0 collective-permute-done.other_ref.query_ref
  26.6 0.0 slice-start
  26.6 3.6 %shard_map.55 = (f32[2,64,1024]{2,1,0:T(8,128)S(1)}, f32[2,64,128]{2,1,0:T(8,128)S(1)}) custom-call(s32[9]{0:T(128)S(1)} %concatenate.9.info, bf16[64,1024]{1,0:T(8,128)(2,1)S(1)} %get-tuple-element.14.own_ref.query_ref, bf16[64,1024]{1,0:T(8,128)(2,1)S(1)} %collective-permute-done.other_ref.query_ref, bf16[2,3,128,128]{3,2,1,0:T(8,128)(2,1)S(1)} %copy.12.k0, ...), custom_call_target="tpu_custom_call" | custom-call | flops 17179869184 | bytes 16777216 | tf_op jit(solution)/shard_map/pallas_call | solution.py:204
  30.3 0.5 collective-permute-done.5.k2
  30.7 1.0 %collective-permute-done.4.k1 = bf16[2,2,128,128]{3,2,1,0:T(8,128)(2,1)S(1)} collective-permute-done((bf16[2,2,128,128]{3,2,1,0:T(8,128)(2,1)S(1)}, bf16[2,2,128,128]{3,2,1,0:T(8,128)(2,1)S(1)}, u32[]{:S(2)}, u32[]{:S(2)}) %collective-permute-start.4) | collective-permute-done | bytes 131104 | tf_op jit(solution)/shard_map/ppermute | solution.py:31
  31.8 1.9 %shard_map.56.context_ref = bf16[64,1024]{1,0:T(8,128)(2,1)S(1)} custom-call(s32[9]{0:T(128)S(1)} %concatenate.9.info, bf16[64,1024]{1,0:T(8,128)(2,1)S(1)} %collective-permute-done.other_ref.query_ref, bf16[2,2,128,128]{3,2,1,0:T(8,128)(2,1)S(1)} %pad_maximum_fusion.1.k0, bf16[2,2,128,128]{3,2,1,0:T(8,128)(2,1)S(1)} %collective-permute-done.4.k1, ...), custom_call_target="tpu_custom_call" | custom-call | flops 17179869184 | bytes 16777216 | tf_op jit(solution)/shard_map/pallas_call | solution.py:216
  33.7 0.2 slice-done.1
  33.9 1.4 %shard_map.58 = bf16[64,2048]{1,0:T(8,128)(2,1)S(1)} custom-call(s32[9]{0:T(128)S(1)} %concatenate.9.info, bf16[64,1024]{1,0:T(8,128)(2,1)S(1)} %shard_map.56.context_ref, bf16[1024,4096]{1,0:T(8,128)(2,1)S(1)} %bitcast.25), custom_call_target="tpu_custom_call" | custom-call | tf_op jit(solution)/shard_map/pallas_call | solution.py:226
  35.3 3.8 %collective-permute-start.12 = (bf16[64,2048]{1,0:T(8,128)(2,1)S(1)}, bf16[64,2048]{1,0:T(8,128)(2,1)S(1)}, u32[]{:S(2)}, u32[]{:S(2)}) collective-permute-start(bf16[64,2048]{1,0:T(8,128)(2,1)S(1)} %shard_map.58), channel_id=1, source_target_pairs={{0,1},{1,0},{2,3},{3,2},{4,5},{5,4},{6,7},{7,6},{8,9},{9,8},{10,11... | collective-permute-start | bytes 786440 | tf_op jit(solution)/shard_map/ppermute | solution.py:31
  39.1 1.4 %shard_map.57 = f32[64,2048]{1,0:T(8,128)S(1)} custom-call(s32[9]{0:T(128)S(1)} %concatenate.9.info, bf16[64,1024]{1,0:T(8,128)(2,1)S(1)} %shard_map.56.context_ref, bf16[1024,4096]{1,0:T(8,128)(2,1)S(1)} %bitcast.25), custom_call_target="tpu_custom_call" | custom-call | tf_op jit(solution)/shard_map/pallas_call | solution.py:226
  40.6 2.6 %collective-permute-start.15 = (bf16[64,2048]{1,0:T(8,128)(2,1)S(1)}, bf16[64,2048]{1,0:T(8,128)(2,1)S(1)}, u32[]{:S(2)}, u32[]{:S(2)}) collective-permute-start(bf16[64,2048]{1,0:T(8,128)(2,1)S(1)} %add_convert_fusion.1), channel_id=1, source_target_pairs={{0,18},{1,19},{2,16},{3,17},{4,22},{5,23},{6,20},{7,21},{8,26},{9,... | collective-permute-start | bytes 786440 | tf_op jit(solution)/shard_map/ppermute | solution.py:31
  43.2 4.3 %shard_map.59 = (bf16[64,1024]{1,0:T(8,128)(2,1)S(1)}, bf16[64,1024]{1,0:T(8,128)(2,1)S(1)}, f32[64,2048]{1,0:T(8,128)S(1)}) custom-call(s32[9]{0:T(128)S(1)} %concatenate.9.info, bf16[64,1024]{1,0:T(8,128)(2,1)S(1)} %get-tuple-element.14.own_ref.query_ref, bf16[2,2,128,128]{3,2,1,0:T(8,128)(2,1)S(1)} %pad_maximum_fusion.1.k0, ...), custom_call_target="tpu_custom_call" | custom-call | tf_op jit(solution)/shard_map/pallas_call | solution.py:241
  47.4 0.5 collective-permute-start.13
  48.0 0.1 collective-permute-start.14
  48.1 0.9 %collective-permute-done.13 = bf16[64,1024]{1,0:T(8,128)(2,1)S(1)} collective-permute-done((bf16[64,1024]{1,0:T(8,128)(2,1)S(1)}, bf16[64,1024]{1,0:T(8,128)(2,1)S(1)}, u32[]{:S(2)}, u32[]{:S(2)}) %collective-permute-start.13) | collective-permute-done | bytes 131104 | tf_op jit(solution)/shard_map/ppermute | solution.py:31
  49.0 0.4 collective-permute-done.14
  49.3 0.4 collective-permute-done.15
  49.7 0.1 add_convert_fusion.refs_0_
  49.8 1.6 %collective-permute-start.16 = (bf16[64,2048]{1,0:T(8,128)(2,1)S(1)}, bf16[64,2048]{1,0:T(8,128)(2,1)S(1)}, u32[]{:S(2)}, u32[]{:S(2)}) collective-permute-start(bf16[64,2048]{1,0:T(8,128)(2,1)S(1)} %add_convert_fusion.refs_0_), channel_id=1, source_target_pairs={{0,2},{1,3},{2,0},{3,1},{4,6},{5,7},{6,4},{7,5},{8,10},{9,11},{10,... | collective-permute-start | bytes 786440 | tf_op jit(solution)/shard_map/ppermute | solution.py:31
  51.4 1.2 %collective-permute-start.17 = (bf16[64,2048]{1,0:T(8,128)(2,1)S(1)}, bf16[64,2048]{1,0:T(8,128)(2,1)S(1)}, u32[]{:S(2)}, u32[]{:S(2)}) collective-permute-start(bf16[64,2048]{1,0:T(8,128)(2,1)S(1)} %add_convert_fusion.refs_0_), channel_id=1, source_target_pairs={{0,1},{1,0},{2,3},{3,2},{4,5},{5,4},{6,7},{7,6},{8,9},{9,8},{10,11... | collective-permute-start | bytes 786440 | tf_op jit(solution)/shard_map/ppermute | solution.py:31
  52.6 5.6 %collective-permute-done.16.refs_1_ = bf16[64,2048]{1,0:T(8,128)(2,1)S(1)} collective-permute-done((bf16[64,2048]{1,0:T(8,128)(2,1)S(1)}, bf16[64,2048]{1,0:T(8,128)(2,1)S(1)}, u32[]{:S(2)}, u32[]{:S(2)}) %collective-permute-start.16) | collective-permute-done | bytes 262176 | tf_op jit(solution)/shard_map/ppermute | solution.py:31
  58.2 1.9 %collective-permute-start.18 = (bf16[64,2048]{1,0:T(8,128)(2,1)S(1)}, bf16[64,2048]{1,0:T(8,128)(2,1)S(1)}, u32[]{:S(2)}, u32[]{:S(2)}) collective-permute-start(bf16[64,2048]{1,0:T(8,128)(2,1)S(1)} %collective-permute-done.16.refs_1_), channel_id=1, source_target_pairs={{0,1},{1,0},{2,3},{3,2},{4,5},{5,4},{6,7},{7,6},{8,9},{9,8},{10,11... | collective-permute-start | bytes 786440 | tf_op jit(solution)/shard_map/ppermute | solution.py:31
  60.1 0.0 collective-permute-done.17.refs_2_
  60.1 1.2 %collective-permute-done.18.refs_3_ = bf16[64,2048]{1,0:T(8,128)(2,1)S(1)} collective-permute-done((bf16[64,2048]{1,0:T(8,128)(2,1)S(1)}, bf16[64,2048]{1,0:T(8,128)(2,1)S(1)}, u32[]{:S(2)}, u32[]{:S(2)}) %collective-permute-start.18) | collective-permute-done | bytes 262176 | tf_op jit(solution)/shard_map/ppermute | solution.py:31
  61.2 1.5 %shard_map.60 = bf16[2,64,4096]{2,1,0:T(8,128)(2,1)} custom-call(s32[9]{0:T(128)S(1)} %concatenate.9.info, bf16[64,2048]{1,0:T(8,128)(2,1)S(1)} %add_convert_fusion.refs_0_, bf16[64,2048]{1,0:T(8,128)(2,1)S(1)} %collective-permute-done.16.refs_1_, bf16[64,2048]{1,0:T(8,128)(2,1)S(1)} %collective-permute-done.17.refs_2_, ...), custom_call_target="tpu_custom_call" | custom-call | tf_op jit(solution)/shard_map/pallas_call | solution.py:260
  (17 shorter events, 0.2 us)
Async XLA Ops:
  0.0 9.2 %copy-start = (s32[2,4096]{1,0:T(2,128)S(1)}, s32[2,4096]{1,0:T(2,128)}, u32[]{:S(2)}) copy-start(s32[2,4096]{1,0:T(2,128)} %param.8) | copy-start | bytes 98308
  0.8 3.4 %collective-permute-start.1 = (bf16[2,64,128]{2,1,0:T(8,128)(2,1)S(1)}, bf16[2,64,128]{2,1,0:T(8,128)(2,1)S(1)}, u32[]{:S(2)}, u32[]{:S(2)}) collective-permute-start(bf16[2,64,128]{2,1,0:T(8,128)(2,1)S(1)} %get-tuple-element.24), channel_id=1, source_target_pairs={{0,16},{1,17},{2,18},{3,19},{4,20},{5,21},{6,22},{7,23},{8,24},{9,... | collective-permute-start | bytes 98312 | tf_op jit(solution)/shard_map/ppermute | solution.py:31
  3.9 22.7 %collective-permute-start = (bf16[64,1024]{1,0:T(8,128)(2,1)S(1)}, bf16[64,1024]{1,0:T(8,128)(2,1)S(1)}, u32[]{:S(2)}, u32[]{:S(2)}) collective-permute-start(bf16[64,1024]{1,0:T(8,128)(2,1)S(1)} %get-tuple-element.20), channel_id=1, source_target_pairs={{0,16},{1,17},{2,18},{3,19},{4,20},{5,21},{6,22},{7,23},{8,24},{9,... | collective-permute-start | bytes 393224 | tf_op jit(solution)/shard_map/ppermute | solution.py:31
  4.2 9.3 %collective-permute-start.7 = (bf16[2,128,128]{2,1,0:T(8,128)(2,1)S(1)}, bf16[2,128,128]{2,1,0:T(8,128)(2,1)S(1)}, u32[]{:S(2)}, u32[]{:S(2)}) collective-permute-start(bf16[2,128,128]{2,1,0:T(8,128)(2,1)S(1)} %get-tuple-element.22), channel_id=1, source_target_pairs={{0,32},{1,33},{2,34},{3,35},{4,36},{5,37},{6,38},{7,39},{8,40},{9,... | collective-permute-start | bytes 196616 | tf_op jit(solution)/shard_map/ppermute | solution.py:31
  6.2 8.2 %collective-permute-start.8 = (bf16[2,128,128]{2,1,0:T(8,128)(2,1)S(1)}, bf16[2,128,128]{2,1,0:T(8,128)(2,1)S(1)}, u32[]{:S(2)}, u32[]{:S(2)}) collective-permute-start(bf16[2,128,128]{2,1,0:T(8,128)(2,1)S(1)} %get-tuple-element.22), channel_id=1, source_target_pairs={{0,64},{1,65},{2,66},{3,67},{4,68},{5,69},{6,70},{7,71},{8,72},{9,... | collective-permute-start | bytes 196616 | tf_op jit(solution)/shard_map/ppermute | solution.py:31
  9.2 9.0 %collective-permute-start.3 = (bf16[2,128,128]{2,1,0:T(8,128)(2,1)S(1)}, bf16[2,128,128]{2,1,0:T(8,128)(2,1)S(1)}, u32[]{:S(2)}, u32[]{:S(2)}) collective-permute-start(bf16[2,128,128]{2,1,0:T(8,128)(2,1)S(1)} %get-tuple-element.22), channel_id=1, source_target_pairs={{0,128},{1,129},{2,130},{3,131},{4,132},{5,133},{6,134},{7,135},{8... | collective-permute-start | bytes 196616 | tf_op jit(solution)/shard_map/ppermute | solution.py:31
  13.5 8.3 %collective-permute-start.2 = (bf16[2,128,128]{2,1,0:T(8,128)(2,1)S(1)}, bf16[2,128,128]{2,1,0:T(8,128)(2,1)S(1)}, u32[]{:S(2)}, u32[]{:S(2)}) collective-permute-start(bf16[2,128,128]{2,1,0:T(8,128)(2,1)S(1)} %get-tuple-element.22), channel_id=1, source_target_pairs={{0,96},{1,97},{2,98},{3,99},{4,100},{5,101},{6,102},{7,103},{8,104... | collective-permute-start | bytes 196616 | tf_op jit(solution)/shard_map/ppermute | solution.py:31
  14.4 10.4 %collective-permute-start.11 = (bf16[2,3,128,128]{3,2,0,1:T(8,128)(2,1)S(1)}, bf16[2,3,128,128]{3,2,0,1:T(8,128)(2,1)S(1)}, u32[]{:S(2)}, u32[]{:S(2)}) collective-permute-start(bf16[2,3,128,128]{3,2,0,1:T(8,128)(2,1)S(1)} %pad_maximum_fusion), channel_id=1, source_target_pairs={{0,8},{1,9},{2,10},{3,11},{4,12},{5,13},{6,14},{7,15},{8,0},{9,1},... | collective-permute-start | bytes 589832 | tf_op jit(solution)/shard_map/ppermute | solution.py:31
  17.4 8.2 %collective-permute-start.10 = (bf16[2,3,128,128]{3,2,0,1:T(8,128)(2,1)S(1)}, bf16[2,3,128,128]{3,2,0,1:T(8,128)(2,1)S(1)}, u32[]{:S(2)}, u32[]{:S(2)}) collective-permute-start(bf16[2,3,128,128]{3,2,0,1:T(8,128)(2,1)S(1)} %pad_maximum_fusion), channel_id=1, source_target_pairs={{0,12},{1,13},{2,14},{3,15},{4,0},{5,1},{6,2},{7,3},{8,4},{9,5},{1... | collective-permute-start | bytes 589832 | tf_op jit(solution)/shard_map/ppermute | solution.py:31
  18.2 8.4 %collective-permute-start.9 = (bf16[2,3,128,128]{3,2,0,1:T(8,128)(2,1)S(1)}, bf16[2,3,128,128]{3,2,0,1:T(8,128)(2,1)S(1)}, u32[]{:S(2)}, u32[]{:S(2)}) collective-permute-start(bf16[2,3,128,128]{3,2,0,1:T(8,128)(2,1)S(1)} %pad_maximum_fusion), channel_id=1, source_target_pairs={{0,4},{1,5},{2,6},{3,7},{4,8},{5,9},{6,10},{7,11},{8,12},{9,13},{1... | collective-permute-start | bytes 589832 | tf_op jit(solution)/shard_map/ppermute | solution.py:31
  21.8 8.5 %collective-permute-start.6 = (bf16[2,2,128,128]{3,2,1,0:T(8,128)(2,1)S(1)}, bf16[2,2,128,128]{3,2,1,0:T(8,128)(2,1)S(1)}, u32[]{:S(2)}, u32[]{:S(2)}) collective-permute-start(bf16[2,2,128,128]{3,2,1,0:T(8,128)(2,1)S(1)} %pad_maximum_fusion.1.k0), channel_id=1, source_target_pairs={{0,8},{1,9},{2,10},{3,11},{4,12},{5,13},{6,14},{7,15},{8,0},{9,1},... | collective-permute-start | bytes 393224 | tf_op jit(solution)/shard_map/ppermute | solution.py:31
  24.8 5.9 %collective-permute-start.5 = (bf16[2,2,128,128]{3,2,1,0:T(8,128)(2,1)S(1)}, bf16[2,2,128,128]{3,2,1,0:T(8,128)(2,1)S(1)}, u32[]{:S(2)}, u32[]{:S(2)}) collective-permute-start(bf16[2,2,128,128]{3,2,1,0:T(8,128)(2,1)S(1)} %pad_maximum_fusion.1.k0), channel_id=1, source_target_pairs={{0,12},{1,13},{2,14},{3,15},{4,0},{5,1},{6,2},{7,3},{8,4},{9,5},{1... | collective-permute-start | bytes 393224 | tf_op jit(solution)/shard_map/ppermute | solution.py:31
  25.6 6.1 %collective-permute-start.4 = (bf16[2,2,128,128]{3,2,1,0:T(8,128)(2,1)S(1)}, bf16[2,2,128,128]{3,2,1,0:T(8,128)(2,1)S(1)}, u32[]{:S(2)}, u32[]{:S(2)}) collective-permute-start(bf16[2,2,128,128]{3,2,1,0:T(8,128)(2,1)S(1)} %pad_maximum_fusion.1.k0), channel_id=1, source_target_pairs={{0,4},{1,5},{2,6},{3,7},{4,8},{5,9},{6,10},{7,11},{8,12},{9,13},{1... | collective-permute-start | bytes 393224 | tf_op jit(solution)/shard_map/ppermute | solution.py:31
  26.6 7.1 %slice-start = ((s8[8388608]{0:T(1024)(128)(4,1)}), s8[4194304]{0:T(1024)(128)(4,1)S(1)}, s32[]{:S(2)}) async-start(s8[8388608]{0:T(1024)(128)(4,1)} %bitcast.24), calls=%async_computation | async-start | bytes 8388608
  31.8 2.2 %slice-start.1 = ((s8[8388608]{0:T(1024)(128)(4,1)}), s8[4194304]{0:T(1024)(128)(4,1)S(1)}, s32[]{:S(2)}) async-start(s8[8388608]{0:T(1024)(128)(4,1)} %bitcast.24), calls=%async_computation.1 | async-start | bytes 8388608
  35.3 5.2 %collective-permute-start.12 = (bf16[64,2048]{1,0:T(8,128)(2,1)S(1)}, bf16[64,2048]{1,0:T(8,128)(2,1)S(1)}, u32[]{:S(2)}, u32[]{:S(2)}) collective-permute-start(bf16[64,2048]{1,0:T(8,128)(2,1)S(1)} %shard_map.58), channel_id=1, source_target_pairs={{0,1},{1,0},{2,3},{3,2},{4,5},{5,4},{6,7},{7,6},{8,9},{9,8},{10,11... | collective-permute-start | bytes 786440 | tf_op jit(solution)/shard_map/ppermute | solution.py:31
  40.6 9.1 %collective-permute-start.15 = (bf16[64,2048]{1,0:T(8,128)(2,1)S(1)}, bf16[64,2048]{1,0:T(8,128)(2,1)S(1)}, u32[]{:S(2)}, u32[]{:S(2)}) collective-permute-start(bf16[64,2048]{1,0:T(8,128)(2,1)S(1)} %add_convert_fusion.1), channel_id=1, source_target_pairs={{0,18},{1,19},{2,16},{3,17},{4,22},{5,23},{6,20},{7,21},{8,26},{9,... | collective-permute-start | bytes 786440 | tf_op jit(solution)/shard_map/ppermute | solution.py:31
  47.4 1.5 %collective-permute-start.13 = (bf16[64,1024]{1,0:T(8,128)(2,1)S(1)}, bf16[64,1024]{1,0:T(8,128)(2,1)S(1)}, u32[]{:S(2)}, u32[]{:S(2)}) collective-permute-start(bf16[64,1024]{1,0:T(8,128)(2,1)S(1)} %get-tuple-element.16), channel_id=1, source_target_pairs={{0,1},{1,0},{2,3},{3,2},{4,5},{5,4},{6,7},{7,6},{8,9},{9,8},{10,11... | collective-permute-start | bytes 393224 | tf_op jit(solution)/shard_map/ppermute | solution.py:31
  48.0 1.3 %collective-permute-start.14 = (bf16[64,1024]{1,0:T(8,128)(2,1)S(1)}, bf16[64,1024]{1,0:T(8,128)(2,1)S(1)}, u32[]{:S(2)}, u32[]{:S(2)}) collective-permute-start(bf16[64,1024]{1,0:T(8,128)(2,1)S(1)} %get-tuple-element.17), channel_id=1, source_target_pairs={{0,1},{1,0},{2,3},{3,2},{4,5},{5,4},{6,7},{7,6},{8,9},{9,8},{10,11... | collective-permute-start | bytes 393224 | tf_op jit(solution)/shard_map/ppermute | solution.py:31
  49.8 8.4 %collective-permute-start.16 = (bf16[64,2048]{1,0:T(8,128)(2,1)S(1)}, bf16[64,2048]{1,0:T(8,128)(2,1)S(1)}, u32[]{:S(2)}, u32[]{:S(2)}) collective-permute-start(bf16[64,2048]{1,0:T(8,128)(2,1)S(1)} %add_convert_fusion.refs_0_), channel_id=1, source_target_pairs={{0,2},{1,3},{2,0},{3,1},{4,6},{5,7},{6,4},{7,5},{8,10},{9,11},{10,... | collective-permute-start | bytes 786440 | tf_op jit(solution)/shard_map/ppermute | solution.py:31
  51.4 8.7 %collective-permute-start.17 = (bf16[64,2048]{1,0:T(8,128)(2,1)S(1)}, bf16[64,2048]{1,0:T(8,128)(2,1)S(1)}, u32[]{:S(2)}, u32[]{:S(2)}) collective-permute-start(bf16[64,2048]{1,0:T(8,128)(2,1)S(1)} %add_convert_fusion.refs_0_), channel_id=1, source_target_pairs={{0,1},{1,0},{2,3},{3,2},{4,5},{5,4},{6,7},{7,6},{8,9},{9,8},{10,11... | collective-permute-start | bytes 786440 | tf_op jit(solution)/shard_map/ppermute | solution.py:31
  58.2 3.0 %collective-permute-start.18 = (bf16[64,2048]{1,0:T(8,128)(2,1)S(1)}, bf16[64,2048]{1,0:T(8,128)(2,1)S(1)}, u32[]{:S(2)}, u32[]{:S(2)}) collective-permute-start(bf16[64,2048]{1,0:T(8,128)(2,1)S(1)} %collective-permute-done.16.refs_1_), channel_id=1, source_target_pairs={{0,1},{1,0},{2,3},{3,2},{4,5},{5,4},{6,7},{7,6},{8,9},{9,8},{10,11... | collective-permute-start | bytes 786440 | tf_op jit(solution)/shard_map/ppermute | solution.py:31

commit v5 on v4

--- a/solution.py
+++ b/solution.py
@@ -17,7 +17,6 @@
 PIECES = 1
 LONG = pl.CostEstimate(flops=16 << 30, bytes_accessed=16 << 20, transcendentals=4 << 20)
 LIMIT = pltpu.CompilerParams(vmem_limit_bytes=24 * 1024 * 1024)
-SMEM = pl.BlockSpec(memory_space=pltpu.SMEM)
 VMEM = pl.BlockSpec(memory_space=pltpu.VMEM)
 HBM = pl.BlockSpec(memory_space=pl.ANY)
 
@@ -55,20 +54,20 @@
     return shift(array, lambda z, x, y, h, c: (z, x, (y + by) % NY, h, c))
 
 
-def row_limits(info, which, block):
-    z, x, y = info[0], info[1], info[2]
+def coordinates():
+    seq, tp = lax.axis_index("seq"), lax.axis_index("tp")
+    return seq // (NX * NY), (seq // NY) % NX, seq % NY, tp // NC, tp % NC
+
+
+def row_positions(which, block):
+    z, x, y, _, _ = coordinates()
     base = (z * NX + (1 - x if which else x)) * (NY * block) + y * block
-    last = base + lax.broadcasted_iota(jnp.int32, (block, 1), 0)
-    first = jnp.zeros_like(last)
-    for at in range(4):
-        start = info[4 + at]
-        first = jnp.where(start <= last, jnp.maximum(first, start), first)
-    return first, last
-
-
-def bias_of(info, which, layers, block):
-    z, x, y = info[0], info[1], info[2]
-    first, last = row_limits(info, which, block)
+    return base + lax.broadcasted_iota(jnp.int32, (block, 1), 0)
+
+
+def bias_of(first_ref, which, layers, block):
+    z, x, y, _, _ = coordinates()
+    first, last = first_ref[which, :, :1], row_positions(which, block)
     lane = lax.broadcasted_iota(jnp.int32, (1, 2 * block), 1)
     own, other = x * (NY * block), (1 - x) * (NY * block)
     within = jnp.where(lane < block, own + lane, other + lane - block)
@@ -102,11 +101,11 @@
     return highest, total, mixed
 
 
-def near_kernel(heads, size, block, info, own_ref, other_ref, k0, k1, k2, k3, mixed_ref, stat_ref):
+def near_kernel(heads, size, block, first_ref, own_ref, other_ref, k0, k1, k2, k3, mixed_ref, stat_ref):
     scale = math.log2(math.e) / math.sqrt(size)
     lane = lax.broadcasted_iota(jnp.int32, (block, 128), 1)
     for which, query_ref in enumerate((own_ref, other_ref)):
-        bias = bias_of(info, which, NEAR, block)
+        bias = bias_of(first_ref, which, NEAR, block)
         stats = jnp.zeros((block, 128), jnp.float32)
         for start in range(0, heads, GROUP):
             group = range(start, start + GROUP)
@@ -120,9 +119,9 @@
         stat_ref[which] = stats
 
 
-def far_block(heads, size, block, which, info, query_ref, kv_refs, mixed_ref, stat_ref, context_ref):
+def far_block(heads, size, block, which, first_ref, query_ref, kv_refs, mixed_ref, stat_ref, context_ref):
     scale = math.log2(math.e) / math.sqrt(size)
-    bias = bias_of(info, which, FAR, block)
+    bias = bias_of(first_ref, which, FAR, block)
     stats = stat_ref[which]
     for start in range(0, heads, GROUP):
         group = range(start, start + GROUP)
@@ -136,31 +135,33 @@
             context_ref[:, at] = ((mixed[part] + mixed_ref[which, :, at] * fade[part]) / whole).astype(jnp.bfloat16)
 
 
-def far_kernel(heads, size, block, info, query_ref, k0, k1, k2, k3, mixed_ref, stat_ref, context_ref):
-    far_block(heads, size, block, 1, info, query_ref, (k0, k1, k2, k3), mixed_ref, stat_ref, context_ref)
-
-
-def project(core, own_half, context_ref, weight_ref, out_ref, pieces=1, piece=0):
+def far_kernel(heads, size, block, first_ref, query_ref, k0, k1, k2, k3, mixed_ref, stat_ref, context_ref):
+    far_block(heads, size, block, 1, first_ref, query_ref, (k0, k1, k2, k3), mixed_ref, stat_ref, context_ref)
+
+
+def project(own_half, context_ref, weight_ref, out_ref, pieces=1, piece=0):
     width = out_ref.shape[1]
+    core = coordinates()[-1]
     which = core if own_half else 1 - core
     columns = pl.ds(pl.multiple_of((which * pieces + piece) * width, width), width)
     out_ref[...] = jnp.dot(context_ref[...], weight_ref[:, columns], preferred_element_type=jnp.float32).astype(out_ref.dtype)
 
 
-def project_kernel(own_half, info, context_ref, weight_ref, out_ref):
-    project(info[3], own_half, context_ref, weight_ref, out_ref)
-
-
-def far_project_kernel(heads, size, block, info, query_ref, k0, k1, k2, k3, mixed_ref, stat_ref, weight_ref, give0_ref, give1_ref, keep_ref, context_ref):
-    far_block(heads, size, block, 0, info, query_ref, (k0, k1, k2, k3), mixed_ref, stat_ref, context_ref)
-    project(info[3], False, context_ref, weight_ref, give0_ref, 2, 0)
-    project(info[3], False, context_ref, weight_ref, give1_ref, 2, 1)
-    project(info[3], True, context_ref, weight_ref, keep_ref)
-
-
-def place_kernel(pieces, info, *refs):
+def project_kernel(own_half, context_ref, weight_ref, out_ref):
+    project(own_half, context_ref, weight_ref, out_ref)
+
+
+def far_project_kernel(heads, size, block, first_ref, query_ref, k0, k1, k2, k3, mixed_ref, stat_ref, weight_ref, give0_ref, give1_ref, keep_ref, context_ref):
+    far_block(heads, size, block, 0, first_ref, query_ref, (k0, k1, k2, k3), mixed_ref, stat_ref, context_ref)
+    project(False, context_ref, weight_ref, give0_ref, 2, 0)
+    project(False, context_ref, weight_ref, give1_ref, 2, 1)
+    project(True, context_ref, weight_ref, keep_ref)
+
+
+def place_kernel(pieces, *refs):
     parts, out_ref, sems = refs[:4 * pieces], refs[-2], refs[-1]
-    batch, core = info[8], info[3]
+    _, x, _, high, core = coordinates()
+    batch = x ^ high
     width = parts[0].shape[1]
     copies = []
     for i, part in enumerate(parts):
@@ -179,9 +180,7 @@
     size = key_projected.shape[2]
     heads = width // size
     features = out_weight.shape[1]
-    seq, tp = lax.axis_index("seq"), lax.axis_index("tp")
-    z, x, y = seq // (NX * NY), (seq // NY) % NX, seq % NY
-    high, core = tp // NC, tp % NC
+    z, x, y, high, core = coordinates()
     batch = x ^ high
     pick = lambda a, i: lax.dynamic_index_in_dim(a, i, 0, keepdims=False)
 
@@ -199,7 +198,9 @@
 
     seg = pick(segments, batch)
     starts = jnp.sum((seg[None, :] < jnp.arange(4, dtype=jnp.int32)[:, None]).astype(jnp.int32), axis=1)
-    info = jnp.concatenate([jnp.stack([z, x, y, core]).astype(jnp.int32), starts, batch[None].astype(jnp.int32)])
+    positions = jnp.stack([row_positions(which, block) for which in (0, 1)])
+    first = jnp.max(jnp.where(starts <= positions, starts, 0), axis=2, keepdims=True)
+    first = jnp.broadcast_to(first, (2, block, 128))
 
     mixed, stats = pl.pallas_call(
         functools.partial(near_kernel, heads, size, block),
@@ -207,29 +208,29 @@
             jax.ShapeDtypeStruct((2, block, width), jnp.float32),
             jax.ShapeDtypeStruct((2, block, 128), jnp.float32),
         ),
-        in_specs=[SMEM] + [VMEM] * 6,
+        in_specs=[VMEM] * 7,
         out_specs=(VMEM, VMEM),
         compiler_params=LIMIT,
         cost_estimate=LONG,
-    )(info, own_q, other_q, *near_all)
+    )(first, own_q, other_q, *near_all)
 
     other_context = pl.pallas_call(
         functools.partial(far_kernel, heads, size, block),
         out_shape=jax.ShapeDtypeStruct((block, width), jnp.bfloat16),
-        in_specs=[SMEM] + [VMEM] * 7,
+        in_specs=[VMEM] * 8,
         out_specs=VMEM,
         compiler_params=LIMIT,
         cost_estimate=LONG,
-    )(info, other_q, *far_all, mixed, stats)
+    )(first, other_q, *far_all, mixed, stats)
 
     def projected(own_half, dtype):
         return pl.pallas_call(
             functools.partial(project_kernel, own_half),
             out_shape=jax.ShapeDtypeStruct((block, features // 2), dtype),
-            in_specs=[SMEM, VMEM, VMEM],
+            in_specs=[VMEM, VMEM],
             out_specs=VMEM,
             compiler_params=LIMIT,
-        )(info, other_context, out_weight)
+        )(other_context, out_weight)
 
     def cut(array):
         return jnp.split(array, PIECES, axis=1)
@@ -245,11 +246,11 @@
             jax.ShapeDtypeStruct((block, features // 4), jnp.bfloat16),
             jax.ShapeDtypeStruct((block, features // 2), jnp.float32),
         ),
-        in_specs=[SMEM] + [VMEM] * 8,
+        in_specs=[VMEM] * 9,
         out_specs=(VMEM, VMEM, VMEM),
         scratch_shapes=[pltpu.VMEM((block, width), jnp.bfloat16)],
         compiler_params=LIMIT,
-    )(info, own_q, *far_all, mixed, stats, out_weight)
+    )(first, own_q, *far_all, mixed, stats, out_weight)
     given = jnp.concatenate([swap_core(given0), swap_core(given1)], axis=1)
     summed = kept + given.astype(jnp.float32)
 
@@ -260,11 +261,11 @@
     return pl.pallas_call(
         functools.partial(place_kernel, PIECES),
         out_shape=jax.ShapeDtypeStruct((batches, block, features), jnp.bfloat16),
-        in_specs=[SMEM] + [VMEM] * len(parts),
+        in_specs=[VMEM] * len(parts),
         out_specs=HBM,
         scratch_shapes=[pltpu.SemaphoreType.DMA((len(parts),))],
         compiler_params=LIMIT,
-    )(info, *parts)
+    )(*parts)
 
 
 def solution(mesh):

time: 63.6 us -> 61.7 us (0.970)
  Pallas kernels: 14.1 us -> 10.8 us
  waiting for transfers between devices: 13.4 us -> 14.2 us
    pallas_call x2, Pallas kernels: 2.76 us -> 1.67 us  [projected(): pl.pallas_call(functools.partial(project_kernel, own_half), out_shape=jax...]
    ppermute x19, waiting for transfers between devices: 13.4 us -> 14.2 us  [shift(): lax.ppermute(array, AXES, [(flat(*d), flat(*move(*d))) for d in devices])]
  transfers between devices with their start and end apart: 19 -> 19, of which waited for: 10 -> 10; matrix products, arithmetic and copies ran while one was open for 2% -> 2% of each run, Pallas kernels for 15% -> 12%
where the time goes in v5:
time: 61.7 us; the launch traced here: 61.4 us
  starting transfers between devices  32.8 us (53%)
  waiting for transfers between devices  14.2 us (23%)
  Pallas kernels  10.8 us (18%)
  local copies, waits for them, and re-layouts  1.96 us (3%)
  other arithmetic  1.21 us (2%)
    ppermute x19, starting transfers between devices, shift(): lax.ppermute(array, AXES, [(flat(*d), flat(*move(*d))) for d in devices])  32.8 us
    ppermute x19, waiting for transfers between devices, shift(): lax.ppermute(array, AXES, [(flat(*d), flat(*move(*d))) for d in devices])  14.2 us
    pallas_call x1, Pallas kernels, body(): pl.pallas_call(functools.partial(far_project_kernel, heads, size, block),...  3.73 us
    pallas_call x1, Pallas kernels, body(): pl.pallas_call(functools.partial(near_kernel, heads, size, block), out_sh...  2.99 us
    pallas_call x2, Pallas kernels, projected(): pl.pallas_call(functools.partial(project_kernel, own_half), out_shape=jax...  1.67 us
    pallas_call x1, Pallas kernels, body(): pl.pallas_call(functools.partial(far_kernel, heads, size, block), out_sha...  1.37 us
  transfers between devices with their start and end apart: 19, of which 10 were waited for; matrix products, arithmetic and copies ran while one was open for 2% of the time, Pallas kernels for 12%

profile of v5, /device:TPU:1, one launch (start us, length us, event | category | flops | bytes accessed | tf_op | source)
XLA Modules:
  0.0 61.4 jit_solution(9297038529657235416)
XLA Ops:
  0.0 0.8 %fusion.3 = (bf16[2,64,128]{2,1,0:T(8,128)(2,1)S(1)}, bf16[2,64,128]{2,1,0:T(8,128)(2,1)S(1)}) fusion(s32[]{:T(128)S(6)} %select_n.49, bf16[2,1,64,128]{3,2,0,1:T(8,128)(2,1)} %bitcast.28, bf16[2,1,64,128]{3,2,0,1:T(8,128)(2,1)} %bitcast.29, s32[]{:T(128)S(6)} %select_n.53), kind=kLoop, calls=%fused_computation.16 | loop fusion | flops 32768 | bytes 131080 | tf_op jit(solution)/shard_map/jit(dynamic_index_in_dim)/squeeze | solution.py:185
  0.8 2.1 %collective-permute-start.1 = (bf16[2,64,128]{2,1,0:T(8,128)(2,1)S(1)}, bf16[2,64,128]{2,1,0:T(8,128)(2,1)S(1)}, u32[]{:S(2)}, u32[]{:S(2)}) collective-permute-start(bf16[2,64,128]{2,1,0:T(8,128)(2,1)S(1)} %get-tuple-element.24), channel_id=1, source_target_pairs={{0,16},{1,17},{2,18},{3,19},{4,20},{5,21},{6,22},{7,23},{8,24},{9,... | collective-permute-start | bytes 98312 | tf_op jit(solution)/shard_map/ppermute | solution.py:30
  2.9 1.0 %dynamic-slice_bitcast_fusion = (bf16[64,1024]{1,0:T(8,128)(2,1)S(1)}, bf16[64,1024]{1,0:T(8,128)(2,1)S(1)}) fusion(bf16[2,64,1024]{2,1,0:T(8,128)(2,1)} %param.5, s32[]{:T(128)S(6)} %select_n.49, s32[]{:T(128)S(6)} %select_n.53), kind=kLoop, calls=%fused_computation.4 | loop fusion | bytes 524296 | tf_op jit(solution)/shard_map/jit(dynamic_index_in_dim)/squeeze | solution.py:185
  3.9 0.1 collective-permute-start
  4.1 0.1 convert_reduce_fusion
  4.2 0.0 collective-permute-done.1
  4.3 1.9 %collective-permute-start.7 = (bf16[2,128,128]{2,1,0:T(8,128)(2,1)S(1)}, bf16[2,128,128]{2,1,0:T(8,128)(2,1)S(1)}, u32[]{:S(2)}, u32[]{:S(2)}) collective-permute-start(bf16[2,128,128]{2,1,0:T(8,128)(2,1)S(1)} %get-tuple-element.22), channel_id=1, source_target_pairs={{0,32},{1,33},{2,34},{3,35},{4,36},{5,37},{6,38},{7,39},{8,40},{9,... | collective-permute-start | bytes 196616 | tf_op jit(solution)/shard_map/ppermute | solution.py:30
  6.2 3.0 %collective-permute-start.8 = (bf16[2,128,128]{2,1,0:T(8,128)(2,1)S(1)}, bf16[2,128,128]{2,1,0:T(8,128)(2,1)S(1)}, u32[]{:S(2)}, u32[]{:S(2)}) collective-permute-start(bf16[2,128,128]{2,1,0:T(8,128)(2,1)S(1)} %get-tuple-element.22), channel_id=1, source_target_pairs={{0,64},{1,65},{2,66},{3,67},{4,68},{5,69},{6,70},{7,71},{8,72},{9,... | collective-permute-start | bytes 196616 | tf_op jit(solution)/shard_map/ppermute | solution.py:30
  9.2 4.2 %collective-permute-start.3 = (bf16[2,128,128]{2,1,0:T(8,128)(2,1)S(1)}, bf16[2,128,128]{2,1,0:T(8,128)(2,1)S(1)}, u32[]{:S(2)}, u32[]{:S(2)}) collective-permute-start(bf16[2,128,128]{2,1,0:T(8,128)(2,1)S(1)} %get-tuple-element.22), channel_id=1, source_target_pairs={{0,128},{1,129},{2,130},{3,131},{4,132},{5,133},{6,134},{7,135},{8... | collective-permute-start | bytes 196616 | tf_op jit(solution)/shard_map/ppermute | solution.py:30
  13.4 0.0 collective-permute-start.2
  13.4 1.0 %collective-permute-done.8 = bf16[2,128,128]{2,1,0:T(8,128)(2,1)S(1)} collective-permute-done((bf16[2,128,128]{2,1,0:T(8,128)(2,1)S(1)}, bf16[2,128,128]{2,1,0:T(8,128)(2,1)S(1)}, u32[]{:S(2)}, u32[]{:S(2)}) %collective-permute-start.8) | collective-permute-done | bytes 65568 | tf_op jit(solution)/shard_map/ppermute | solution.py:30
  14.4 3.0 %collective-permute-start.11 = (bf16[2,3,128,128]{3,2,0,1:T(8,128)(2,1)S(1)}, bf16[2,3,128,128]{3,2,0,1:T(8,128)(2,1)S(1)}, u32[]{:S(2)}, u32[]{:S(2)}) collective-permute-start(bf16[2,3,128,128]{3,2,0,1:T(8,128)(2,1)S(1)} %pad_maximum_fusion), channel_id=1, source_target_pairs={{0,8},{1,9},{2,10},{3,11},{4,12},{5,13},{6,14},{7,15},{8,0},{9,1},... | collective-permute-start | bytes 589832 | tf_op jit(solution)/shard_map/ppermute | solution.py:30
  17.4 0.8 %collective-permute-start.10 = (bf16[2,3,128,128]{3,2,0,1:T(8,128)(2,1)S(1)}, bf16[2,3,128,128]{3,2,0,1:T(8,128)(2,1)S(1)}, u32[]{:S(2)}, u32[]{:S(2)}) collective-permute-start(bf16[2,3,128,128]{3,2,0,1:T(8,128)(2,1)S(1)} %pad_maximum_fusion), channel_id=1, source_target_pairs={{0,12},{1,13},{2,14},{3,15},{4,0},{5,1},{6,2},{7,3},{8,4},{9,5},{1... | collective-permute-start | bytes 589832 | tf_op jit(solution)/shard_map/ppermute | solution.py:30
  18.2 0.7 %collective-permute-start.9 = (bf16[2,3,128,128]{3,2,0,1:T(8,128)(2,1)S(1)}, bf16[2,3,128,128]{3,2,0,1:T(8,128)(2,1)S(1)}, u32[]{:S(2)}, u32[]{:S(2)}) collective-permute-start(bf16[2,3,128,128]{3,2,0,1:T(8,128)(2,1)S(1)} %pad_maximum_fusion), channel_id=1, source_target_pairs={{0,4},{1,5},{2,6},{3,7},{4,8},{5,9},{6,10},{7,11},{8,12},{9,13},{1... | collective-permute-start | bytes 589832 | tf_op jit(solution)/shard_map/ppermute | solution.py:30
  18.9 0.1 select_reduce_fusion
  19.0 2.7 %collective-permute-done.2 = bf16[2,128,128]{2,1,0:T(8,128)(2,1)S(1)} collective-permute-done((bf16[2,128,128]{2,1,0:T(8,128)(2,1)S(1)}, bf16[2,128,128]{2,1,0:T(8,128)(2,1)S(1)}, u32[]{:S(2)}, u32[]{:S(2)}) %collective-permute-start.2) | collective-permute-done | bytes 65568 | tf_op jit(solution)/shard_map/ppermute | solution.py:30
  21.8 3.0 %collective-permute-start.6 = (bf16[2,2,128,128]{3,2,1,0:T(8,128)(2,1)S(1)}, bf16[2,2,128,128]{3,2,1,0:T(8,128)(2,1)S(1)}, u32[]{:S(2)}, u32[]{:S(2)}) collective-permute-start(bf16[2,2,128,128]{3,2,1,0:T(8,128)(2,1)S(1)} %pad_maximum_fusion.1.k0), channel_id=1, source_target_pairs={{0,8},{1,9},{2,10},{3,11},{4,12},{5,13},{6,14},{7,15},{8,0},{9,1},... | collective-permute-start | bytes 393224 | tf_op jit(solution)/shard_map/ppermute | solution.py:30
  24.8 0.0 collective-permute-done.11
  24.8 0.8 %collective-permute-start.5 = (bf16[2,2,128,128]{3,2,1,0:T(8,128)(2,1)S(1)}, bf16[2,2,128,128]{3,2,1,0:T(8,128)(2,1)S(1)}, u32[]{:S(2)}, u32[]{:S(2)}) collective-permute-start(bf16[2,2,128,128]{3,2,1,0:T(8,128)(2,1)S(1)} %pad_maximum_fusion.1.k0), channel_id=1, source_target_pairs={{0,12},{1,13},{2,14},{3,15},{4,0},{5,1},{6,2},{7,3},{8,4},{9,5},{1... | collective-permute-start | bytes 393224 | tf_op jit(solution)/shard_map/ppermute | solution.py:30
  25.6 0.0 collective-permute-done.10
  25.6 0.9 %collective-permute-start.4 = (bf16[2,2,128,128]{3,2,1,0:T(8,128)(2,1)S(1)}, bf16[2,2,128,128]{3,2,1,0:T(8,128)(2,1)S(1)}, u32[]{:S(2)}, u32[]{:S(2)}) collective-permute-start(bf16[2,2,128,128]{3,2,1,0:T(8,128)(2,1)S(1)} %pad_maximum_fusion.1.k0), channel_id=1, source_target_pairs={{0,4},{1,5},{2,6},{3,7},{4,8},{5,9},{6,10},{7,11},{8,12},{9,13},{1... | collective-permute-start | bytes 393224 | tf_op jit(solution)/shard_map/ppermute | solution.py:30
  26.6 0.0 collective-permute-done.other_ref.query_ref
  26.6 0.1 broadcast_in_dim.9.first_ref
  26.7 3.0 %shard_map.55 = (f32[2,64,1024]{2,1,0:T(8,128)S(1)}, f32[2,64,128]{2,1,0:T(8,128)S(1)}) custom-call(s32[2,64,128]{2,1,0:T(8,128)S(1)} %broadcast_in_dim.9.first_ref, bf16[64,1024]{1,0:T(8,128)(2,1)S(1)} %get-tuple-element.14.own_ref.query_ref, bf16[64,1024]{1,0:T(8,128)(2,1)S(1)} %collective-permute-done.other_ref.query_ref, ...), custom_call_target="tpu_custom_call" | custom-call | flops 17179869184 | bytes 16777216 | tf_op jit(solution)/shard_map/pallas_call | solution.py:205
  29.7 0.0 collective-permute-done.6.k3
  29.7 1.1 %collective-permute-done.5.k2 = bf16[2,2,128,128]{3,2,1,0:T(8,128)(2,1)S(1)} collective-permute-done((bf16[2,2,128,128]{3,2,1,0:T(8,128)(2,1)S(1)}, bf16[2,2,128,128]{3,2,1,0:T(8,128)(2,1)S(1)}, u32[]{:S(2)}, u32[]{:S(2)}) %collective-permute-start.5) | collective-permute-done | bytes 131104 | tf_op jit(solution)/shard_map/ppermute | solution.py:30
  30.8 1.2 %collective-permute-done.4.k1 = bf16[2,2,128,128]{3,2,1,0:T(8,128)(2,1)S(1)} collective-permute-done((bf16[2,2,128,128]{3,2,1,0:T(8,128)(2,1)S(1)}, bf16[2,2,128,128]{3,2,1,0:T(8,128)(2,1)S(1)}, u32[]{:S(2)}, u32[]{:S(2)}) %collective-permute-start.4) | collective-permute-done | bytes 131104 | tf_op jit(solution)/shard_map/ppermute | solution.py:30
  32.0 1.4 %shard_map.56.context_ref = bf16[64,1024]{1,0:T(8,128)(2,1)S(1)} custom-call(s32[2,64,128]{2,1,0:T(8,128)S(1)} %broadcast_in_dim.9.first_ref, bf16[64,1024]{1,0:T(8,128)(2,1)S(1)} %collective-permute-done.other_ref.query_ref, bf16[2,2,128,128]{3,2,1,0:T(8,128)(2,1)S(1)} %pad_maximum_fusion.1.k0, bf16[2,2,128,128]{3,2,1,0:T(8,128)(2,1)S(1)} %collective-permute-done.4.k1, ...), custom_call_target="tpu_custom_call" | custom-call | flops 17179869184 | bytes 16777216 | tf_op jit(solution)/shard_map/pallas_call | solution.py:217
  33.4 0.8 %slice-done.1 = s8[4194304]{0:T(1024)(128)(4,1)S(1)} async-done(((s8[8388608]{0:T(1024)(128)(4,1)}), s8[4194304]{0:T(1024)(128)(4,1)S(1)}, s32[]{:S(2)}) %slice-start.1) | async-done | bytes 4194328
  34.2 0.8 %shard_map.58 = bf16[64,2048]{1,0:T(8,128)(2,1)S(1)} custom-call(bf16[64,1024]{1,0:T(8,128)(2,1)S(1)} %shard_map.56.context_ref, bf16[1024,4096]{1,0:T(8,128)(2,1)S(1)} %bitcast.22), custom_call_target="tpu_custom_call" | custom-call | tf_op jit(solution)/shard_map/pallas_call | solution.py:227
  35.0 3.6 %collective-permute-start.12 = (bf16[64,2048]{1,0:T(8,128)(2,1)S(1)}, bf16[64,2048]{1,0:T(8,128)(2,1)S(1)}, u32[]{:S(2)}, u32[]{:S(2)}) collective-permute-start(bf16[64,2048]{1,0:T(8,128)(2,1)S(1)} %shard_map.58), channel_id=1, source_target_pairs={{0,1},{1,0},{2,3},{3,2},{4,5},{5,4},{6,7},{7,6},{8,9},{9,8},{10,11... | collective-permute-start | bytes 786440 | tf_op jit(solution)/shard_map/ppermute | solution.py:30
  38.6 0.8 %shard_map.57 = f32[64,2048]{1,0:T(8,128)S(1)} custom-call(bf16[64,1024]{1,0:T(8,128)(2,1)S(1)} %shard_map.56.context_ref, bf16[1024,4096]{1,0:T(8,128)(2,1)S(1)} %bitcast.22), custom_call_target="tpu_custom_call" | custom-call | tf_op jit(solution)/shard_map/pallas_call | solution.py:227
  39.4 0.3 collective-permute-done.12
  39.8 2.6 %collective-permute-start.15 = (bf16[64,2048]{1,0:T(8,128)(2,1)S(1)}, bf16[64,2048]{1,0:T(8,128)(2,1)S(1)}, u32[]{:S(2)}, u32[]{:S(2)}) collective-permute-start(bf16[64,2048]{1,0:T(8,128)(2,1)S(1)} %add_convert_fusion.1), channel_id=1, source_target_pairs={{0,18},{1,19},{2,16},{3,17},{4,22},{5,23},{6,20},{7,21},{8,26},{9,... | collective-permute-start | bytes 786440 | tf_op jit(solution)/shard_map/ppermute | solution.py:30
  42.4 3.7 %shard_map.59 = (bf16[64,1024]{1,0:T(8,128)(2,1)S(1)}, bf16[64,1024]{1,0:T(8,128)(2,1)S(1)}, f32[64,2048]{1,0:T(8,128)S(1)}) custom-call(s32[2,64,128]{2,1,0:T(8,128)S(1)} %broadcast_in_dim.9.first_ref, bf16[64,1024]{1,0:T(8,128)(2,1)S(1)} %get-tuple-element.14.own_ref.query_ref, bf16[2,2,128,128]{3,2,1,0:T(8,128)(2,1)S(1)} %pad_maximum_fusion.1.k0, ...), custom_call_target="tpu_custom_call" | custom-call | tf_op jit(solution)/shard_map/pallas_call | solution.py:242
  46.1 0.7 %collective-permute-start.13 = (bf16[64,1024]{1,0:T(8,128)(2,1)S(1)}, bf16[64,1024]{1,0:T(8,128)(2,1)S(1)}, u32[]{:S(2)}, u32[]{:S(2)}) collective-permute-start(bf16[64,1024]{1,0:T(8,128)(2,1)S(1)} %get-tuple-element.16), channel_id=1, source_target_pairs={{0,1},{1,0},{2,3},{3,2},{4,5},{5,4},{6,7},{7,6},{8,9},{9,8},{10,11... | collective-permute-start | bytes 393224 | tf_op jit(solution)/shard_map/ppermute | solution.py:30
  46.9 0.1 collective-permute-start.14
  47.0 0.9 %collective-permute-done.13 = bf16[64,1024]{1,0:T(8,128)(2,1)S(1)} collective-permute-done((bf16[64,1024]{1,0:T(8,128)(2,1)S(1)}, bf16[64,1024]{1,0:T(8,128)(2,1)S(1)}, u32[]{:S(2)}, u32[]{:S(2)}) %collective-permute-start.13) | collective-permute-done | bytes 131104 | tf_op jit(solution)/shard_map/ppermute | solution.py:30
  47.8 0.4 collective-permute-done.14
  48.2 0.4 collective-permute-done.15
  48.6 0.1 add_convert_fusion.refs_0_
  48.7 1.6 %collective-permute-start.16 = (bf16[64,2048]{1,0:T(8,128)(2,1)S(1)}, bf16[64,2048]{1,0:T(8,128)(2,1)S(1)}, u32[]{:S(2)}, u32[]{:S(2)}) collective-permute-start(bf16[64,2048]{1,0:T(8,128)(2,1)S(1)} %add_convert_fusion.refs_0_), channel_id=1, source_target_pairs={{0,2},{1,3},{2,0},{3,1},{4,6},{5,7},{6,4},{7,5},{8,10},{9,11},{10,... | collective-permute-start | bytes 786440 | tf_op jit(solution)/shard_map/ppermute | solution.py:30
  50.3 1.5 %collective-permute-start.17 = (bf16[64,2048]{1,0:T(8,128)(2,1)S(1)}, bf16[64,2048]{1,0:T(8,128)(2,1)S(1)}, u32[]{:S(2)}, u32[]{:S(2)}) collective-permute-start(bf16[64,2048]{1,0:T(8,128)(2,1)S(1)} %add_convert_fusion.refs_0_), channel_id=1, source_target_pairs={{0,1},{1,0},{2,3},{3,2},{4,5},{5,4},{6,7},{7,6},{8,9},{9,8},{10,11... | collective-permute-start | bytes 786440 | tf_op jit(solution)/shard_map/ppermute | solution.py:30
  51.8 5.1 %collective-permute-done.16.refs_1_ = bf16[64,2048]{1,0:T(8,128)(2,1)S(1)} collective-permute-done((bf16[64,2048]{1,0:T(8,128)(2,1)S(1)}, bf16[64,2048]{1,0:T(8,128)(2,1)S(1)}, u32[]{:S(2)}, u32[]{:S(2)}) %collective-permute-start.16) | collective-permute-done | bytes 262176 | tf_op jit(solution)/shard_map/ppermute | solution.py:30
  56.9 2.1 %collective-permute-start.18 = (bf16[64,2048]{1,0:T(8,128)(2,1)S(1)}, bf16[64,2048]{1,0:T(8,128)(2,1)S(1)}, u32[]{:S(2)}, u32[]{:S(2)}) collective-permute-start(bf16[64,2048]{1,0:T(8,128)(2,1)S(1)} %collective-permute-done.16.refs_1_), channel_id=1, source_target_pairs={{0,1},{1,0},{2,3},{3,2},{4,5},{5,4},{6,7},{7,6},{8,9},{9,8},{10,11... | collective-permute-start | bytes 786440 | tf_op jit(solution)/shard_map/ppermute | solution.py:30
  59.0 0.0 collective-permute-done.17.refs_2_
  59.0 1.2 %collective-permute-done.18.refs_3_ = bf16[64,2048]{1,0:T(8,128)(2,1)S(1)} collective-permute-done((bf16[64,2048]{1,0:T(8,128)(2,1)S(1)}, bf16[64,2048]{1,0:T(8,128)(2,1)S(1)}, u32[]{:S(2)}, u32[]{:S(2)}) %collective-permute-start.18) | collective-permute-done | bytes 262176 | tf_op jit(solution)/shard_map/ppermute | solution.py:30
  60.2 1.0 %shard_map.60 = bf16[2,64,4096]{2,1,0:T(8,128)(2,1)} custom-call(bf16[64,2048]{1,0:T(8,128)(2,1)S(1)} %add_convert_fusion.refs_0_, bf16[64,2048]{1,0:T(8,128)(2,1)S(1)} %collective-permute-done.16.refs_1_, bf16[64,2048]{1,0:T(8,128)(2,1)S(1)} %collective-permute-done.17.refs_2_, bf16[64,2048]{1,0:T(8,128)(2,1)S(1)} %collective-permute-done.18.refs_3_), custom_call_target="tpu_custom_call" | custom-call | tf_op jit(solution)/shard_map/pallas_call | solution.py:261
  (20 shorter events, 0.2 us)
Async XLA Ops:
  0.0 4.0 %copy-start = (s32[2,4096]{1,0:T(2,128)S(1)}, s32[2,4096]{1,0:T(2,128)}, u32[]{:S(2)}) copy-start(s32[2,4096]{1,0:T(2,128)} %param.8) | copy-start | bytes 98308
  0.8 3.4 %collective-permute-start.1 = (bf16[2,64,128]{2,1,0:T(8,128)(2,1)S(1)}, bf16[2,64,128]{2,1,0:T(8,128)(2,1)S(1)}, u32[]{:S(2)}, u32[]{:S(2)}) collective-permute-start(bf16[2,64,128]{2,1,0:T(8,128)(2,1)S(1)} %get-tuple-element.24), channel_id=1, source_target_pairs={{0,16},{1,17},{2,18},{3,19},{4,20},{5,21},{6,22},{7,23},{8,24},{9,... | collective-permute-start | bytes 98312 | tf_op jit(solution)/shard_map/ppermute | solution.py:30
  3.9 22.7 %collective-permute-start = (bf16[64,1024]{1,0:T(8,128)(2,1)S(1)}, bf16[64,1024]{1,0:T(8,128)(2,1)S(1)}, u32[]{:S(2)}, u32[]{:S(2)}) collective-permute-start(bf16[64,1024]{1,0:T(8,128)(2,1)S(1)} %get-tuple-element.20), channel_id=1, source_target_pairs={{0,16},{1,17},{2,18},{3,19},{4,20},{5,21},{6,22},{7,23},{8,24},{9,... | collective-permute-start | bytes 393224 | tf_op jit(solution)/shard_map/ppermute | solution.py:30
  4.3 9.2 %collective-permute-start.7 = (bf16[2,128,128]{2,1,0:T(8,128)(2,1)S(1)}, bf16[2,128,128]{2,1,0:T(8,128)(2,1)S(1)}, u32[]{:S(2)}, u32[]{:S(2)}) collective-permute-start(bf16[2,128,128]{2,1,0:T(8,128)(2,1)S(1)} %get-tuple-element.22), channel_id=1, source_target_pairs={{0,32},{1,33},{2,34},{3,35},{4,36},{5,37},{6,38},{7,39},{8,40},{9,... | collective-permute-start | bytes 196616 | tf_op jit(solution)/shard_map/ppermute | solution.py:30
  6.2 8.2 %collective-permute-start.8 = (bf16[2,128,128]{2,1,0:T(8,128)(2,1)S(1)}, bf16[2,128,128]{2,1,0:T(8,128)(2,1)S(1)}, u32[]{:S(2)}, u32[]{:S(2)}) collective-permute-start(bf16[2,128,128]{2,1,0:T(8,128)(2,1)S(1)} %get-tuple-element.22), channel_id=1, source_target_pairs={{0,64},{1,65},{2,66},{3,67},{4,68},{5,69},{6,70},{7,71},{8,72},{9,... | collective-permute-start | bytes 196616 | tf_op jit(solution)/shard_map/ppermute | solution.py:30
  9.2 9.0 %collective-permute-start.3 = (bf16[2,128,128]{2,1,0:T(8,128)(2,1)S(1)}, bf16[2,128,128]{2,1,0:T(8,128)(2,1)S(1)}, u32[]{:S(2)}, u32[]{:S(2)}) collective-permute-start(bf16[2,128,128]{2,1,0:T(8,128)(2,1)S(1)} %get-tuple-element.22), channel_id=1, source_target_pairs={{0,128},{1,129},{2,130},{3,131},{4,132},{5,133},{6,134},{7,135},{8... | collective-permute-start | bytes 196616 | tf_op jit(solution)/shard_map/ppermute | solution.py:30
  13.4 8.4 %collective-permute-start.2 = (bf16[2,128,128]{2,1,0:T(8,128)(2,1)S(1)}, bf16[2,128,128]{2,1,0:T(8,128)(2,1)S(1)}, u32[]{:S(2)}, u32[]{:S(2)}) collective-permute-start(bf16[2,128,128]{2,1,0:T(8,128)(2,1)S(1)} %get-tuple-element.22), channel_id=1, source_target_pairs={{0,96},{1,97},{2,98},{3,99},{4,100},{5,101},{6,102},{7,103},{8,104... | collective-permute-start | bytes 196616 | tf_op jit(solution)/shard_map/ppermute | solution.py:30
  14.4 10.4 %collective-permute-start.11 = (bf16[2,3,128,128]{3,2,0,1:T(8,128)(2,1)S(1)}, bf16[2,3,128,128]{3,2,0,1:T(8,128)(2,1)S(1)}, u32[]{:S(2)}, u32[]{:S(2)}) collective-permute-start(bf16[2,3,128,128]{3,2,0,1:T(8,128)(2,1)S(1)} %pad_maximum_fusion), channel_id=1, source_target_pairs={{0,8},{1,9},{2,10},{3,11},{4,12},{5,13},{6,14},{7,15},{8,0},{9,1},... | collective-permute-start | bytes 589832 | tf_op jit(solution)/shard_map/ppermute | solution.py:30
  17.4 8.2 %collective-permute-start.10 = (bf16[2,3,128,128]{3,2,0,1:T(8,128)(2,1)S(1)}, bf16[2,3,128,128]{3,2,0,1:T(8,128)(2,1)S(1)}, u32[]{:S(2)}, u32[]{:S(2)}) collective-permute-start(bf16[2,3,128,128]{3,2,0,1:T(8,128)(2,1)S(1)} %pad_maximum_fusion), channel_id=1, source_target_pairs={{0,12},{1,13},{2,14},{3,15},{4,0},{5,1},{6,2},{7,3},{8,4},{9,5},{1... | collective-permute-start | bytes 589832 | tf_op jit(solution)/shard_map/ppermute | solution.py:30
  18.2 8.4 %collective-permute-start.9 = (bf16[2,3,128,128]{3,2,0,1:T(8,128)(2,1)S(1)}, bf16[2,3,128,128]{3,2,0,1:T(8,128)(2,1)S(1)}, u32[]{:S(2)}, u32[]{:S(2)}) collective-permute-start(bf16[2,3,128,128]{3,2,0,1:T(8,128)(2,1)S(1)} %pad_maximum_fusion), channel_id=1, source_target_pairs={{0,4},{1,5},{2,6},{3,7},{4,8},{5,9},{6,10},{7,11},{8,12},{9,13},{1... | collective-permute-start | bytes 589832 | tf_op jit(solution)/shard_map/ppermute | solution.py:30
  21.8 7.9 %collective-permute-start.6 = (bf16[2,2,128,128]{3,2,1,0:T(8,128)(2,1)S(1)}, bf16[2,2,128,128]{3,2,1,0:T(8,128)(2,1)S(1)}, u32[]{:S(2)}, u32[]{:S(2)}) collective-permute-start(bf16[2,2,128,128]{3,2,1,0:T(8,128)(2,1)S(1)} %pad_maximum_fusion.1.k0), channel_id=1, source_target_pairs={{0,8},{1,9},{2,10},{3,11},{4,12},{5,13},{6,14},{7,15},{8,0},{9,1},... | collective-permute-start | bytes 393224 | tf_op jit(solution)/shard_map/ppermute | solution.py:30
  24.8 6.0 %collective-permute-start.5 = (bf16[2,2,128,128]{3,2,1,0:T(8,128)(2,1)S(1)}, bf16[2,2,128,128]{3,2,1,0:T(8,128)(2,1)S(1)}, u32[]{:S(2)}, u32[]{:S(2)}) collective-permute-start(bf16[2,2,128,128]{3,2,1,0:T(8,128)(2,1)S(1)} %pad_maximum_fusion.1.k0), channel_id=1, source_target_pairs={{0,12},{1,13},{2,14},{3,15},{4,0},{5,1},{6,2},{7,3},{8,4},{9,5},{1... | collective-permute-start | bytes 393224 | tf_op jit(solution)/shard_map/ppermute | solution.py:30
  25.6 6.4 %collective-permute-start.4 = (bf16[2,2,128,128]{3,2,1,0:T(8,128)(2,1)S(1)}, bf16[2,2,128,128]{3,2,1,0:T(8,128)(2,1)S(1)}, u32[]{:S(2)}, u32[]{:S(2)}) collective-permute-start(bf16[2,2,128,128]{3,2,1,0:T(8,128)(2,1)S(1)} %pad_maximum_fusion.1.k0), channel_id=1, source_target_pairs={{0,4},{1,5},{2,6},{3,7},{4,8},{5,9},{6,10},{7,11},{8,12},{9,13},{1... | collective-permute-start | bytes 393224 | tf_op jit(solution)/shard_map/ppermute | solution.py:30
  26.7 6.7 %slice-start = ((s8[8388608]{0:T(1024)(128)(4,1)}), s8[4194304]{0:T(1024)(128)(4,1)S(1)}, s32[]{:S(2)}) async-start(s8[8388608]{0:T(1024)(128)(4,1)} %bitcast.21), calls=%async_computation | async-start | bytes 8388608
  32.0 2.2 %slice-start.1 = ((s8[8388608]{0:T(1024)(128)(4,1)}), s8[4194304]{0:T(1024)(128)(4,1)S(1)}, s32[]{:S(2)}) async-start(s8[8388608]{0:T(1024)(128)(4,1)} %bitcast.21), calls=%async_computation.1 | async-start | bytes 8388608
  35.0 4.8 %collective-permute-start.12 = (bf16[64,2048]{1,0:T(8,128)(2,1)S(1)}, bf16[64,2048]{1,0:T(8,128)(2,1)S(1)}, u32[]{:S(2)}, u32[]{:S(2)}) collective-permute-start(bf16[64,2048]{1,0:T(8,128)(2,1)S(1)} %shard_map.58), channel_id=1, source_target_pairs={{0,1},{1,0},{2,3},{3,2},{4,5},{5,4},{6,7},{7,6},{8,9},{9,8},{10,11... | collective-permute-start | bytes 786440 | tf_op jit(solution)/shard_map/ppermute | solution.py:30
  39.8 8.8 %collective-permute-start.15 = (bf16[64,2048]{1,0:T(8,128)(2,1)S(1)}, bf16[64,2048]{1,0:T(8,128)(2,1)S(1)}, u32[]{:S(2)}, u32[]{:S(2)}) collective-permute-start(bf16[64,2048]{1,0:T(8,128)(2,1)S(1)} %add_convert_fusion.1), channel_id=1, source_target_pairs={{0,18},{1,19},{2,16},{3,17},{4,22},{5,23},{6,20},{7,21},{8,26},{9,... | collective-permute-start | bytes 786440 | tf_op jit(solution)/shard_map/ppermute | solution.py:30
  46.1 1.7 %collective-permute-start.13 = (bf16[64,1024]{1,0:T(8,128)(2,1)S(1)}, bf16[64,1024]{1,0:T(8,128)(2,1)S(1)}, u32[]{:S(2)}, u32[]{:S(2)}) collective-permute-start(bf16[64,1024]{1,0:T(8,128)(2,1)S(1)} %get-tuple-element.16), channel_id=1, source_target_pairs={{0,1},{1,0},{2,3},{3,2},{4,5},{5,4},{6,7},{7,6},{8,9},{9,8},{10,11... | collective-permute-start | bytes 393224 | tf_op jit(solution)/shard_map/ppermute | solution.py:30
  46.9 1.3 %collective-permute-start.14 = (bf16[64,1024]{1,0:T(8,128)(2,1)S(1)}, bf16[64,1024]{1,0:T(8,128)(2,1)S(1)}, u32[]{:S(2)}, u32[]{:S(2)}) collective-permute-start(bf16[64,1024]{1,0:T(8,128)(2,1)S(1)} %get-tuple-element.17), channel_id=1, source_target_pairs={{0,1},{1,0},{2,3},{3,2},{4,5},{5,4},{6,7},{7,6},{8,9},{9,8},{10,11... | collective-permute-start | bytes 393224 | tf_op jit(solution)/shard_map/ppermute | solution.py:30
  48.7 8.2 %collective-permute-start.16 = (bf16[64,2048]{1,0:T(8,128)(2,1)S(1)}, bf16[64,2048]{1,0:T(8,128)(2,1)S(1)}, u32[]{:S(2)}, u32[]{:S(2)}) collective-permute-start(bf16[64,2048]{1,0:T(8,128)(2,1)S(1)} %add_convert_fusion.refs_0_), channel_id=1, source_target_pairs={{0,2},{1,3},{2,0},{3,1},{4,6},{5,7},{6,4},{7,5},{8,10},{9,11},{10,... | collective-permute-start | bytes 786440 | tf_op jit(solution)/shard_map/ppermute | solution.py:30
  50.3 8.7 %collective-permute-start.17 = (bf16[64,2048]{1,0:T(8,128)(2,1)S(1)}, bf16[64,2048]{1,0:T(8,128)(2,1)S(1)}, u32[]{:S(2)}, u32[]{:S(2)}) collective-permute-start(bf16[64,2048]{1,0:T(8,128)(2,1)S(1)} %add_convert_fusion.refs_0_), channel_id=1, source_target_pairs={{0,1},{1,0},{2,3},{3,2},{4,5},{5,4},{6,7},{7,6},{8,9},{9,8},{10,11... | collective-permute-start | bytes 786440 | tf_op jit(solution)/shard_map/ppermute | solution.py:30
  56.9 3.3 %collective-permute-start.18 = (bf16[64,2048]{1,0:T(8,128)(2,1)S(1)}, bf16[64,2048]{1,0:T(8,128)(2,1)S(1)}, u32[]{:S(2)}, u32[]{:S(2)}) collective-permute-start(bf16[64,2048]{1,0:T(8,128)(2,1)S(1)} %collective-permute-done.16.refs_1_), channel_id=1, source_target_pairs={{0,1},{1,0},{2,3},{3,2},{4,5},{5,4},{6,7},{7,6},{8,9},{9,8},{10,11... | collective-permute-start | bytes 786440 | tf_op jit(solution)/shard_map/ppermute | solution.py:30

commit v6 on v5

--- a/solution.py
+++ b/solution.py
@@ -220,7 +220,6 @@
         in_specs=[VMEM] * 8,
         out_specs=VMEM,
         compiler_params=LIMIT,
-        cost_estimate=LONG,
     )(first, other_q, *far_all, mixed, stats)
 
     def projected(own_half, dtype):

time: 61.7 us -> 60.9 us (0.987)
  local copies, waits for them, and re-layouts: 1.96 us -> 1.15 us
    unnamed x6, local copies, waits for them, and re-layouts: 0.82 us -> 0.01 us
where the time goes in v6:
time: 60.9 us; the launch traced here: 60.6 us
  starting transfers between devices  32.8 us (54%)
  waiting for transfers between devices  14.2 us (23%)
  Pallas kernels  10.8 us (18%)
  other arithmetic  1.21 us (2%)
  local copies, waits for them, and re-layouts  1.15 us (2%)
    ppermute x19, starting transfers between devices, shift(): lax.ppermute(array, AXES, [(flat(*d), flat(*move(*d))) for d in devices])  32.8 us
    ppermute x19, waiting for transfers between devices, shift(): lax.ppermute(array, AXES, [(flat(*d), flat(*move(*d))) for d in devices])  14.2 us
    pallas_call x1, Pallas kernels, body(): pl.pallas_call(functools.partial(far_project_kernel, heads, size, block),...  3.73 us
    pallas_call x1, Pallas kernels, body(): pl.pallas_call(functools.partial(near_kernel, heads, size, block), out_sh...  2.99 us
    pallas_call x2, Pallas kernels, projected(): pl.pallas_call(functools.partial(project_kernel, own_half), out_shape=jax...  1.68 us
    pallas_call x1, Pallas kernels, body(): pl.pallas_call(functools.partial(far_kernel, heads, size, block), out_sha...  1.37 us
  transfers between devices with their start and end apart: 19, of which 10 were waited for; matrix products, arithmetic and copies ran while one was open for 2% of the time, Pallas kernels for 12%

profile of v6, /device:TPU:1, one launch (start us, length us, event | category | flops | bytes accessed | tf_op | source)
XLA Modules:
  0.0 60.6 jit_solution(17166484530824699091)
XLA Ops:
  0.0 0.8 %fusion.3 = (bf16[2,64,128]{2,1,0:T(8,128)(2,1)S(1)}, bf16[2,64,128]{2,1,0:T(8,128)(2,1)S(1)}) fusion(s32[]{:T(128)S(6)} %select_n.49, bf16[2,1,64,128]{3,2,0,1:T(8,128)(2,1)} %bitcast.28, bf16[2,1,64,128]{3,2,0,1:T(8,128)(2,1)} %bitcast.29, s32[]{:T(128)S(6)} %select_n.53), kind=kLoop, calls=%fused_computation.16 | loop fusion | flops 32768 | bytes 131080 | tf_op jit(solution)/shard_map/jit(dynamic_index_in_dim)/squeeze | solution.py:185
  0.8 2.1 %collective-permute-start.1 = (bf16[2,64,128]{2,1,0:T(8,128)(2,1)S(1)}, bf16[2,64,128]{2,1,0:T(8,128)(2,1)S(1)}, u32[]{:S(2)}, u32[]{:S(2)}) collective-permute-start(bf16[2,64,128]{2,1,0:T(8,128)(2,1)S(1)} %get-tuple-element.24), channel_id=1, source_target_pairs={{0,16},{1,17},{2,18},{3,19},{4,20},{5,21},{6,22},{7,23},{8,24},{9,... | collective-permute-start | bytes 98312 | tf_op jit(solution)/shard_map/ppermute | solution.py:30
  2.9 1.0 %dynamic-slice_bitcast_fusion = (bf16[64,1024]{1,0:T(8,128)(2,1)S(1)}, bf16[64,1024]{1,0:T(8,128)(2,1)S(1)}) fusion(bf16[2,64,1024]{2,1,0:T(8,128)(2,1)} %param.5, s32[]{:T(128)S(6)} %select_n.49, s32[]{:T(128)S(6)} %select_n.53), kind=kLoop, calls=%fused_computation.4 | loop fusion | bytes 524296 | tf_op jit(solution)/shard_map/jit(dynamic_index_in_dim)/squeeze | solution.py:185
  3.9 0.1 collective-permute-start
  4.1 0.1 convert_reduce_fusion
  4.2 0.0 collective-permute-done.1
  4.3 1.9 %collective-permute-start.7 = (bf16[2,128,128]{2,1,0:T(8,128)(2,1)S(1)}, bf16[2,128,128]{2,1,0:T(8,128)(2,1)S(1)}, u32[]{:S(2)}, u32[]{:S(2)}) collective-permute-start(bf16[2,128,128]{2,1,0:T(8,128)(2,1)S(1)} %get-tuple-element.22), channel_id=1, source_target_pairs={{0,32},{1,33},{2,34},{3,35},{4,36},{5,37},{6,38},{7,39},{8,40},{9,... | collective-permute-start | bytes 196616 | tf_op jit(solution)/shard_map/ppermute | solution.py:30
  6.2 3.0 %collective-permute-start.8 = (bf16[2,128,128]{2,1,0:T(8,128)(2,1)S(1)}, bf16[2,128,128]{2,1,0:T(8,128)(2,1)S(1)}, u32[]{:S(2)}, u32[]{:S(2)}) collective-permute-start(bf16[2,128,128]{2,1,0:T(8,128)(2,1)S(1)} %get-tuple-element.22), channel_id=1, source_target_pairs={{0,64},{1,65},{2,66},{3,67},{4,68},{5,69},{6,70},{7,71},{8,72},{9,... | collective-permute-start | bytes 196616 | tf_op jit(solution)/shard_map/ppermute | solution.py:30
  9.2 4.2 %collective-permute-start.3 = (bf16[2,128,128]{2,1,0:T(8,128)(2,1)S(1)}, bf16[2,128,128]{2,1,0:T(8,128)(2,1)S(1)}, u32[]{:S(2)}, u32[]{:S(2)}) collective-permute-start(bf16[2,128,128]{2,1,0:T(8,128)(2,1)S(1)} %get-tuple-element.22), channel_id=1, source_target_pairs={{0,128},{1,129},{2,130},{3,131},{4,132},{5,133},{6,134},{7,135},{8... | collective-permute-start | bytes 196616 | tf_op jit(solution)/shard_map/ppermute | solution.py:30
  13.4 0.0 collective-permute-start.2
  13.4 0.0 collective-permute-done.7
  13.4 1.0 %collective-permute-done.8 = bf16[2,128,128]{2,1,0:T(8,128)(2,1)S(1)} collective-permute-done((bf16[2,128,128]{2,1,0:T(8,128)(2,1)S(1)}, bf16[2,128,128]{2,1,0:T(8,128)(2,1)S(1)}, u32[]{:S(2)}, u32[]{:S(2)}) %collective-permute-start.8) | collective-permute-done | bytes 65568 | tf_op jit(solution)/shard_map/ppermute | solution.py:30
  14.4 3.0 %collective-permute-start.11 = (bf16[2,3,128,128]{3,2,0,1:T(8,128)(2,1)S(1)}, bf16[2,3,128,128]{3,2,0,1:T(8,128)(2,1)S(1)}, u32[]{:S(2)}, u32[]{:S(2)}) collective-permute-start(bf16[2,3,128,128]{3,2,0,1:T(8,128)(2,1)S(1)} %pad_maximum_fusion), channel_id=1, source_target_pairs={{0,8},{1,9},{2,10},{3,11},{4,12},{5,13},{6,14},{7,15},{8,0},{9,1},... | collective-permute-start | bytes 589832 | tf_op jit(solution)/shard_map/ppermute | solution.py:30
  17.4 0.8 %collective-permute-start.10 = (bf16[2,3,128,128]{3,2,0,1:T(8,128)(2,1)S(1)}, bf16[2,3,128,128]{3,2,0,1:T(8,128)(2,1)S(1)}, u32[]{:S(2)}, u32[]{:S(2)}) collective-permute-start(bf16[2,3,128,128]{3,2,0,1:T(8,128)(2,1)S(1)} %pad_maximum_fusion), channel_id=1, source_target_pairs={{0,12},{1,13},{2,14},{3,15},{4,0},{5,1},{6,2},{7,3},{8,4},{9,5},{1... | collective-permute-start | bytes 589832 | tf_op jit(solution)/shard_map/ppermute | solution.py:30
  18.2 0.0 collective-permute-done.3
  18.2 0.7 %collective-permute-start.9 = (bf16[2,3,128,128]{3,2,0,1:T(8,128)(2,1)S(1)}, bf16[2,3,128,128]{3,2,0,1:T(8,128)(2,1)S(1)}, u32[]{:S(2)}, u32[]{:S(2)}) collective-permute-start(bf16[2,3,128,128]{3,2,0,1:T(8,128)(2,1)S(1)} %pad_maximum_fusion), channel_id=1, source_target_pairs={{0,4},{1,5},{2,6},{3,7},{4,8},{5,9},{6,10},{7,11},{8,12},{9,13},{1... | collective-permute-start | bytes 589832 | tf_op jit(solution)/shard_map/ppermute | solution.py:30
  18.9 0.1 select_reduce_fusion
  19.0 2.7 %collective-permute-done.2 = bf16[2,128,128]{2,1,0:T(8,128)(2,1)S(1)} collective-permute-done((bf16[2,128,128]{2,1,0:T(8,128)(2,1)S(1)}, bf16[2,128,128]{2,1,0:T(8,128)(2,1)S(1)}, u32[]{:S(2)}, u32[]{:S(2)}) %collective-permute-start.2) | collective-permute-done | bytes 65568 | tf_op jit(solution)/shard_map/ppermute | solution.py:30
  21.8 3.0 %collective-permute-start.6 = (bf16[2,2,128,128]{3,2,1,0:T(8,128)(2,1)S(1)}, bf16[2,2,128,128]{3,2,1,0:T(8,128)(2,1)S(1)}, u32[]{:S(2)}, u32[]{:S(2)}) collective-permute-start(bf16[2,2,128,128]{3,2,1,0:T(8,128)(2,1)S(1)} %pad_maximum_fusion.1.k0), channel_id=1, source_target_pairs={{0,8},{1,9},{2,10},{3,11},{4,12},{5,13},{6,14},{7,15},{8,0},{9,1},... | collective-permute-start | bytes 393224 | tf_op jit(solution)/shard_map/ppermute | solution.py:30
  24.8 0.0 collective-permute-done.11
  24.8 0.8 %collective-permute-start.5 = (bf16[2,2,128,128]{3,2,1,0:T(8,128)(2,1)S(1)}, bf16[2,2,128,128]{3,2,1,0:T(8,128)(2,1)S(1)}, u32[]{:S(2)}, u32[]{:S(2)}) collective-permute-start(bf16[2,2,128,128]{3,2,1,0:T(8,128)(2,1)S(1)} %pad_maximum_fusion.1.k0), channel_id=1, source_target_pairs={{0,12},{1,13},{2,14},{3,15},{4,0},{5,1},{6,2},{7,3},{8,4},{9,5},{1... | collective-permute-start | bytes 393224 | tf_op jit(solution)/shard_map/ppermute | solution.py:30
  25.6 0.0 collective-permute-done.10
  25.6 0.9 %collective-permute-start.4 = (bf16[2,2,128,128]{3,2,1,0:T(8,128)(2,1)S(1)}, bf16[2,2,128,128]{3,2,1,0:T(8,128)(2,1)S(1)}, u32[]{:S(2)}, u32[]{:S(2)}) collective-permute-start(bf16[2,2,128,128]{3,2,1,0:T(8,128)(2,1)S(1)} %pad_maximum_fusion.1.k0), channel_id=1, source_target_pairs={{0,4},{1,5},{2,6},{3,7},{4,8},{5,9},{6,10},{7,11},{8,12},{9,13},{1... | collective-permute-start | bytes 393224 | tf_op jit(solution)/shard_map/ppermute | solution.py:30
  26.6 0.0 collective-permute-done.9
  26.6 0.0 collective-permute-done.other_ref.query_ref
  26.6 0.1 broadcast_in_dim.9.first_ref
  26.7 3.0 %shard_map.55 = (f32[2,64,1024]{2,1,0:T(8,128)S(1)}, f32[2,64,128]{2,1,0:T(8,128)S(1)}) custom-call(s32[2,64,128]{2,1,0:T(8,128)S(1)} %broadcast_in_dim.9.first_ref, bf16[64,1024]{1,0:T(8,128)(2,1)S(1)} %get-tuple-element.14.own_ref.query_ref, bf16[64,1024]{1,0:T(8,128)(2,1)S(1)} %collective-permute-done.other_ref.query_ref, ...), custom_call_target="tpu_custom_call" | custom-call | flops 17179869184 | bytes 16777216 | tf_op jit(solution)/shard_map/pallas_call | solution.py:205
  29.7 1.1 %collective-permute-done.5.k2 = bf16[2,2,128,128]{3,2,1,0:T(8,128)(2,1)S(1)} collective-permute-done((bf16[2,2,128,128]{3,2,1,0:T(8,128)(2,1)S(1)}, bf16[2,2,128,128]{3,2,1,0:T(8,128)(2,1)S(1)}, u32[]{:S(2)}, u32[]{:S(2)}) %collective-permute-start.5) | collective-permute-done | bytes 131104 | tf_op jit(solution)/shard_map/ppermute | solution.py:30
  30.8 1.2 %collective-permute-done.4.k1 = bf16[2,2,128,128]{3,2,1,0:T(8,128)(2,1)S(1)} collective-permute-done((bf16[2,2,128,128]{3,2,1,0:T(8,128)(2,1)S(1)}, bf16[2,2,128,128]{3,2,1,0:T(8,128)(2,1)S(1)}, u32[]{:S(2)}, u32[]{:S(2)}) %collective-permute-start.4) | collective-permute-done | bytes 131104 | tf_op jit(solution)/shard_map/ppermute | solution.py:30
  32.0 1.4 %shard_map.56.context_ref = bf16[64,1024]{1,0:T(8,128)(2,1)S(1)} custom-call(s32[2,64,128]{2,1,0:T(8,128)S(1)} %broadcast_in_dim.9.first_ref, bf16[64,1024]{1,0:T(8,128)(2,1)S(1)} %collective-permute-done.other_ref.query_ref, bf16[2,2,128,128]{3,2,1,0:T(8,128)(2,1)S(1)} %pad_maximum_fusion.1.k0, bf16[2,2,128,128]{3,2,1,0:T(8,128)(2,1)S(1)} %collective-permute-done.4.k1, ...), custom_call_target="tpu_custom_call" | custom-call | tf_op jit(solution)/shard_map/pallas_call | solution.py:217
  33.4 0.8 %shard_map.58 = bf16[64,2048]{1,0:T(8,128)(2,1)S(1)} custom-call(bf16[64,1024]{1,0:T(8,128)(2,1)S(1)} %shard_map.56.context_ref, bf16[1024,4096]{1,0:T(8,128)(2,1)S(1)} %bitcast.22), custom_call_target="tpu_custom_call" | custom-call | tf_op jit(solution)/shard_map/pallas_call | solution.py:226
  34.2 3.6 %collective-permute-start.12 = (bf16[64,2048]{1,0:T(8,128)(2,1)S(1)}, bf16[64,2048]{1,0:T(8,128)(2,1)S(1)}, u32[]{:S(2)}, u32[]{:S(2)}) collective-permute-start(bf16[64,2048]{1,0:T(8,128)(2,1)S(1)} %shard_map.58), channel_id=1, source_target_pairs={{0,1},{1,0},{2,3},{3,2},{4,5},{5,4},{6,7},{7,6},{8,9},{9,8},{10,11... | collective-permute-start | bytes 786440 | tf_op jit(solution)/shard_map/ppermute | solution.py:30
  37.8 0.8 %shard_map.57 = f32[64,2048]{1,0:T(8,128)S(1)} custom-call(bf16[64,1024]{1,0:T(8,128)(2,1)S(1)} %shard_map.56.context_ref, bf16[1024,4096]{1,0:T(8,128)(2,1)S(1)} %bitcast.22), custom_call_target="tpu_custom_call" | custom-call | tf_op jit(solution)/shard_map/pallas_call | solution.py:226
  38.7 0.3 collective-permute-done.12
  39.0 2.6 %collective-permute-start.15 = (bf16[64,2048]{1,0:T(8,128)(2,1)S(1)}, bf16[64,2048]{1,0:T(8,128)(2,1)S(1)}, u32[]{:S(2)}, u32[]{:S(2)}) collective-permute-start(bf16[64,2048]{1,0:T(8,128)(2,1)S(1)} %add_convert_fusion.1), channel_id=1, source_target_pairs={{0,18},{1,19},{2,16},{3,17},{4,22},{5,23},{6,20},{7,21},{8,26},{9,... | collective-permute-start | bytes 786440 | tf_op jit(solution)/shard_map/ppermute | solution.py:30
  41.6 3.7 %shard_map.59 = (bf16[64,1024]{1,0:T(8,128)(2,1)S(1)}, bf16[64,1024]{1,0:T(8,128)(2,1)S(1)}, f32[64,2048]{1,0:T(8,128)S(1)}) custom-call(s32[2,64,128]{2,1,0:T(8,128)S(1)} %broadcast_in_dim.9.first_ref, bf16[64,1024]{1,0:T(8,128)(2,1)S(1)} %get-tuple-element.14.own_ref.query_ref, bf16[2,2,128,128]{3,2,1,0:T(8,128)(2,1)S(1)} %pad_maximum_fusion.1.k0, ...), custom_call_target="tpu_custom_call" | custom-call | tf_op jit(solution)/shard_map/pallas_call | solution.py:241
  45.3 0.7 %collective-permute-start.13 = (bf16[64,1024]{1,0:T(8,128)(2,1)S(1)}, bf16[64,1024]{1,0:T(8,128)(2,1)S(1)}, u32[]{:S(2)}, u32[]{:S(2)}) collective-permute-start(bf16[64,1024]{1,0:T(8,128)(2,1)S(1)} %get-tuple-element.16), channel_id=1, source_target_pairs={{0,1},{1,0},{2,3},{3,2},{4,5},{5,4},{6,7},{7,6},{8,9},{9,8},{10,11... | collective-permute-start | bytes 393224 | tf_op jit(solution)/shard_map/ppermute | solution.py:30
  46.1 0.1 collective-permute-start.14
  46.2 0.9 %collective-permute-done.13 = bf16[64,1024]{1,0:T(8,128)(2,1)S(1)} collective-permute-done((bf16[64,1024]{1,0:T(8,128)(2,1)S(1)}, bf16[64,1024]{1,0:T(8,128)(2,1)S(1)}, u32[]{:S(2)}, u32[]{:S(2)}) %collective-permute-start.13) | collective-permute-done | bytes 131104 | tf_op jit(solution)/shard_map/ppermute | solution.py:30
  47.1 0.4 collective-permute-done.14
  47.4 0.4 collective-permute-done.15
  47.8 0.1 add_convert_fusion.refs_0_
  47.9 1.6 %collective-permute-start.16 = (bf16[64,2048]{1,0:T(8,128)(2,1)S(1)}, bf16[64,2048]{1,0:T(8,128)(2,1)S(1)}, u32[]{:S(2)}, u32[]{:S(2)}) collective-permute-start(bf16[64,2048]{1,0:T(8,128)(2,1)S(1)} %add_convert_fusion.refs_0_), channel_id=1, source_target_pairs={{0,2},{1,3},{2,0},{3,1},{4,6},{5,7},{6,4},{7,5},{8,10},{9,11},{10,... | collective-permute-start | bytes 786440 | tf_op jit(solution)/shard_map/ppermute | solution.py:30
  49.5 1.5 %collective-permute-start.17 = (bf16[64,2048]{1,0:T(8,128)(2,1)S(1)}, bf16[64,2048]{1,0:T(8,128)(2,1)S(1)}, u32[]{:S(2)}, u32[]{:S(2)}) collective-permute-start(bf16[64,2048]{1,0:T(8,128)(2,1)S(1)} %add_convert_fusion.refs_0_), channel_id=1, source_target_pairs={{0,1},{1,0},{2,3},{3,2},{4,5},{5,4},{6,7},{7,6},{8,9},{9,8},{10,11... | collective-permute-start | bytes 786440 | tf_op jit(solution)/shard_map/ppermute | solution.py:30
  51.0 5.1 %collective-permute-done.16.refs_1_ = bf16[64,2048]{1,0:T(8,128)(2,1)S(1)} collective-permute-done((bf16[64,2048]{1,0:T(8,128)(2,1)S(1)}, bf16[64,2048]{1,0:T(8,128)(2,1)S(1)}, u32[]{:S(2)}, u32[]{:S(2)}) %collective-permute-start.16) | collective-permute-done | bytes 262176 | tf_op jit(solution)/shard_map/ppermute | solution.py:30
  56.1 2.1 %collective-permute-start.18 = (bf16[64,2048]{1,0:T(8,128)(2,1)S(1)}, bf16[64,2048]{1,0:T(8,128)(2,1)S(1)}, u32[]{:S(2)}, u32[]{:S(2)}) collective-permute-start(bf16[64,2048]{1,0:T(8,128)(2,1)S(1)} %collective-permute-done.16.refs_1_), channel_id=1, source_target_pairs={{0,1},{1,0},{2,3},{3,2},{4,5},{5,4},{6,7},{7,6},{8,9},{9,8},{10,11... | collective-permute-start | bytes 786440 | tf_op jit(solution)/shard_map/ppermute | solution.py:30
  58.2 1.2 %collective-permute-done.18.refs_3_ = bf16[64,2048]{1,0:T(8,128)(2,1)S(1)} collective-permute-done((bf16[64,2048]{1,0:T(8,128)(2,1)S(1)}, bf16[64,2048]{1,0:T(8,128)(2,1)S(1)}, u32[]{:S(2)}, u32[]{:S(2)}) %collective-permute-start.18) | collective-permute-done | bytes 262176 | tf_op jit(solution)/shard_map/ppermute | solution.py:30
  59.4 1.0 %shard_map.60 = bf16[2,64,4096]{2,1,0:T(8,128)(2,1)} custom-call(bf16[64,2048]{1,0:T(8,128)(2,1)S(1)} %add_convert_fusion.refs_0_, bf16[64,2048]{1,0:T(8,128)(2,1)S(1)} %collective-permute-done.16.refs_1_, bf16[64,2048]{1,0:T(8,128)(2,1)S(1)} %collective-permute-done.17.refs_2_, bf16[64,2048]{1,0:T(8,128)(2,1)S(1)} %collective-permute-done.18.refs_3_), custom_call_target="tpu_custom_call" | custom-call | tf_op jit(solution)/shard_map/pallas_call | solution.py:260
  (20 shorter events, 0.2 us)
Async XLA Ops:
  0.0 4.0 %copy-start = (s32[2,4096]{1,0:T(2,128)S(1)}, s32[2,4096]{1,0:T(2,128)}, u32[]{:S(2)}) copy-start(s32[2,4096]{1,0:T(2,128)} %param.8) | copy-start | bytes 98308
  0.8 3.4 %collective-permute-start.1 = (bf16[2,64,128]{2,1,0:T(8,128)(2,1)S(1)}, bf16[2,64,128]{2,1,0:T(8,128)(2,1)S(1)}, u32[]{:S(2)}, u32[]{:S(2)}) collective-permute-start(bf16[2,64,128]{2,1,0:T(8,128)(2,1)S(1)} %get-tuple-element.24), channel_id=1, source_target_pairs={{0,16},{1,17},{2,18},{3,19},{4,20},{5,21},{6,22},{7,23},{8,24},{9,... | collective-permute-start | bytes 98312 | tf_op jit(solution)/shard_map/ppermute | solution.py:30
  3.9 22.7 %collective-permute-start = (bf16[64,1024]{1,0:T(8,128)(2,1)S(1)}, bf16[64,1024]{1,0:T(8,128)(2,1)S(1)}, u32[]{:S(2)}, u32[]{:S(2)}) collective-permute-start(bf16[64,1024]{1,0:T(8,128)(2,1)S(1)} %get-tuple-element.20), channel_id=1, source_target_pairs={{0,16},{1,17},{2,18},{3,19},{4,20},{5,21},{6,22},{7,23},{8,24},{9,... | collective-permute-start | bytes 393224 | tf_op jit(solution)/shard_map/ppermute | solution.py:30
  4.3 9.2 %collective-permute-start.7 = (bf16[2,128,128]{2,1,0:T(8,128)(2,1)S(1)}, bf16[2,128,128]{2,1,0:T(8,128)(2,1)S(1)}, u32[]{:S(2)}, u32[]{:S(2)}) collective-permute-start(bf16[2,128,128]{2,1,0:T(8,128)(2,1)S(1)} %get-tuple-element.22), channel_id=1, source_target_pairs={{0,32},{1,33},{2,34},{3,35},{4,36},{5,37},{6,38},{7,39},{8,40},{9,... | collective-permute-start | bytes 196616 | tf_op jit(solution)/shard_map/ppermute | solution.py:30
  6.2 8.2 %collective-permute-start.8 = (bf16[2,128,128]{2,1,0:T(8,128)(2,1)S(1)}, bf16[2,128,128]{2,1,0:T(8,128)(2,1)S(1)}, u32[]{:S(2)}, u32[]{:S(2)}) collective-permute-start(bf16[2,128,128]{2,1,0:T(8,128)(2,1)S(1)} %get-tuple-element.22), channel_id=1, source_target_pairs={{0,64},{1,65},{2,66},{3,67},{4,68},{5,69},{6,70},{7,71},{8,72},{9,... | collective-permute-start | bytes 196616 | tf_op jit(solution)/shard_map/ppermute | solution.py:30
  9.2 9.0 %collective-permute-start.3 = (bf16[2,128,128]{2,1,0:T(8,128)(2,1)S(1)}, bf16[2,128,128]{2,1,0:T(8,128)(2,1)S(1)}, u32[]{:S(2)}, u32[]{:S(2)}) collective-permute-start(bf16[2,128,128]{2,1,0:T(8,128)(2,1)S(1)} %get-tuple-element.22), channel_id=1, source_target_pairs={{0,128},{1,129},{2,130},{3,131},{4,132},{5,133},{6,134},{7,135},{8... | collective-permute-start | bytes 196616 | tf_op jit(solution)/shard_map/ppermute | solution.py:30
  13.4 8.4 %collective-permute-start.2 = (bf16[2,128,128]{2,1,0:T(8,128)(2,1)S(1)}, bf16[2,128,128]{2,1,0:T(8,128)(2,1)S(1)}, u32[]{:S(2)}, u32[]{:S(2)}) collective-permute-start(bf16[2,128,128]{2,1,0:T(8,128)(2,1)S(1)} %get-tuple-element.22), channel_id=1, source_target_pairs={{0,96},{1,97},{2,98},{3,99},{4,100},{5,101},{6,102},{7,103},{8,104... | collective-permute-start | bytes 196616 | tf_op jit(solution)/shard_map/ppermute | solution.py:30
  14.4 10.4 %collective-permute-start.11 = (bf16[2,3,128,128]{3,2,0,1:T(8,128)(2,1)S(1)}, bf16[2,3,128,128]{3,2,0,1:T(8,128)(2,1)S(1)}, u32[]{:S(2)}, u32[]{:S(2)}) collective-permute-start(bf16[2,3,128,128]{3,2,0,1:T(8,128)(2,1)S(1)} %pad_maximum_fusion), channel_id=1, source_target_pairs={{0,8},{1,9},{2,10},{3,11},{4,12},{5,13},{6,14},{7,15},{8,0},{9,1},... | collective-permute-start | bytes 589832 | tf_op jit(solution)/shard_map/ppermute | solution.py:30
  17.4 8.2 %collective-permute-start.10 = (bf16[2,3,128,128]{3,2,0,1:T(8,128)(2,1)S(1)}, bf16[2,3,128,128]{3,2,0,1:T(8,128)(2,1)S(1)}, u32[]{:S(2)}, u32[]{:S(2)}) collective-permute-start(bf16[2,3,128,128]{3,2,0,1:T(8,128)(2,1)S(1)} %pad_maximum_fusion), channel_id=1, source_target_pairs={{0,12},{1,13},{2,14},{3,15},{4,0},{5,1},{6,2},{7,3},{8,4},{9,5},{1... | collective-permute-start | bytes 589832 | tf_op jit(solution)/shard_map/ppermute | solution.py:30
  18.2 8.4 %collective-permute-start.9 = (bf16[2,3,128,128]{3,2,0,1:T(8,128)(2,1)S(1)}, bf16[2,3,128,128]{3,2,0,1:T(8,128)(2,1)S(1)}, u32[]{:S(2)}, u32[]{:S(2)}) collective-permute-start(bf16[2,3,128,128]{3,2,0,1:T(8,128)(2,1)S(1)} %pad_maximum_fusion), channel_id=1, source_target_pairs={{0,4},{1,5},{2,6},{3,7},{4,8},{5,9},{6,10},{7,11},{8,12},{9,13},{1... | collective-permute-start | bytes 589832 | tf_op jit(solution)/shard_map/ppermute | solution.py:30
  21.8 7.9 %collective-permute-start.6 = (bf16[2,2,128,128]{3,2,1,0:T(8,128)(2,1)S(1)}, bf16[2,2,128,128]{3,2,1,0:T(8,128)(2,1)S(1)}, u32[]{:S(2)}, u32[]{:S(2)}) collective-permute-start(bf16[2,2,128,128]{3,2,1,0:T(8,128)(2,1)S(1)} %pad_maximum_fusion.1.k0), channel_id=1, source_target_pairs={{0,8},{1,9},{2,10},{3,11},{4,12},{5,13},{6,14},{7,15},{8,0},{9,1},... | collective-permute-start | bytes 393224 | tf_op jit(solution)/shard_map/ppermute | solution.py:30
  24.8 6.0 %collective-permute-start.5 = (bf16[2,2,128,128]{3,2,1,0:T(8,128)(2,1)S(1)}, bf16[2,2,128,128]{3,2,1,0:T(8,128)(2,1)S(1)}, u32[]{:S(2)}, u32[]{:S(2)}) collective-permute-start(bf16[2,2,128,128]{3,2,1,0:T(8,128)(2,1)S(1)} %pad_maximum_fusion.1.k0), channel_id=1, source_target_pairs={{0,12},{1,13},{2,14},{3,15},{4,0},{5,1},{6,2},{7,3},{8,4},{9,5},{1... | collective-permute-start | bytes 393224 | tf_op jit(solution)/shard_map/ppermute | solution.py:30
  25.6 6.4 %collective-permute-start.4 = (bf16[2,2,128,128]{3,2,1,0:T(8,128)(2,1)S(1)}, bf16[2,2,128,128]{3,2,1,0:T(8,128)(2,1)S(1)}, u32[]{:S(2)}, u32[]{:S(2)}) collective-permute-start(bf16[2,2,128,128]{3,2,1,0:T(8,128)(2,1)S(1)} %pad_maximum_fusion.1.k0), channel_id=1, source_target_pairs={{0,4},{1,5},{2,6},{3,7},{4,8},{5,9},{6,10},{7,11},{8,12},{9,13},{1... | collective-permute-start | bytes 393224 | tf_op jit(solution)/shard_map/ppermute | solution.py:30
  26.6 6.8 %slice-start = ((s8[8388608]{0:T(1024)(128)(4,1)}), s8[4194304]{0:T(1024)(128)(4,1)S(1)}, s32[]{:S(2)}) async-start(s8[8388608]{0:T(1024)(128)(4,1)} %bitcast.21), calls=%async_computation | async-start | bytes 8388608
  26.7 6.7 %slice-start.1 = ((s8[8388608]{0:T(1024)(128)(4,1)}), s8[4194304]{0:T(1024)(128)(4,1)S(1)}, s32[]{:S(2)}) async-start(s8[8388608]{0:T(1024)(128)(4,1)} %bitcast.21), calls=%async_computation.1 | async-start | bytes 8388608
  34.2 4.8 %collective-permute-start.12 = (bf16[64,2048]{1,0:T(8,128)(2,1)S(1)}, bf16[64,2048]{1,0:T(8,128)(2,1)S(1)}, u32[]{:S(2)}, u32[]{:S(2)}) collective-permute-start(bf16[64,2048]{1,0:T(8,128)(2,1)S(1)} %shard_map.58), channel_id=1, source_target_pairs={{0,1},{1,0},{2,3},{3,2},{4,5},{5,4},{6,7},{7,6},{8,9},{9,8},{10,11... | collective-permute-start | bytes 786440 | tf_op jit(solution)/shard_map/ppermute | solution.py:30
  39.0 8.8 %collective-permute-start.15 = (bf16[64,2048]{1,0:T(8,128)(2,1)S(1)}, bf16[64,2048]{1,0:T(8,128)(2,1)S(1)}, u32[]{:S(2)}, u32[]{:S(2)}) collective-permute-start(bf16[64,2048]{1,0:T(8,128)(2,1)S(1)} %add_convert_fusion.1), channel_id=1, source_target_pairs={{0,18},{1,19},{2,16},{3,17},{4,22},{5,23},{6,20},{7,21},{8,26},{9,... | collective-permute-start | bytes 786440 | tf_op jit(solution)/shard_map/ppermute | solution.py:30
  45.3 1.7 %collective-permute-start.13 = (bf16[64,1024]{1,0:T(8,128)(2,1)S(1)}, bf16[64,1024]{1,0:T(8,128)(2,1)S(1)}, u32[]{:S(2)}, u32[]{:S(2)}) collective-permute-start(bf16[64,1024]{1,0:T(8,128)(2,1)S(1)} %get-tuple-element.16), channel_id=1, source_target_pairs={{0,1},{1,0},{2,3},{3,2},{4,5},{5,4},{6,7},{7,6},{8,9},{9,8},{10,11... | collective-permute-start | bytes 393224 | tf_op jit(solution)/shard_map/ppermute | solution.py:30
  46.1 1.3 %collective-permute-start.14 = (bf16[64,1024]{1,0:T(8,128)(2,1)S(1)}, bf16[64,1024]{1,0:T(8,128)(2,1)S(1)}, u32[]{:S(2)}, u32[]{:S(2)}) collective-permute-start(bf16[64,1024]{1,0:T(8,128)(2,1)S(1)} %get-tuple-element.17), channel_id=1, source_target_pairs={{0,1},{1,0},{2,3},{3,2},{4,5},{5,4},{6,7},{7,6},{8,9},{9,8},{10,11... | collective-permute-start | bytes 393224 | tf_op jit(solution)/shard_map/ppermute | solution.py:30
  47.9 8.2 %collective-permute-start.16 = (bf16[64,2048]{1,0:T(8,128)(2,1)S(1)}, bf16[64,2048]{1,0:T(8,128)(2,1)S(1)}, u32[]{:S(2)}, u32[]{:S(2)}) collective-permute-start(bf16[64,2048]{1,0:T(8,128)(2,1)S(1)} %add_convert_fusion.refs_0_), channel_id=1, source_target_pairs={{0,2},{1,3},{2,0},{3,1},{4,6},{5,7},{6,4},{7,5},{8,10},{9,11},{10,... | collective-permute-start | bytes 786440 | tf_op jit(solution)/shard_map/ppermute | solution.py:30
  49.5 8.7 %collective-permute-start.17 = (bf16[64,2048]{1,0:T(8,128)(2,1)S(1)}, bf16[64,2048]{1,0:T(8,128)(2,1)S(1)}, u32[]{:S(2)}, u32[]{:S(2)}) collective-permute-start(bf16[64,2048]{1,0:T(8,128)(2,1)S(1)} %add_convert_fusion.refs_0_), channel_id=1, source_target_pairs={{0,1},{1,0},{2,3},{3,2},{4,5},{5,4},{6,7},{7,6},{8,9},{9,8},{10,11... | collective-permute-start | bytes 786440 | tf_op jit(solution)/shard_map/ppermute | solution.py:30
  56.1 3.3 %collective-permute-start.18 = (bf16[64,2048]{1,0:T(8,128)(2,1)S(1)}, bf16[64,2048]{1,0:T(8,128)(2,1)S(1)}, u32[]{:S(2)}, u32[]{:S(2)}) collective-permute-start(bf16[64,2048]{1,0:T(8,128)(2,1)S(1)} %collective-permute-done.16.refs_1_), channel_id=1, source_target_pairs={{0,1},{1,0},{2,3},{3,2},{4,5},{5,4},{6,7},{7,6},{8,9},{9,8},{10,11... | collective-permute-start | bytes 786440 | tf_op jit(solution)/shard_map/ppermute | solution.py:30

commit v7 on v6

--- a/solution.py
+++ b/solution.py
@@ -11,7 +11,6 @@
 NZ, NX, NY, NH, NC = 8, 2, 4, 2, 2
 AXES = ("seq", "tp")
 MASKED = -1e30
-NEAR, FAR = (0, 1, 2), (3, 4)
 COLUMNS_BACK = (0, 1, 3, 2)
 GROUP = 4
 PIECES = 1
@@ -65,18 +64,24 @@
     return base + lax.broadcasted_iota(jnp.int32, (block, 1), 0)
 
 
-def bias_of(first_ref, which, layers, block):
-    z, x, y, _, _ = coordinates()
+def bias_of(first_ref, which, far, block):
+    z, _, y, _, _ = coordinates()
     first, last = first_ref[which, :, :1], row_positions(which, block)
-    lane = lax.broadcasted_iota(jnp.int32, (1, 2 * block), 1)
-    own, other = x * (NY * block), (1 - x) * (NY * block)
-    within = jnp.where(lane < block, own + lane, other + lane - block)
     parts = []
     for back in COLUMNS_BACK:
-        column = lax.rem(y + NY - back, NY) * block
+        column = lax.rem(y + NY - back, NY)
+        start = lambda layer, x: ((z - layer) * NX + x) * (NY * block) + column * block
+        if far:
+            shared = start(4, 0) if back == 0 else jnp.where(y >= back, start(0, 1), start(4, 0))
+            starts = [shared, start(4, 1), start(3, 0), start(3, 1)]
+        else:
+            starts = [start(0, 0)] + ([start(0, 1)] if back == 0 else [])
+            starts += [start(layer, x) for layer in (1, 2) for x in (0, 1)]
         tiles = []
-        for layer_back in layers:
-            at = within + ((z - layer_back) * (NX * NY * block) + column)
+        for i in range(0, len(starts), 2):
+            pair = starts[i:i + 2]
+            lane = lax.broadcasted_iota(jnp.int32, (1, len(pair) * block), 1)
+            at = pair[0] + lane if len(pair) == 1 else jnp.where(lane < block, pair[0] + lane, pair[1] + lane - block)
             tiles.append(jnp.where((at >= first) & (at <= last), 0.0, MASKED))
         parts.append(jnp.concatenate(tiles, axis=1))
     return parts
@@ -105,7 +110,7 @@
     scale = math.log2(math.e) / math.sqrt(size)
     lane = lax.broadcasted_iota(jnp.int32, (block, 128), 1)
     for which, query_ref in enumerate((own_ref, other_ref)):
-        bias = bias_of(first_ref, which, NEAR, block)
+        bias = bias_of(first_ref, which, False, block)
         stats = jnp.zeros((block, 128), jnp.float32)
         for start in range(0, heads, GROUP):
             group = range(start, start + GROUP)
@@ -121,7 +126,7 @@
 
 def far_block(heads, size, block, which, first_ref, query_ref, kv_refs, mixed_ref, stat_ref, context_ref):
     scale = math.log2(math.e) / math.sqrt(size)
-    bias = bias_of(first_ref, which, FAR, block)
+    bias = bias_of(first_ref, which, True, block)
     stats = stat_ref[which]
     for start in range(0, heads, GROUP):
         group = range(start, start + GROUP)
@@ -137,6 +142,17 @@
 
 def far_kernel(heads, size, block, first_ref, query_ref, k0, k1, k2, k3, mixed_ref, stat_ref, context_ref):
     far_block(heads, size, block, 1, first_ref, query_ref, (k0, k1, k2, k3), mixed_ref, stat_ref, context_ref)
+
+
+def pack_kernel(block, unit_ref, third_ref, fourth_ref, *out_refs):
+    y = coordinates()[2]
+    for by, out_ref in zip(COLUMNS_BACK, out_refs):
+        shared = fourth_ref[:, :block]
+        if by:
+            shared = jnp.where(y + by < NY, unit_ref[:, block:], shared)
+        out_ref[:, :block] = shared
+        out_ref[:, block:2 * block] = fourth_ref[:, block:]
+        out_ref[:, 2 * block:] = third_ref[...]
 
 
 def project(own_half, context_ref, weight_ref, out_ref, pieces=1, piece=0):
@@ -185,14 +201,21 @@
     pick = lambda a, i: lax.dynamic_index_in_dim(a, i, 0, keepdims=False)
 
     pair = jnp.stack([key_projected, values], axis=1)
-    unit = jnp.concatenate([pick(pair, batch), swap_x(pick(pair, 1 - batch))], axis=1)
-    back = {0: unit}
-    for by in (1, 2, 3, 4):
-        back[by] = shift_z(unit, by)
-    near = jnp.stack([back[layer] for layer in NEAR], axis=1)
-    far = jnp.stack([back[layer] for layer in FAR], axis=1)
-    near_all = [near] + [shift_y(near, by) for by in COLUMNS_BACK[1:]]
-    far_all = [far] + [shift_y(far, by) for by in COLUMNS_BACK[1:]]
+    mine, theirs = lax.optimization_barrier((pick(pair, batch), pick(pair, 1 - batch)))
+    theirs = swap_x(theirs)
+    unit = jnp.concatenate([jnp.where(x == 0, mine, theirs), jnp.where(x == 0, theirs, mine)], axis=1)
+    back = [unit] + [shift_z(unit, by) for by in (1, 2, 3, 4)]
+    near = jnp.concatenate(back[:3], axis=1)
+    near_sent = jnp.concatenate([back[0][:, :block], back[1], back[2]], axis=1)
+    near_all = [near] + [shift_y(near_sent, by) for by in COLUMNS_BACK[1:]]
+    packed = pl.pallas_call(
+        functools.partial(pack_kernel, block),
+        out_shape=[jax.ShapeDtypeStruct((2, 4 * block, size), jnp.bfloat16)] * NY,
+        in_specs=[VMEM] * 3,
+        out_specs=[VMEM] * NY,
+        compiler_params=LIMIT,
+    )(back[0], back[3], back[4])
+    far_all = [packed[0]] + [shift_y(array, by) for array, by in zip(packed[1:], COLUMNS_BACK[1:])]
     own_q = pick(queries, batch)
     other_q = swap_x(pick(queries, 1 - batch))
 

time: 60.9 us -> 60 us (0.985)
  waiting for transfers between devices: 14.2 us -> 13.2 us
    ppermute x19, waiting for transfers between devices: 14.2 us -> 13.2 us  [shift(): lax.ppermute(array, AXES, [(flat(*d), flat(*move(*d))) for d in devices])]
  transfers between devices with their start and end apart: 19 -> 19, of which waited for: 10 -> 9; matrix products, arithmetic and copies ran while one was open for 2% -> 2% of each run, Pallas kernels for 12% -> 13%
where the time goes in v7:
time: 60 us; the launch traced here: 59.8 us
  starting transfers between devices  33.2 us (55%)
  waiting for transfers between devices  13.2 us (22%)
  Pallas kernels  10.8 us (18%)
  other arithmetic  1.2 us (2%)
  local copies, waits for them, and re-layouts  1.09 us (2%)
    ppermute x19, starting transfers between devices, shift(): lax.ppermute(array, AXES, [(flat(*d), flat(*move(*d))) for d in devices])  33.2 us
    ppermute x19, waiting for transfers between devices, shift(): lax.ppermute(array, AXES, [(flat(*d), flat(*move(*d))) for d in devices])  13.2 us
    pallas_call x1, Pallas kernels, body(): pl.pallas_call(functools.partial(far_project_kernel, heads, size, block),...  3.75 us
    pallas_call x1, Pallas kernels, body(): pl.pallas_call(functools.partial(near_kernel, heads, size, block), out_sh...  2.96 us
    pallas_call x2, Pallas kernels, projected(): pl.pallas_call(functools.partial(project_kernel, own_half), out_shape=jax...  1.68 us
    pallas_call x1, Pallas kernels, body(): pl.pallas_call(functools.partial(far_kernel, heads, size, block), out_sha...  1.36 us
  transfers between devices with their start and end apart: 19, of which 9 were waited for; matrix products, arithmetic and copies ran while one was open for 2% of the time, Pallas kernels for 13%

profile of v7, /device:TPU:1, one launch (start us, length us, event | category | flops | bytes accessed | tf_op | source)
XLA Modules:
  0.0 59.8 jit_solution(5572338259559058579)
XLA Ops:
  0.0 0.8 %fusion.1 = (bf16[2,64,128]{2,1,0:T(8,128)(2,1)S(1)}, bf16[2,64,128]{2,1,0:T(8,128)(2,1)S(1)}) fusion(s32[]{:T(128)S(6)} %select_n.65, bf16[2,1,64,128]{3,2,0,1:T(8,128)(2,1)} %bitcast.16, bf16[2,1,64,128]{3,2,0,1:T(8,128)(2,1)} %bitcast.17, s32[]{:T(128)S(6)} %select_n.61), kind=kLoop, calls=%fused_computation.14 | loop fusion | flops 32768 | bytes 131080 | tf_op jit(solution)/shard_map/jit(dynamic_index_in_dim)/squeeze | solution.py:201
  0.8 2.1 %collective-permute-start.1 = (bf16[2,64,128]{2,1,0:T(8,128)(2,1)S(1)}, bf16[2,64,128]{2,1,0:T(8,128)(2,1)S(1)}, u32[]{:S(2)}, u32[]{:S(2)}) collective-permute-start(bf16[2,64,128]{2,1,0:T(8,128)(2,1)S(1)} %get-tuple-element.19), channel_id=1, source_target_pairs={{0,16},{1,17},{2,18},{3,19},{4,20},{5,21},{6,22},{7,23},{8,24},{9,... | collective-permute-start | bytes 98312 | tf_op jit(solution)/shard_map/ppermute | solution.py:29
  2.9 1.0 %dynamic-slice_bitcast_fusion = (bf16[64,1024]{1,0:T(8,128)(2,1)S(1)}, bf16[64,1024]{1,0:T(8,128)(2,1)S(1)}) fusion(bf16[2,64,1024]{2,1,0:T(8,128)(2,1)} %param.5, s32[]{:T(128)S(6)} %select_n.61, s32[]{:T(128)S(6)} %select_n.65), kind=kLoop, calls=%fused_computation.4 | loop fusion | bytes 524296 | tf_op jit(solution)/shard_map/jit(dynamic_index_in_dim)/squeeze | solution.py:201
  3.9 0.1 collective-permute-start
  4.1 0.1 convert_reduce_fusion
  4.2 0.0 collective-permute-done.1
  4.3 3.3 %collective-permute-start.8 = (bf16[2,128,128]{2,1,0:T(8,128)(2,1)S(1)}, bf16[2,128,128]{2,1,0:T(8,128)(2,1)S(1)}, u32[]{:S(2)}, u32[]{:S(2)}) collective-permute-start(bf16[2,128,128]{2,1,0:T(8,128)(2,1)S(1)} %pad_maximum_fusion.2.unit_ref), channel_id=1, source_target_pairs={{0,64},{1,65},{2,66},{3,67},{4,68},{5,69},{6,70},{7,71},{8,72},{9,... | collective-permute-start | bytes 196616 | tf_op jit(solution)/shard_map/ppermute | solution.py:29
  7.6 1.6 %collective-permute-start.7 = (bf16[2,128,128]{2,1,0:T(8,128)(2,1)S(1)}, bf16[2,128,128]{2,1,0:T(8,128)(2,1)S(1)}, u32[]{:S(2)}, u32[]{:S(2)}) collective-permute-start(bf16[2,128,128]{2,1,0:T(8,128)(2,1)S(1)} %pad_maximum_fusion.2.unit_ref), channel_id=1, source_target_pairs={{0,32},{1,33},{2,34},{3,35},{4,36},{5,37},{6,38},{7,39},{8,40},{9,... | collective-permute-start | bytes 196616 | tf_op jit(solution)/shard_map/ppermute | solution.py:29
  9.2 4.2 %collective-permute-start.3 = (bf16[2,128,128]{2,1,0:T(8,128)(2,1)S(1)}, bf16[2,128,128]{2,1,0:T(8,128)(2,1)S(1)}, u32[]{:S(2)}, u32[]{:S(2)}) collective-permute-start(bf16[2,128,128]{2,1,0:T(8,128)(2,1)S(1)} %pad_maximum_fusion.2.unit_ref), channel_id=1, source_target_pairs={{0,128},{1,129},{2,130},{3,131},{4,132},{5,133},{6,134},{7,135},{8... | collective-permute-start | bytes 196616 | tf_op jit(solution)/shard_map/ppermute | solution.py:29
  13.4 0.0 collective-permute-start.2
  13.4 0.0 collective-permute-done.8
  13.4 0.0 collective-permute-done.7
  13.4 0.0 slice-start
  13.5 3.0 %collective-permute-start.11 = (bf16[2,320,128]{2,1,0:T(8,128)(2,1)S(1)}, bf16[2,320,128]{2,1,0:T(8,128)(2,1)S(1)}, u32[]{:S(2)}, u32[]{:S(2)}) collective-permute-start(bf16[2,320,128]{2,1,0:T(8,128)(2,1)S(1)} %pad_maximum_fusion.1), channel_id=1, source_target_pairs={{0,8},{1,9},{2,10},{3,11},{4,12},{5,13},{6,14},{7,15},{8,0},{9,1},... | collective-permute-start | bytes 491528 | tf_op jit(solution)/shard_map/ppermute | solution.py:29
  16.5 0.8 %collective-permute-start.10 = (bf16[2,320,128]{2,1,0:T(8,128)(2,1)S(1)}, bf16[2,320,128]{2,1,0:T(8,128)(2,1)S(1)}, u32[]{:S(2)}, u32[]{:S(2)}) collective-permute-start(bf16[2,320,128]{2,1,0:T(8,128)(2,1)S(1)} %pad_maximum_fusion.1), channel_id=1, source_target_pairs={{0,12},{1,13},{2,14},{3,15},{4,0},{5,1},{6,2},{7,3},{8,4},{9,5},{1... | collective-permute-start | bytes 491528 | tf_op jit(solution)/shard_map/ppermute | solution.py:29
  17.2 0.1 collective-permute-done.3.fourth_ref
  17.3 1.3 %collective-permute-start.9 = (bf16[2,320,128]{2,1,0:T(8,128)(2,1)S(1)}, bf16[2,320,128]{2,1,0:T(8,128)(2,1)S(1)}, u32[]{:S(2)}, u32[]{:S(2)}) collective-permute-start(bf16[2,320,128]{2,1,0:T(8,128)(2,1)S(1)} %pad_maximum_fusion.1), channel_id=1, source_target_pairs={{0,4},{1,5},{2,6},{3,7},{4,8},{5,9},{6,10},{7,11},{8,12},{9,13},{1... | collective-permute-start | bytes 491528 | tf_op jit(solution)/shard_map/ppermute | solution.py:29
  18.6 0.1 select_reduce_fusion
  18.7 2.4 %collective-permute-done.2.third_ref = bf16[2,128,128]{2,1,0:T(8,128)(2,1)S(1)} collective-permute-done((bf16[2,128,128]{2,1,0:T(8,128)(2,1)S(1)}, bf16[2,128,128]{2,1,0:T(8,128)(2,1)S(1)}, u32[]{:S(2)}, u32[]{:S(2)}) %collective-permute-start.2) | collective-permute-done | bytes 65568 | tf_op jit(solution)/shard_map/ppermute | solution.py:29
  21.2 0.1 shard_map.55
  21.2 1.4 %collective-permute-start.4 = (bf16[2,256,128]{2,1,0:T(8,128)(2,1)S(1)}, bf16[2,256,128]{2,1,0:T(8,128)(2,1)S(1)}, u32[]{:S(2)}, u32[]{:S(2)}) collective-permute-start(bf16[2,256,128]{2,1,0:T(8,128)(2,1)S(1)} %get-tuple-element.21), channel_id=1, source_target_pairs={{0,4},{1,5},{2,6},{3,7},{4,8},{5,9},{6,10},{7,11},{8,12},{9,13},{1... | collective-permute-start | bytes 393224 | tf_op jit(solution)/shard_map/ppermute | solution.py:29
  22.6 1.5 %collective-permute-start.5 = (bf16[2,256,128]{2,1,0:T(8,128)(2,1)S(1)}, bf16[2,256,128]{2,1,0:T(8,128)(2,1)S(1)}, u32[]{:S(2)}, u32[]{:S(2)}) collective-permute-start(bf16[2,256,128]{2,1,0:T(8,128)(2,1)S(1)} %get-tuple-element.22), channel_id=1, source_target_pairs={{0,12},{1,13},{2,14},{3,15},{4,0},{5,1},{6,2},{7,3},{8,4},{9,5},{1... | collective-permute-start | bytes 393224 | tf_op jit(solution)/shard_map/ppermute | solution.py:29
  24.2 0.0 collective-permute-done.11.k3
  24.2 1.6 %collective-permute-start.6 = (bf16[2,256,128]{2,1,0:T(8,128)(2,1)S(1)}, bf16[2,256,128]{2,1,0:T(8,128)(2,1)S(1)}, u32[]{:S(2)}, u32[]{:S(2)}) collective-permute-start(bf16[2,256,128]{2,1,0:T(8,128)(2,1)S(1)} %get-tuple-element.23), channel_id=1, source_target_pairs={{0,8},{1,9},{2,10},{3,11},{4,12},{5,13},{6,14},{7,15},{8,0},{9,1},... | collective-permute-start | bytes 393224 | tf_op jit(solution)/shard_map/ppermute | solution.py:29
  25.8 0.1 broadcast_in_dim.9.first_ref
  25.9 0.0 slice-start.1
  25.9 3.0 %shard_map.56 = (f32[2,64,1024]{2,1,0:T(8,128)S(1)}, f32[2,64,128]{2,1,0:T(8,128)S(1)}) custom-call(s32[2,64,128]{2,1,0:T(8,128)S(1)} %broadcast_in_dim.9.first_ref, bf16[64,1024]{1,0:T(8,128)(2,1)S(1)} %get-tuple-element.26.own_ref.query_ref, bf16[64,1024]{1,0:T(8,128)(2,1)S(1)} %collective-permute-done.other_ref.query_ref, ...), custom_call_target="tpu_custom_call" | custom-call | flops 17179869184 | bytes 16777216 | tf_op jit(solution)/shard_map/pallas_call | solution.py:228
  28.9 0.0 collective-permute-done.5.k2
  28.9 2.4 %collective-permute-done.6.k3 = bf16[2,256,128]{2,1,0:T(8,128)(2,1)S(1)} collective-permute-done((bf16[2,256,128]{2,1,0:T(8,128)(2,1)S(1)}, bf16[2,256,128]{2,1,0:T(8,128)(2,1)S(1)}, u32[]{:S(2)}, u32[]{:S(2)}) %collective-permute-start.6) | collective-permute-done | bytes 131104 | tf_op jit(solution)/shard_map/ppermute | solution.py:29
  31.2 1.4 %shard_map.57.context_ref = bf16[64,1024]{1,0:T(8,128)(2,1)S(1)} custom-call(s32[2,64,128]{2,1,0:T(8,128)S(1)} %broadcast_in_dim.9.first_ref, bf16[64,1024]{1,0:T(8,128)(2,1)S(1)} %collective-permute-done.other_ref.query_ref, bf16[2,256,128]{2,1,0:T(8,128)(2,1)S(1)} %get-tuple-element.20.k0, bf16[2,256,128]{2,1,0:T(8,128)(2,1)S(1)} %collective-permute-done.4.k1, ...), custom_call_target="tpu_custom_call" | custom-call | tf_op jit(solution)/shard_map/pallas_call | solution.py:240
  32.6 0.8 %shard_map.59 = bf16[64,2048]{1,0:T(8,128)(2,1)S(1)} custom-call(bf16[64,1024]{1,0:T(8,128)(2,1)S(1)} %shard_map.57.context_ref, bf16[1024,4096]{1,0:T(8,128)(2,1)S(1)} %bitcast.14), custom_call_target="tpu_custom_call" | custom-call | tf_op jit(solution)/shard_map/pallas_call | solution.py:249
  33.5 3.6 %collective-permute-start.12 = (bf16[64,2048]{1,0:T(8,128)(2,1)S(1)}, bf16[64,2048]{1,0:T(8,128)(2,1)S(1)}, u32[]{:S(2)}, u32[]{:S(2)}) collective-permute-start(bf16[64,2048]{1,0:T(8,128)(2,1)S(1)} %shard_map.59), channel_id=1, source_target_pairs={{0,1},{1,0},{2,3},{3,2},{4,5},{5,4},{6,7},{7,6},{8,9},{9,8},{10,11... | collective-permute-start | bytes 786440 | tf_op jit(solution)/shard_map/ppermute | solution.py:29
  37.1 0.8 %shard_map.58 = f32[64,2048]{1,0:T(8,128)S(1)} custom-call(bf16[64,1024]{1,0:T(8,128)(2,1)S(1)} %shard_map.57.context_ref, bf16[1024,4096]{1,0:T(8,128)(2,1)S(1)} %bitcast.14), custom_call_target="tpu_custom_call" | custom-call | tf_op jit(solution)/shard_map/pallas_call | solution.py:249
  37.9 0.3 collective-permute-done.12
  38.3 2.6 %collective-permute-start.15 = (bf16[64,2048]{1,0:T(8,128)(2,1)S(1)}, bf16[64,2048]{1,0:T(8,128)(2,1)S(1)}, u32[]{:S(2)}, u32[]{:S(2)}) collective-permute-start(bf16[64,2048]{1,0:T(8,128)(2,1)S(1)} %add_convert_fusion.1), channel_id=1, source_target_pairs={{0,18},{1,19},{2,16},{3,17},{4,22},{5,23},{6,20},{7,21},{8,26},{9,... | collective-permute-start | bytes 786440 | tf_op jit(solution)/shard_map/ppermute | solution.py:29
  40.9 3.7 %shard_map.60 = (bf16[64,1024]{1,0:T(8,128)(2,1)S(1)}, bf16[64,1024]{1,0:T(8,128)(2,1)S(1)}, f32[64,2048]{1,0:T(8,128)S(1)}) custom-call(s32[2,64,128]{2,1,0:T(8,128)S(1)} %broadcast_in_dim.9.first_ref, bf16[64,1024]{1,0:T(8,128)(2,1)S(1)} %get-tuple-element.26.own_ref.query_ref, bf16[2,256,128]{2,1,0:T(8,128)(2,1)S(1)} %get-tuple-element.20.k0, ...), custom_call_target="tpu_custom_call" | custom-call | tf_op jit(solution)/shard_map/pallas_call | solution.py:264
  44.6 0.7 %collective-permute-start.13 = (bf16[64,1024]{1,0:T(8,128)(2,1)S(1)}, bf16[64,1024]{1,0:T(8,128)(2,1)S(1)}, u32[]{:S(2)}, u32[]{:S(2)}) collective-permute-start(bf16[64,1024]{1,0:T(8,128)(2,1)S(1)} %get-tuple-element.28), channel_id=1, source_target_pairs={{0,1},{1,0},{2,3},{3,2},{4,5},{5,4},{6,7},{7,6},{8,9},{9,8},{10,11... | collective-permute-start | bytes 393224 | tf_op jit(solution)/shard_map/ppermute | solution.py:29
  45.3 0.1 collective-permute-start.14
  45.4 0.9 %collective-permute-done.13 = bf16[64,1024]{1,0:T(8,128)(2,1)S(1)} collective-permute-done((bf16[64,1024]{1,0:T(8,128)(2,1)S(1)}, bf16[64,1024]{1,0:T(8,128)(2,1)S(1)}, u32[]{:S(2)}, u32[]{:S(2)}) %collective-permute-start.13) | collective-permute-done | bytes 131104 | tf_op jit(solution)/shard_map/ppermute | solution.py:29
  46.3 0.4 collective-permute-done.14
  46.7 0.4 collective-permute-done.15
  47.1 0.1 add_convert_fusion.refs_0_
  47.2 1.6 %collective-permute-start.16 = (bf16[64,2048]{1,0:T(8,128)(2,1)S(1)}, bf16[64,2048]{1,0:T(8,128)(2,1)S(1)}, u32[]{:S(2)}, u32[]{:S(2)}) collective-permute-start(bf16[64,2048]{1,0:T(8,128)(2,1)S(1)} %add_convert_fusion.refs_0_), channel_id=1, source_target_pairs={{0,2},{1,3},{2,0},{3,1},{4,6},{5,7},{6,4},{7,5},{8,10},{9,11},{10,... | collective-permute-start | bytes 786440 | tf_op jit(solution)/shard_map/ppermute | solution.py:29
  48.8 1.5 %collective-permute-start.17 = (bf16[64,2048]{1,0:T(8,128)(2,1)S(1)}, bf16[64,2048]{1,0:T(8,128)(2,1)S(1)}, u32[]{:S(2)}, u32[]{:S(2)}) collective-permute-start(bf16[64,2048]{1,0:T(8,128)(2,1)S(1)} %add_convert_fusion.refs_0_), channel_id=1, source_target_pairs={{0,1},{1,0},{2,3},{3,2},{4,5},{5,4},{6,7},{7,6},{8,9},{9,8},{10,11... | collective-permute-start | bytes 786440 | tf_op jit(solution)/shard_map/ppermute | solution.py:29
  50.3 5.1 %collective-permute-done.16.refs_1_ = bf16[64,2048]{1,0:T(8,128)(2,1)S(1)} collective-permute-done((bf16[64,2048]{1,0:T(8,128)(2,1)S(1)}, bf16[64,2048]{1,0:T(8,128)(2,1)S(1)}, u32[]{:S(2)}, u32[]{:S(2)}) %collective-permute-start.16) | collective-permute-done | bytes 262176 | tf_op jit(solution)/shard_map/ppermute | solution.py:29
  55.4 2.1 %collective-permute-start.18 = (bf16[64,2048]{1,0:T(8,128)(2,1)S(1)}, bf16[64,2048]{1,0:T(8,128)(2,1)S(1)}, u32[]{:S(2)}, u32[]{:S(2)}) collective-permute-start(bf16[64,2048]{1,0:T(8,128)(2,1)S(1)} %collective-permute-done.16.refs_1_), channel_id=1, source_target_pairs={{0,1},{1,0},{2,3},{3,2},{4,5},{5,4},{6,7},{7,6},{8,9},{9,8},{10,11... | collective-permute-start | bytes 786440 | tf_op jit(solution)/shard_map/ppermute | solution.py:29
  57.5 1.2 %collective-permute-done.18.refs_3_ = bf16[64,2048]{1,0:T(8,128)(2,1)S(1)} collective-permute-done((bf16[64,2048]{1,0:T(8,128)(2,1)S(1)}, bf16[64,2048]{1,0:T(8,128)(2,1)S(1)}, u32[]{:S(2)}, u32[]{:S(2)}) %collective-permute-start.18) | collective-permute-done | bytes 262176 | tf_op jit(solution)/shard_map/ppermute | solution.py:29
  58.7 1.0 %shard_map.61 = bf16[2,64,4096]{2,1,0:T(8,128)(2,1)} custom-call(bf16[64,2048]{1,0:T(8,128)(2,1)S(1)} %add_convert_fusion.refs_0_, bf16[64,2048]{1,0:T(8,128)(2,1)S(1)} %collective-permute-done.16.refs_1_, bf16[64,2048]{1,0:T(8,128)(2,1)S(1)} %collective-permute-done.17.refs_2_, bf16[64,2048]{1,0:T(8,128)(2,1)S(1)} %collective-permute-done.18.refs_3_), custom_call_target="tpu_custom_call" | custom-call | tf_op jit(solution)/shard_map/pallas_call | solution.py:283
  (18 shorter events, 0.1 us)
Async XLA Ops:
  0.0 4.0 %copy-start = (s32[2,4096]{1,0:T(2,128)S(1)}, s32[2,4096]{1,0:T(2,128)}, u32[]{:S(2)}) copy-start(s32[2,4096]{1,0:T(2,128)} %param.8) | copy-start | bytes 98308
  0.8 3.4 %collective-permute-start.1 = (bf16[2,64,128]{2,1,0:T(8,128)(2,1)S(1)}, bf16[2,64,128]{2,1,0:T(8,128)(2,1)S(1)}, u32[]{:S(2)}, u32[]{:S(2)}) collective-permute-start(bf16[2,64,128]{2,1,0:T(8,128)(2,1)S(1)} %get-tuple-element.19), channel_id=1, source_target_pairs={{0,16},{1,17},{2,18},{3,19},{4,20},{5,21},{6,22},{7,23},{8,24},{9,... | collective-permute-start | bytes 98312 | tf_op jit(solution)/shard_map/ppermute | solution.py:29
  3.9 18.7 %collective-permute-start = (bf16[64,1024]{1,0:T(8,128)(2,1)S(1)}, bf16[64,1024]{1,0:T(8,128)(2,1)S(1)}, u32[]{:S(2)}, u32[]{:S(2)}) collective-permute-start(bf16[64,1024]{1,0:T(8,128)(2,1)S(1)} %get-tuple-element.32), channel_id=1, source_target_pairs={{0,16},{1,17},{2,18},{3,19},{4,20},{5,21},{6,22},{7,23},{8,24},{9,... | collective-permute-start | bytes 393224 | tf_op jit(solution)/shard_map/ppermute | solution.py:29
  4.3 9.2 %collective-permute-start.8 = (bf16[2,128,128]{2,1,0:T(8,128)(2,1)S(1)}, bf16[2,128,128]{2,1,0:T(8,128)(2,1)S(1)}, u32[]{:S(2)}, u32[]{:S(2)}) collective-permute-start(bf16[2,128,128]{2,1,0:T(8,128)(2,1)S(1)} %pad_maximum_fusion.2.unit_ref), channel_id=1, source_target_pairs={{0,64},{1,65},{2,66},{3,67},{4,68},{5,69},{6,70},{7,71},{8,72},{9,... | collective-permute-start | bytes 196616 | tf_op jit(solution)/shard_map/ppermute | solution.py:29
  7.6 5.9 %collective-permute-start.7 = (bf16[2,128,128]{2,1,0:T(8,128)(2,1)S(1)}, bf16[2,128,128]{2,1,0:T(8,128)(2,1)S(1)}, u32[]{:S(2)}, u32[]{:S(2)}) collective-permute-start(bf16[2,128,128]{2,1,0:T(8,128)(2,1)S(1)} %pad_maximum_fusion.2.unit_ref), channel_id=1, source_target_pairs={{0,32},{1,33},{2,34},{3,35},{4,36},{5,37},{6,38},{7,39},{8,40},{9,... | collective-permute-start | bytes 196616 | tf_op jit(solution)/shard_map/ppermute | solution.py:29
  9.2 8.1 %collective-permute-start.3 = (bf16[2,128,128]{2,1,0:T(8,128)(2,1)S(1)}, bf16[2,128,128]{2,1,0:T(8,128)(2,1)S(1)}, u32[]{:S(2)}, u32[]{:S(2)}) collective-permute-start(bf16[2,128,128]{2,1,0:T(8,128)(2,1)S(1)} %pad_maximum_fusion.2.unit_ref), channel_id=1, source_target_pairs={{0,128},{1,129},{2,130},{3,131},{4,132},{5,133},{6,134},{7,135},{8... | collective-permute-start | bytes 196616 | tf_op jit(solution)/shard_map/ppermute | solution.py:29
  13.4 7.8 %collective-permute-start.2 = (bf16[2,128,128]{2,1,0:T(8,128)(2,1)S(1)}, bf16[2,128,128]{2,1,0:T(8,128)(2,1)S(1)}, u32[]{:S(2)}, u32[]{:S(2)}) collective-permute-start(bf16[2,128,128]{2,1,0:T(8,128)(2,1)S(1)} %pad_maximum_fusion.2.unit_ref), channel_id=1, source_target_pairs={{0,96},{1,97},{2,98},{3,99},{4,100},{5,101},{6,102},{7,103},{8,104... | collective-permute-start | bytes 196616 | tf_op jit(solution)/shard_map/ppermute | solution.py:29
  13.4 19.2 %slice-start = ((s8[8388608]{0:T(1024)(128)(4,1)}), s8[4194304]{0:T(1024)(128)(4,1)S(1)}, s32[]{:S(2)}) async-start(s8[8388608]{0:T(1024)(128)(4,1)} %bitcast.13), calls=%async_computation | async-start | bytes 8388608
  13.5 10.7 %collective-permute-start.11 = (bf16[2,320,128]{2,1,0:T(8,128)(2,1)S(1)}, bf16[2,320,128]{2,1,0:T(8,128)(2,1)S(1)}, u32[]{:S(2)}, u32[]{:S(2)}) collective-permute-start(bf16[2,320,128]{2,1,0:T(8,128)(2,1)S(1)} %pad_maximum_fusion.1), channel_id=1, source_target_pairs={{0,8},{1,9},{2,10},{3,11},{4,12},{5,13},{6,14},{7,15},{8,0},{9,1},... | collective-permute-start | bytes 491528 | tf_op jit(solution)/shard_map/ppermute | solution.py:29
  16.5 9.4 %collective-permute-start.10 = (bf16[2,320,128]{2,1,0:T(8,128)(2,1)S(1)}, bf16[2,320,128]{2,1,0:T(8,128)(2,1)S(1)}, u32[]{:S(2)}, u32[]{:S(2)}) collective-permute-start(bf16[2,320,128]{2,1,0:T(8,128)(2,1)S(1)} %pad_maximum_fusion.1), channel_id=1, source_target_pairs={{0,12},{1,13},{2,14},{3,15},{4,0},{5,1},{6,2},{7,3},{8,4},{9,5},{1... | collective-permute-start | bytes 491528 | tf_op jit(solution)/shard_map/ppermute | solution.py:29
  17.3 8.5 %collective-permute-start.9 = (bf16[2,320,128]{2,1,0:T(8,128)(2,1)S(1)}, bf16[2,320,128]{2,1,0:T(8,128)(2,1)S(1)}, u32[]{:S(2)}, u32[]{:S(2)}) collective-permute-start(bf16[2,320,128]{2,1,0:T(8,128)(2,1)S(1)} %pad_maximum_fusion.1), channel_id=1, source_target_pairs={{0,4},{1,5},{2,6},{3,7},{4,8},{5,9},{6,10},{7,11},{8,12},{9,13},{1... | collective-permute-start | bytes 491528 | tf_op jit(solution)/shard_map/ppermute | solution.py:29
  21.2 7.6 %collective-permute-start.4 = (bf16[2,256,128]{2,1,0:T(8,128)(2,1)S(1)}, bf16[2,256,128]{2,1,0:T(8,128)(2,1)S(1)}, u32[]{:S(2)}, u32[]{:S(2)}) collective-permute-start(bf16[2,256,128]{2,1,0:T(8,128)(2,1)S(1)} %get-tuple-element.21), channel_id=1, source_target_pairs={{0,4},{1,5},{2,6},{3,7},{4,8},{5,9},{6,10},{7,11},{8,12},{9,13},{1... | collective-permute-start | bytes 393224 | tf_op jit(solution)/shard_map/ppermute | solution.py:29
  22.6 6.2 %collective-permute-start.5 = (bf16[2,256,128]{2,1,0:T(8,128)(2,1)S(1)}, bf16[2,256,128]{2,1,0:T(8,128)(2,1)S(1)}, u32[]{:S(2)}, u32[]{:S(2)}) collective-permute-start(bf16[2,256,128]{2,1,0:T(8,128)(2,1)S(1)} %get-tuple-element.22), channel_id=1, source_target_pairs={{0,12},{1,13},{2,14},{3,15},{4,0},{5,1},{6,2},{7,3},{8,4},{9,5},{1... | collective-permute-start | bytes 393224 | tf_op jit(solution)/shard_map/ppermute | solution.py:29
  24.2 7.1 %collective-permute-start.6 = (bf16[2,256,128]{2,1,0:T(8,128)(2,1)S(1)}, bf16[2,256,128]{2,1,0:T(8,128)(2,1)S(1)}, u32[]{:S(2)}, u32[]{:S(2)}) collective-permute-start(bf16[2,256,128]{2,1,0:T(8,128)(2,1)S(1)} %get-tuple-element.23), channel_id=1, source_target_pairs={{0,8},{1,9},{2,10},{3,11},{4,12},{5,13},{6,14},{7,15},{8,0},{9,1},... | collective-permute-start | bytes 393224 | tf_op jit(solution)/shard_map/ppermute | solution.py:29
  25.9 6.7 %slice-start.1 = ((s8[8388608]{0:T(1024)(128)(4,1)}), s8[4194304]{0:T(1024)(128)(4,1)S(1)}, s32[]{:S(2)}) async-start(s8[8388608]{0:T(1024)(128)(4,1)} %bitcast.13), calls=%async_computation.1 | async-start | bytes 8388608
  33.5 4.8 %collective-permute-start.12 = (bf16[64,2048]{1,0:T(8,128)(2,1)S(1)}, bf16[64,2048]{1,0:T(8,128)(2,1)S(1)}, u32[]{:S(2)}, u32[]{:S(2)}) collective-permute-start(bf16[64,2048]{1,0:T(8,128)(2,1)S(1)} %shard_map.59), channel_id=1, source_target_pairs={{0,1},{1,0},{2,3},{3,2},{4,5},{5,4},{6,7},{7,6},{8,9},{9,8},{10,11... | collective-permute-start | bytes 786440 | tf_op jit(solution)/shard_map/ppermute | solution.py:29
  38.3 8.8 %collective-permute-start.15 = (bf16[64,2048]{1,0:T(8,128)(2,1)S(1)}, bf16[64,2048]{1,0:T(8,128)(2,1)S(1)}, u32[]{:S(2)}, u32[]{:S(2)}) collective-permute-start(bf16[64,2048]{1,0:T(8,128)(2,1)S(1)} %add_convert_fusion.1), channel_id=1, source_target_pairs={{0,18},{1,19},{2,16},{3,17},{4,22},{5,23},{6,20},{7,21},{8,26},{9,... | collective-permute-start | bytes 786440 | tf_op jit(solution)/shard_map/ppermute | solution.py:29
  44.6 1.7 %collective-permute-start.13 = (bf16[64,1024]{1,0:T(8,128)(2,1)S(1)}, bf16[64,1024]{1,0:T(8,128)(2,1)S(1)}, u32[]{:S(2)}, u32[]{:S(2)}) collective-permute-start(bf16[64,1024]{1,0:T(8,128)(2,1)S(1)} %get-tuple-element.28), channel_id=1, source_target_pairs={{0,1},{1,0},{2,3},{3,2},{4,5},{5,4},{6,7},{7,6},{8,9},{9,8},{10,11... | collective-permute-start | bytes 393224 | tf_op jit(solution)/shard_map/ppermute | solution.py:29
  45.3 1.3 %collective-permute-start.14 = (bf16[64,1024]{1,0:T(8,128)(2,1)S(1)}, bf16[64,1024]{1,0:T(8,128)(2,1)S(1)}, u32[]{:S(2)}, u32[]{:S(2)}) collective-permute-start(bf16[64,1024]{1,0:T(8,128)(2,1)S(1)} %get-tuple-element.29), channel_id=1, source_target_pairs={{0,1},{1,0},{2,3},{3,2},{4,5},{5,4},{6,7},{7,6},{8,9},{9,8},{10,11... | collective-permute-start | bytes 393224 | tf_op jit(solution)/shard_map/ppermute | solution.py:29
  47.2 8.2 %collective-permute-start.16 = (bf16[64,2048]{1,0:T(8,128)(2,1)S(1)}, bf16[64,2048]{1,0:T(8,128)(2,1)S(1)}, u32[]{:S(2)}, u32[]{:S(2)}) collective-permute-start(bf16[64,2048]{1,0:T(8,128)(2,1)S(1)} %add_convert_fusion.refs_0_), channel_id=1, source_target_pairs={{0,2},{1,3},{2,0},{3,1},{4,6},{5,7},{6,4},{7,5},{8,10},{9,11},{10,... | collective-permute-start | bytes 786440 | tf_op jit(solution)/shard_map/ppermute | solution.py:29
  48.8 8.7 %collective-permute-start.17 = (bf16[64,2048]{1,0:T(8,128)(2,1)S(1)}, bf16[64,2048]{1,0:T(8,128)(2,1)S(1)}, u32[]{:S(2)}, u32[]{:S(2)}) collective-permute-start(bf16[64,2048]{1,0:T(8,128)(2,1)S(1)} %add_convert_fusion.refs_0_), channel_id=1, source_target_pairs={{0,1},{1,0},{2,3},{3,2},{4,5},{5,4},{6,7},{7,6},{8,9},{9,8},{10,11... | collective-permute-start | bytes 786440 | tf_op jit(solution)/shard_map/ppermute | solution.py:29
  55.4 3.3 %collective-permute-start.18 = (bf16[64,2048]{1,0:T(8,128)(2,1)S(1)}, bf16[64,2048]{1,0:T(8,128)(2,1)S(1)}, u32[]{:S(2)}, u32[]{:S(2)}) collective-permute-start(bf16[64,2048]{1,0:T(8,128)(2,1)S(1)} %collective-permute-done.16.refs_1_), channel_id=1, source_target_pairs={{0,1},{1,0},{2,3},{3,2},{4,5},{5,4},{6,7},{7,6},{8,9},{9,8},{10,11... | collective-permute-start | bytes 786440 | tf_op jit(solution)/shard_map/ppermute | solution.py:29

commit v8 on v7

--- a/solution.py
+++ b/solution.py
@@ -106,16 +106,16 @@
     return highest, total, mixed
 
 
-def near_kernel(heads, size, block, first_ref, own_ref, other_ref, k0, k1, k2, k3, mixed_ref, stat_ref):
+def near_kernel(heads, size, block, first_ref, own_ref, other_ref, k0, k1, k2, k3, far_own, mixed_ref, stat_ref):
     scale = math.log2(math.e) / math.sqrt(size)
     lane = lax.broadcasted_iota(jnp.int32, (block, 128), 1)
     for which, query_ref in enumerate((own_ref, other_ref)):
-        bias = bias_of(first_ref, which, False, block)
+        bias = bias_of(first_ref, which, False, block) + bias_of(first_ref, which, True, block)[:1]
         stats = jnp.zeros((block, 128), jnp.float32)
         for start in range(0, heads, GROUP):
             group = range(start, start + GROUP)
             queries = jnp.concatenate([query_ref[:, h * size:(h + 1) * size] for h in group], axis=0)
-            highest, total, mixed = attend_group(queries, (k0, k1, k2, k3), bias, None, scale)
+            highest, total, mixed = attend_group(queries, (k0, k1, k2, k3, far_own), bias, None, scale)
             for i, head in enumerate(group):
                 part = slice(i * block, (i + 1) * block)
                 mixed_ref[which, :, head * size:(head + 1) * size] = mixed[part]
@@ -126,7 +126,7 @@
 
 def far_block(heads, size, block, which, first_ref, query_ref, kv_refs, mixed_ref, stat_ref, context_ref):
     scale = math.log2(math.e) / math.sqrt(size)
-    bias = bias_of(first_ref, which, True, block)
+    bias = bias_of(first_ref, which, True, block)[1:]
     stats = stat_ref[which]
     for start in range(0, heads, GROUP):
         group = range(start, start + GROUP)
@@ -140,8 +140,8 @@
             context_ref[:, at] = ((mixed[part] + mixed_ref[which, :, at] * fade[part]) / whole).astype(jnp.bfloat16)
 
 
-def far_kernel(heads, size, block, first_ref, query_ref, k0, k1, k2, k3, mixed_ref, stat_ref, context_ref):
-    far_block(heads, size, block, 1, first_ref, query_ref, (k0, k1, k2, k3), mixed_ref, stat_ref, context_ref)
+def far_kernel(heads, size, block, first_ref, query_ref, k1, k2, k3, mixed_ref, stat_ref, context_ref):
+    far_block(heads, size, block, 1, first_ref, query_ref, (k1, k2, k3), mixed_ref, stat_ref, context_ref)
 
 
 def pack_kernel(block, unit_ref, third_ref, fourth_ref, *out_refs):
@@ -167,8 +167,8 @@
     project(own_half, context_ref, weight_ref, out_ref)
 
 
-def far_project_kernel(heads, size, block, first_ref, query_ref, k0, k1, k2, k3, mixed_ref, stat_ref, weight_ref, give0_ref, give1_ref, keep_ref, context_ref):
-    far_block(heads, size, block, 0, first_ref, query_ref, (k0, k1, k2, k3), mixed_ref, stat_ref, context_ref)
+def far_project_kernel(heads, size, block, first_ref, query_ref, k1, k2, k3, mixed_ref, stat_ref, weight_ref, give0_ref, give1_ref, keep_ref, context_ref):
+    far_block(heads, size, block, 0, first_ref, query_ref, (k1, k2, k3), mixed_ref, stat_ref, context_ref)
     project(False, context_ref, weight_ref, give0_ref, 2, 0)
     project(False, context_ref, weight_ref, give1_ref, 2, 1)
     project(True, context_ref, weight_ref, keep_ref)
@@ -231,19 +231,19 @@
             jax.ShapeDtypeStruct((2, block, width), jnp.float32),
             jax.ShapeDtypeStruct((2, block, 128), jnp.float32),
         ),
-        in_specs=[VMEM] * 7,
+        in_specs=[VMEM] * 8,
         out_specs=(VMEM, VMEM),
         compiler_params=LIMIT,
         cost_estimate=LONG,
-    )(first, own_q, other_q, *near_all)
+    )(first, own_q, other_q, *near_all, far_all[0])
 
     other_context = pl.pallas_call(
         functools.partial(far_kernel, heads, size, block),
         out_shape=jax.ShapeDtypeStruct((block, width), jnp.bfloat16),
-        in_specs=[VMEM] * 8,
+        in_specs=[VMEM] * 7,
         out_specs=VMEM,
         compiler_params=LIMIT,
-    )(first, other_q, *far_all, mixed, stats)
+    )(first, other_q, *far_all[1:], mixed, stats)
 
     def projected(own_half, dtype):
         return pl.pallas_call(
@@ -268,11 +268,11 @@
             jax.ShapeDtypeStruct((block, features // 4), jnp.bfloat16),
             jax.ShapeDtypeStruct((block, features // 2), jnp.float32),
         ),
-        in_specs=[VMEM] * 9,
+        in_specs=[VMEM] * 8,
         out_specs=(VMEM, VMEM, VMEM),
         scratch_shapes=[pltpu.VMEM((block, width), jnp.bfloat16)],
         compiler_params=LIMIT,
-    )(first, own_q, *far_all, mixed, stats, out_weight)
+    )(first, own_q, *far_all[1:], mixed, stats, out_weight)
     given = jnp.concatenate([swap_core(given0), swap_core(given1)], axis=1)
     summed = kept + given.astype(jnp.float32)
 

time: 60 us -> 60 us (level)
  no operation moved by 1% of the time
where the time goes in v8:
time: 60 us; the launch traced here: 59.8 us
  starting transfers between devices  33.2 us (55%)
  waiting for transfers between devices  13 us (22%)
  Pallas kernels  10.9 us (18%)
  other arithmetic  1.2 us (2%)
  local copies, waits for them, and re-layouts  1.09 us (2%)
    ppermute x19, starting transfers between devices, shift(): lax.ppermute(array, AXES, [(flat(*d), flat(*move(*d))) for d in devices])  33.2 us
    ppermute x19, waiting for transfers between devices, shift(): lax.ppermute(array, AXES, [(flat(*d), flat(*move(*d))) for d in devices])  13 us
    pallas_call x1, Pallas kernels, body(): pl.pallas_call(functools.partial(far_project_kernel, heads, size, block),...  3.55 us
    pallas_call x1, Pallas kernels, body(): pl.pallas_call(functools.partial(near_kernel, heads, size, block), out_sh...  3.28 us
    pallas_call x2, Pallas kernels, projected(): pl.pallas_call(functools.partial(project_kernel, own_half), out_shape=jax...  1.68 us
    pallas_call x1, Pallas kernels, body(): pl.pallas_call(functools.partial(far_kernel, heads, size, block), out_sha...  1.31 us
  transfers between devices with their start and end apart: 19, of which 9 were waited for; matrix products, arithmetic and copies ran while one was open for 2% of the time, Pallas kernels for 13%

profile of v8, /device:TPU:1, one launch (start us, length us, event | category | flops | bytes accessed | tf_op | source)
XLA Modules:
  0.0 59.8 jit_solution(8368890354747873323)
XLA Ops:
  0.0 0.8 %fusion.1 = (bf16[2,64,128]{2,1,0:T(8,128)(2,1)S(1)}, bf16[2,64,128]{2,1,0:T(8,128)(2,1)S(1)}) fusion(s32[]{:T(128)S(6)} %select_n.65, bf16[2,1,64,128]{3,2,0,1:T(8,128)(2,1)} %bitcast.16, bf16[2,1,64,128]{3,2,0,1:T(8,128)(2,1)} %bitcast.17, s32[]{:T(128)S(6)} %select_n.61), kind=kLoop, calls=%fused_computation.14 | loop fusion | flops 32768 | bytes 131080 | tf_op jit(solution)/shard_map/jit(dynamic_index_in_dim)/squeeze | solution.py:201
  0.8 2.1 %collective-permute-start.1 = (bf16[2,64,128]{2,1,0:T(8,128)(2,1)S(1)}, bf16[2,64,128]{2,1,0:T(8,128)(2,1)S(1)}, u32[]{:S(2)}, u32[]{:S(2)}) collective-permute-start(bf16[2,64,128]{2,1,0:T(8,128)(2,1)S(1)} %get-tuple-element.19), channel_id=1, source_target_pairs={{0,16},{1,17},{2,18},{3,19},{4,20},{5,21},{6,22},{7,23},{8,24},{9,... | collective-permute-start | bytes 98312 | tf_op jit(solution)/shard_map/ppermute | solution.py:29
  2.9 1.0 %dynamic-slice_bitcast_fusion = (bf16[64,1024]{1,0:T(8,128)(2,1)S(1)}, bf16[64,1024]{1,0:T(8,128)(2,1)S(1)}) fusion(bf16[2,64,1024]{2,1,0:T(8,128)(2,1)} %param.5, s32[]{:T(128)S(6)} %select_n.61, s32[]{:T(128)S(6)} %select_n.65), kind=kLoop, calls=%fused_computation.4 | loop fusion | bytes 524296 | tf_op jit(solution)/shard_map/jit(dynamic_index_in_dim)/squeeze | solution.py:201
  3.9 0.1 collective-permute-start
  4.1 0.1 convert_reduce_fusion
  4.2 0.0 collective-permute-done.1
  4.3 3.3 %collective-permute-start.8 = (bf16[2,128,128]{2,1,0:T(8,128)(2,1)S(1)}, bf16[2,128,128]{2,1,0:T(8,128)(2,1)S(1)}, u32[]{:S(2)}, u32[]{:S(2)}) collective-permute-start(bf16[2,128,128]{2,1,0:T(8,128)(2,1)S(1)} %pad_maximum_fusion.2.unit_ref), channel_id=1, source_target_pairs={{0,64},{1,65},{2,66},{3,67},{4,68},{5,69},{6,70},{7,71},{8,72},{9,... | collective-permute-start | bytes 196616 | tf_op jit(solution)/shard_map/ppermute | solution.py:29
  7.6 1.6 %collective-permute-start.7 = (bf16[2,128,128]{2,1,0:T(8,128)(2,1)S(1)}, bf16[2,128,128]{2,1,0:T(8,128)(2,1)S(1)}, u32[]{:S(2)}, u32[]{:S(2)}) collective-permute-start(bf16[2,128,128]{2,1,0:T(8,128)(2,1)S(1)} %pad_maximum_fusion.2.unit_ref), channel_id=1, source_target_pairs={{0,32},{1,33},{2,34},{3,35},{4,36},{5,37},{6,38},{7,39},{8,40},{9,... | collective-permute-start | bytes 196616 | tf_op jit(solution)/shard_map/ppermute | solution.py:29
  9.2 4.2 %collective-permute-start.3 = (bf16[2,128,128]{2,1,0:T(8,128)(2,1)S(1)}, bf16[2,128,128]{2,1,0:T(8,128)(2,1)S(1)}, u32[]{:S(2)}, u32[]{:S(2)}) collective-permute-start(bf16[2,128,128]{2,1,0:T(8,128)(2,1)S(1)} %pad_maximum_fusion.2.unit_ref), channel_id=1, source_target_pairs={{0,128},{1,129},{2,130},{3,131},{4,132},{5,133},{6,134},{7,135},{8... | collective-permute-start | bytes 196616 | tf_op jit(solution)/shard_map/ppermute | solution.py:29
  13.4 0.0 collective-permute-start.2
  13.4 0.0 collective-permute-done.8
  13.4 0.0 slice-start
  13.5 3.0 %collective-permute-start.11 = (bf16[2,320,128]{2,1,0:T(8,128)(2,1)S(1)}, bf16[2,320,128]{2,1,0:T(8,128)(2,1)S(1)}, u32[]{:S(2)}, u32[]{:S(2)}) collective-permute-start(bf16[2,320,128]{2,1,0:T(8,128)(2,1)S(1)} %pad_maximum_fusion.1), channel_id=1, source_target_pairs={{0,8},{1,9},{2,10},{3,11},{4,12},{5,13},{6,14},{7,15},{8,0},{9,1},... | collective-permute-start | bytes 491528 | tf_op jit(solution)/shard_map/ppermute | solution.py:29
  16.5 0.8 %collective-permute-start.10 = (bf16[2,320,128]{2,1,0:T(8,128)(2,1)S(1)}, bf16[2,320,128]{2,1,0:T(8,128)(2,1)S(1)}, u32[]{:S(2)}, u32[]{:S(2)}) collective-permute-start(bf16[2,320,128]{2,1,0:T(8,128)(2,1)S(1)} %pad_maximum_fusion.1), channel_id=1, source_target_pairs={{0,12},{1,13},{2,14},{3,15},{4,0},{5,1},{6,2},{7,3},{8,4},{9,5},{1... | collective-permute-start | bytes 491528 | tf_op jit(solution)/shard_map/ppermute | solution.py:29
  17.2 0.1 collective-permute-done.3.fourth_ref
  17.3 1.3 %collective-permute-start.9 = (bf16[2,320,128]{2,1,0:T(8,128)(2,1)S(1)}, bf16[2,320,128]{2,1,0:T(8,128)(2,1)S(1)}, u32[]{:S(2)}, u32[]{:S(2)}) collective-permute-start(bf16[2,320,128]{2,1,0:T(8,128)(2,1)S(1)} %pad_maximum_fusion.1), channel_id=1, source_target_pairs={{0,4},{1,5},{2,6},{3,7},{4,8},{5,9},{6,10},{7,11},{8,12},{9,13},{1... | collective-permute-start | bytes 491528 | tf_op jit(solution)/shard_map/ppermute | solution.py:29
  18.6 0.1 select_reduce_fusion
  18.7 2.4 %collective-permute-done.2.third_ref = bf16[2,128,128]{2,1,0:T(8,128)(2,1)S(1)} collective-permute-done((bf16[2,128,128]{2,1,0:T(8,128)(2,1)S(1)}, bf16[2,128,128]{2,1,0:T(8,128)(2,1)S(1)}, u32[]{:S(2)}, u32[]{:S(2)}) %collective-permute-start.2) | collective-permute-done | bytes 65568 | tf_op jit(solution)/shard_map/ppermute | solution.py:29
  21.2 0.1 shard_map.55
  21.2 1.4 %collective-permute-start.4 = (bf16[2,256,128]{2,1,0:T(8,128)(2,1)S(1)}, bf16[2,256,128]{2,1,0:T(8,128)(2,1)S(1)}, u32[]{:S(2)}, u32[]{:S(2)}) collective-permute-start(bf16[2,256,128]{2,1,0:T(8,128)(2,1)S(1)} %get-tuple-element.20), channel_id=1, source_target_pairs={{0,4},{1,5},{2,6},{3,7},{4,8},{5,9},{6,10},{7,11},{8,12},{9,13},{1... | collective-permute-start | bytes 393224 | tf_op jit(solution)/shard_map/ppermute | solution.py:29
  22.6 1.5 %collective-permute-start.5 = (bf16[2,256,128]{2,1,0:T(8,128)(2,1)S(1)}, bf16[2,256,128]{2,1,0:T(8,128)(2,1)S(1)}, u32[]{:S(2)}, u32[]{:S(2)}) collective-permute-start(bf16[2,256,128]{2,1,0:T(8,128)(2,1)S(1)} %get-tuple-element.21), channel_id=1, source_target_pairs={{0,12},{1,13},{2,14},{3,15},{4,0},{5,1},{6,2},{7,3},{8,4},{9,5},{1... | collective-permute-start | bytes 393224 | tf_op jit(solution)/shard_map/ppermute | solution.py:29
  24.2 0.0 collective-permute-done.11.k3
  24.2 1.6 %collective-permute-start.6 = (bf16[2,256,128]{2,1,0:T(8,128)(2,1)S(1)}, bf16[2,256,128]{2,1,0:T(8,128)(2,1)S(1)}, u32[]{:S(2)}, u32[]{:S(2)}) collective-permute-start(bf16[2,256,128]{2,1,0:T(8,128)(2,1)S(1)} %get-tuple-element.22), channel_id=1, source_target_pairs={{0,8},{1,9},{2,10},{3,11},{4,12},{5,13},{6,14},{7,15},{8,0},{9,1},... | collective-permute-start | bytes 393224 | tf_op jit(solution)/shard_map/ppermute | solution.py:29
  25.8 0.1 broadcast_in_dim.9.first_ref
  25.9 0.0 slice-start.1
  25.9 3.3 %shard_map.56 = (f32[2,64,1024]{2,1,0:T(8,128)S(1)}, f32[2,64,128]{2,1,0:T(8,128)S(1)}) custom-call(s32[2,64,128]{2,1,0:T(8,128)S(1)} %broadcast_in_dim.9.first_ref, bf16[64,1024]{1,0:T(8,128)(2,1)S(1)} %get-tuple-element.26.own_ref.query_ref, bf16[64,1024]{1,0:T(8,128)(2,1)S(1)} %collective-permute-done.other_ref.query_ref, ...), custom_call_target="tpu_custom_call" | custom-call | flops 17179869184 | bytes 16777216 | tf_op jit(solution)/shard_map/pallas_call | solution.py:228
  29.2 0.0 collective-permute-done.4.k1
  29.2 0.0 collective-permute-done.5.k2
  29.2 2.0 %collective-permute-done.6.k3 = bf16[2,256,128]{2,1,0:T(8,128)(2,1)S(1)} collective-permute-done((bf16[2,256,128]{2,1,0:T(8,128)(2,1)S(1)}, bf16[2,256,128]{2,1,0:T(8,128)(2,1)S(1)}, u32[]{:S(2)}, u32[]{:S(2)}) %collective-permute-start.6) | collective-permute-done | bytes 131104 | tf_op jit(solution)/shard_map/ppermute | solution.py:29
  31.2 1.3 %shard_map.57.context_ref = bf16[64,1024]{1,0:T(8,128)(2,1)S(1)} custom-call(s32[2,64,128]{2,1,0:T(8,128)S(1)} %broadcast_in_dim.9.first_ref, bf16[64,1024]{1,0:T(8,128)(2,1)S(1)} %collective-permute-done.other_ref.query_ref, bf16[2,256,128]{2,1,0:T(8,128)(2,1)S(1)} %collective-permute-done.4.k1, bf16[2,256,128]{2,1,0:T(8,128)(2,1)S(1)} %collective-permute-done.5.k2, ...), custom_call_target="tpu_custom_call" | custom-call | tf_op jit(solution)/shard_map/pallas_call | solution.py:240
  32.6 0.8 %shard_map.59 = bf16[64,2048]{1,0:T(8,128)(2,1)S(1)} custom-call(bf16[64,1024]{1,0:T(8,128)(2,1)S(1)} %shard_map.57.context_ref, bf16[1024,4096]{1,0:T(8,128)(2,1)S(1)} %bitcast.14), custom_call_target="tpu_custom_call" | custom-call | tf_op jit(solution)/shard_map/pallas_call | solution.py:249
  33.4 3.6 %collective-permute-start.12 = (bf16[64,2048]{1,0:T(8,128)(2,1)S(1)}, bf16[64,2048]{1,0:T(8,128)(2,1)S(1)}, u32[]{:S(2)}, u32[]{:S(2)}) collective-permute-start(bf16[64,2048]{1,0:T(8,128)(2,1)S(1)} %shard_map.59), channel_id=1, source_target_pairs={{0,1},{1,0},{2,3},{3,2},{4,5},{5,4},{6,7},{7,6},{8,9},{9,8},{10,11... | collective-permute-start | bytes 786440 | tf_op jit(solution)/shard_map/ppermute | solution.py:29
  37.0 0.8 %shard_map.58 = f32[64,2048]{1,0:T(8,128)S(1)} custom-call(bf16[64,1024]{1,0:T(8,128)(2,1)S(1)} %shard_map.57.context_ref, bf16[1024,4096]{1,0:T(8,128)(2,1)S(1)} %bitcast.14), custom_call_target="tpu_custom_call" | custom-call | tf_op jit(solution)/shard_map/pallas_call | solution.py:249
  37.9 0.3 collective-permute-done.12
  38.3 2.6 %collective-permute-start.15 = (bf16[64,2048]{1,0:T(8,128)(2,1)S(1)}, bf16[64,2048]{1,0:T(8,128)(2,1)S(1)}, u32[]{:S(2)}, u32[]{:S(2)}) collective-permute-start(bf16[64,2048]{1,0:T(8,128)(2,1)S(1)} %add_convert_fusion.1), channel_id=1, source_target_pairs={{0,18},{1,19},{2,16},{3,17},{4,22},{5,23},{6,20},{7,21},{8,26},{9,... | collective-permute-start | bytes 786440 | tf_op jit(solution)/shard_map/ppermute | solution.py:29
  40.8 3.5 %shard_map.60 = (bf16[64,1024]{1,0:T(8,128)(2,1)S(1)}, bf16[64,1024]{1,0:T(8,128)(2,1)S(1)}, f32[64,2048]{1,0:T(8,128)S(1)}) custom-call(s32[2,64,128]{2,1,0:T(8,128)S(1)} %broadcast_in_dim.9.first_ref, bf16[64,1024]{1,0:T(8,128)(2,1)S(1)} %get-tuple-element.26.own_ref.query_ref, bf16[2,256,128]{2,1,0:T(8,128)(2,1)S(1)} %collective-permute-done.4.k1, ...), custom_call_target="tpu_custom_call" | custom-call | tf_op jit(solution)/shard_map/pallas_call | solution.py:264
  44.4 0.7 %collective-permute-start.13 = (bf16[64,1024]{1,0:T(8,128)(2,1)S(1)}, bf16[64,1024]{1,0:T(8,128)(2,1)S(1)}, u32[]{:S(2)}, u32[]{:S(2)}) collective-permute-start(bf16[64,1024]{1,0:T(8,128)(2,1)S(1)} %get-tuple-element.28), channel_id=1, source_target_pairs={{0,1},{1,0},{2,3},{3,2},{4,5},{5,4},{6,7},{7,6},{8,9},{9,8},{10,11... | collective-permute-start | bytes 393224 | tf_op jit(solution)/shard_map/ppermute | solution.py:29
  45.1 0.1 collective-permute-start.14
  45.2 0.9 %collective-permute-done.13 = bf16[64,1024]{1,0:T(8,128)(2,1)S(1)} collective-permute-done((bf16[64,1024]{1,0:T(8,128)(2,1)S(1)}, bf16[64,1024]{1,0:T(8,128)(2,1)S(1)}, u32[]{:S(2)}, u32[]{:S(2)}) %collective-permute-start.13) | collective-permute-done | bytes 131104 | tf_op jit(solution)/shard_map/ppermute | solution.py:29
  46.1 0.4 collective-permute-done.14
  46.5 0.6 %collective-permute-done.15 = bf16[64,2048]{1,0:T(8,128)(2,1)S(1)} collective-permute-done((bf16[64,2048]{1,0:T(8,128)(2,1)S(1)}, bf16[64,2048]{1,0:T(8,128)(2,1)S(1)}, u32[]{:S(2)}, u32[]{:S(2)}) %collective-permute-start.15) | collective-permute-done | bytes 262176 | tf_op jit(solution)/shard_map/ppermute | solution.py:29
  47.1 0.1 add_convert_fusion.refs_0_
  47.2 1.6 %collective-permute-start.16 = (bf16[64,2048]{1,0:T(8,128)(2,1)S(1)}, bf16[64,2048]{1,0:T(8,128)(2,1)S(1)}, u32[]{:S(2)}, u32[]{:S(2)}) collective-permute-start(bf16[64,2048]{1,0:T(8,128)(2,1)S(1)} %add_convert_fusion.refs_0_), channel_id=1, source_target_pairs={{0,2},{1,3},{2,0},{3,1},{4,6},{5,7},{6,4},{7,5},{8,10},{9,11},{10,... | collective-permute-start | bytes 786440 | tf_op jit(solution)/shard_map/ppermute | solution.py:29
  48.8 1.5 %collective-permute-start.17 = (bf16[64,2048]{1,0:T(8,128)(2,1)S(1)}, bf16[64,2048]{1,0:T(8,128)(2,1)S(1)}, u32[]{:S(2)}, u32[]{:S(2)}) collective-permute-start(bf16[64,2048]{1,0:T(8,128)(2,1)S(1)} %add_convert_fusion.refs_0_), channel_id=1, source_target_pairs={{0,1},{1,0},{2,3},{3,2},{4,5},{5,4},{6,7},{7,6},{8,9},{9,8},{10,11... | collective-permute-start | bytes 786440 | tf_op jit(solution)/shard_map/ppermute | solution.py:29
  50.3 5.1 %collective-permute-done.16.refs_1_ = bf16[64,2048]{1,0:T(8,128)(2,1)S(1)} collective-permute-done((bf16[64,2048]{1,0:T(8,128)(2,1)S(1)}, bf16[64,2048]{1,0:T(8,128)(2,1)S(1)}, u32[]{:S(2)}, u32[]{:S(2)}) %collective-permute-start.16) | collective-permute-done | bytes 262176 | tf_op jit(solution)/shard_map/ppermute | solution.py:29
  55.4 2.1 %collective-permute-start.18 = (bf16[64,2048]{1,0:T(8,128)(2,1)S(1)}, bf16[64,2048]{1,0:T(8,128)(2,1)S(1)}, u32[]{:S(2)}, u32[]{:S(2)}) collective-permute-start(bf16[64,2048]{1,0:T(8,128)(2,1)S(1)} %collective-permute-done.16.refs_1_), channel_id=1, source_target_pairs={{0,1},{1,0},{2,3},{3,2},{4,5},{5,4},{6,7},{7,6},{8,9},{9,8},{10,11... | collective-permute-start | bytes 786440 | tf_op jit(solution)/shard_map/ppermute | solution.py:29
  57.5 1.2 %collective-permute-done.18.refs_3_ = bf16[64,2048]{1,0:T(8,128)(2,1)S(1)} collective-permute-done((bf16[64,2048]{1,0:T(8,128)(2,1)S(1)}, bf16[64,2048]{1,0:T(8,128)(2,1)S(1)}, u32[]{:S(2)}, u32[]{:S(2)}) %collective-permute-start.18) | collective-permute-done | bytes 262176 | tf_op jit(solution)/shard_map/ppermute | solution.py:29
  58.6 1.0 %shard_map.61 = bf16[2,64,4096]{2,1,0:T(8,128)(2,1)} custom-call(bf16[64,2048]{1,0:T(8,128)(2,1)S(1)} %add_convert_fusion.refs_0_, bf16[64,2048]{1,0:T(8,128)(2,1)S(1)} %collective-permute-done.16.refs_1_, bf16[64,2048]{1,0:T(8,128)(2,1)S(1)} %collective-permute-done.17.refs_2_, bf16[64,2048]{1,0:T(8,128)(2,1)S(1)} %collective-permute-done.18.refs_3_), custom_call_target="tpu_custom_call" | custom-call | tf_op jit(solution)/shard_map/pallas_call | solution.py:283
  (18 shorter events, 0.1 us)
Async XLA Ops:
  0.0 4.0 %copy-start = (s32[2,4096]{1,0:T(2,128)S(1)}, s32[2,4096]{1,0:T(2,128)}, u32[]{:S(2)}) copy-start(s32[2,4096]{1,0:T(2,128)} %param.8) | copy-start | bytes 98308
  0.8 3.4 %collective-permute-start.1 = (bf16[2,64,128]{2,1,0:T(8,128)(2,1)S(1)}, bf16[2,64,128]{2,1,0:T(8,128)(2,1)S(1)}, u32[]{:S(2)}, u32[]{:S(2)}) collective-permute-start(bf16[2,64,128]{2,1,0:T(8,128)(2,1)S(1)} %get-tuple-element.19), channel_id=1, source_target_pairs={{0,16},{1,17},{2,18},{3,19},{4,20},{5,21},{6,22},{7,23},{8,24},{9,... | collective-permute-start | bytes 98312 | tf_op jit(solution)/shard_map/ppermute | solution.py:29
  3.9 18.7 %collective-permute-start = (bf16[64,1024]{1,0:T(8,128)(2,1)S(1)}, bf16[64,1024]{1,0:T(8,128)(2,1)S(1)}, u32[]{:S(2)}, u32[]{:S(2)}) collective-permute-start(bf16[64,1024]{1,0:T(8,128)(2,1)S(1)} %get-tuple-element.32), channel_id=1, source_target_pairs={{0,16},{1,17},{2,18},{3,19},{4,20},{5,21},{6,22},{7,23},{8,24},{9,... | collective-permute-start | bytes 393224 | tf_op jit(solution)/shard_map/ppermute | solution.py:29
  4.3 9.2 %collective-permute-start.8 = (bf16[2,128,128]{2,1,0:T(8,128)(2,1)S(1)}, bf16[2,128,128]{2,1,0:T(8,128)(2,1)S(1)}, u32[]{:S(2)}, u32[]{:S(2)}) collective-permute-start(bf16[2,128,128]{2,1,0:T(8,128)(2,1)S(1)} %pad_maximum_fusion.2.unit_ref), channel_id=1, source_target_pairs={{0,64},{1,65},{2,66},{3,67},{4,68},{5,69},{6,70},{7,71},{8,72},{9,... | collective-permute-start | bytes 196616 | tf_op jit(solution)/shard_map/ppermute | solution.py:29
  7.6 5.9 %collective-permute-start.7 = (bf16[2,128,128]{2,1,0:T(8,128)(2,1)S(1)}, bf16[2,128,128]{2,1,0:T(8,128)(2,1)S(1)}, u32[]{:S(2)}, u32[]{:S(2)}) collective-permute-start(bf16[2,128,128]{2,1,0:T(8,128)(2,1)S(1)} %pad_maximum_fusion.2.unit_ref), channel_id=1, source_target_pairs={{0,32},{1,33},{2,34},{3,35},{4,36},{5,37},{6,38},{7,39},{8,40},{9,... | collective-permute-start | bytes 196616 | tf_op jit(solution)/shard_map/ppermute | solution.py:29
  9.2 8.1 %collective-permute-start.3 = (bf16[2,128,128]{2,1,0:T(8,128)(2,1)S(1)}, bf16[2,128,128]{2,1,0:T(8,128)(2,1)S(1)}, u32[]{:S(2)}, u32[]{:S(2)}) collective-permute-start(bf16[2,128,128]{2,1,0:T(8,128)(2,1)S(1)} %pad_maximum_fusion.2.unit_ref), channel_id=1, source_target_pairs={{0,128},{1,129},{2,130},{3,131},{4,132},{5,133},{6,134},{7,135},{8... | collective-permute-start | bytes 196616 | tf_op jit(solution)/shard_map/ppermute | solution.py:29
  13.4 7.8 %collective-permute-start.2 = (bf16[2,128,128]{2,1,0:T(8,128)(2,1)S(1)}, bf16[2,128,128]{2,1,0:T(8,128)(2,1)S(1)}, u32[]{:S(2)}, u32[]{:S(2)}) collective-permute-start(bf16[2,128,128]{2,1,0:T(8,128)(2,1)S(1)} %pad_maximum_fusion.2.unit_ref), channel_id=1, source_target_pairs={{0,96},{1,97},{2,98},{3,99},{4,100},{5,101},{6,102},{7,103},{8,104... | collective-permute-start | bytes 196616 | tf_op jit(solution)/shard_map/ppermute | solution.py:29
  13.4 19.1 %slice-start = ((s8[8388608]{0:T(1024)(128)(4,1)}), s8[4194304]{0:T(1024)(128)(4,1)S(1)}, s32[]{:S(2)}) async-start(s8[8388608]{0:T(1024)(128)(4,1)} %bitcast.13), calls=%async_computation | async-start | bytes 8388608
  13.5 10.7 %collective-permute-start.11 = (bf16[2,320,128]{2,1,0:T(8,128)(2,1)S(1)}, bf16[2,320,128]{2,1,0:T(8,128)(2,1)S(1)}, u32[]{:S(2)}, u32[]{:S(2)}) collective-permute-start(bf16[2,320,128]{2,1,0:T(8,128)(2,1)S(1)} %pad_maximum_fusion.1), channel_id=1, source_target_pairs={{0,8},{1,9},{2,10},{3,11},{4,12},{5,13},{6,14},{7,15},{8,0},{9,1},... | collective-permute-start | bytes 491528 | tf_op jit(solution)/shard_map/ppermute | solution.py:29
  16.5 9.4 %collective-permute-start.10 = (bf16[2,320,128]{2,1,0:T(8,128)(2,1)S(1)}, bf16[2,320,128]{2,1,0:T(8,128)(2,1)S(1)}, u32[]{:S(2)}, u32[]{:S(2)}) collective-permute-start(bf16[2,320,128]{2,1,0:T(8,128)(2,1)S(1)} %pad_maximum_fusion.1), channel_id=1, source_target_pairs={{0,12},{1,13},{2,14},{3,15},{4,0},{5,1},{6,2},{7,3},{8,4},{9,5},{1... | collective-permute-start | bytes 491528 | tf_op jit(solution)/shard_map/ppermute | solution.py:29
  17.3 8.5 %collective-permute-start.9 = (bf16[2,320,128]{2,1,0:T(8,128)(2,1)S(1)}, bf16[2,320,128]{2,1,0:T(8,128)(2,1)S(1)}, u32[]{:S(2)}, u32[]{:S(2)}) collective-permute-start(bf16[2,320,128]{2,1,0:T(8,128)(2,1)S(1)} %pad_maximum_fusion.1), channel_id=1, source_target_pairs={{0,4},{1,5},{2,6},{3,7},{4,8},{5,9},{6,10},{7,11},{8,12},{9,13},{1... | collective-permute-start | bytes 491528 | tf_op jit(solution)/shard_map/ppermute | solution.py:29
  21.2 7.9 %collective-permute-start.4 = (bf16[2,256,128]{2,1,0:T(8,128)(2,1)S(1)}, bf16[2,256,128]{2,1,0:T(8,128)(2,1)S(1)}, u32[]{:S(2)}, u32[]{:S(2)}) collective-permute-start(bf16[2,256,128]{2,1,0:T(8,128)(2,1)S(1)} %get-tuple-element.20), channel_id=1, source_target_pairs={{0,4},{1,5},{2,6},{3,7},{4,8},{5,9},{6,10},{7,11},{8,12},{9,13},{1... | collective-permute-start | bytes 393224 | tf_op jit(solution)/shard_map/ppermute | solution.py:29
  22.6 6.6 %collective-permute-start.5 = (bf16[2,256,128]{2,1,0:T(8,128)(2,1)S(1)}, bf16[2,256,128]{2,1,0:T(8,128)(2,1)S(1)}, u32[]{:S(2)}, u32[]{:S(2)}) collective-permute-start(bf16[2,256,128]{2,1,0:T(8,128)(2,1)S(1)} %get-tuple-element.21), channel_id=1, source_target_pairs={{0,12},{1,13},{2,14},{3,15},{4,0},{5,1},{6,2},{7,3},{8,4},{9,5},{1... | collective-permute-start | bytes 393224 | tf_op jit(solution)/shard_map/ppermute | solution.py:29
  24.2 7.1 %collective-permute-start.6 = (bf16[2,256,128]{2,1,0:T(8,128)(2,1)S(1)}, bf16[2,256,128]{2,1,0:T(8,128)(2,1)S(1)}, u32[]{:S(2)}, u32[]{:S(2)}) collective-permute-start(bf16[2,256,128]{2,1,0:T(8,128)(2,1)S(1)} %get-tuple-element.22), channel_id=1, source_target_pairs={{0,8},{1,9},{2,10},{3,11},{4,12},{5,13},{6,14},{7,15},{8,0},{9,1},... | collective-permute-start | bytes 393224 | tf_op jit(solution)/shard_map/ppermute | solution.py:29
  25.9 6.7 %slice-start.1 = ((s8[8388608]{0:T(1024)(128)(4,1)}), s8[4194304]{0:T(1024)(128)(4,1)S(1)}, s32[]{:S(2)}) async-start(s8[8388608]{0:T(1024)(128)(4,1)} %bitcast.13), calls=%async_computation.1 | async-start | bytes 8388608
  33.4 4.8 %collective-permute-start.12 = (bf16[64,2048]{1,0:T(8,128)(2,1)S(1)}, bf16[64,2048]{1,0:T(8,128)(2,1)S(1)}, u32[]{:S(2)}, u32[]{:S(2)}) collective-permute-start(bf16[64,2048]{1,0:T(8,128)(2,1)S(1)} %shard_map.59), channel_id=1, source_target_pairs={{0,1},{1,0},{2,3},{3,2},{4,5},{5,4},{6,7},{7,6},{8,9},{9,8},{10,11... | collective-permute-start | bytes 786440 | tf_op jit(solution)/shard_map/ppermute | solution.py:29
  38.3 8.8 %collective-permute-start.15 = (bf16[64,2048]{1,0:T(8,128)(2,1)S(1)}, bf16[64,2048]{1,0:T(8,128)(2,1)S(1)}, u32[]{:S(2)}, u32[]{:S(2)}) collective-permute-start(bf16[64,2048]{1,0:T(8,128)(2,1)S(1)} %add_convert_fusion.1), channel_id=1, source_target_pairs={{0,18},{1,19},{2,16},{3,17},{4,22},{5,23},{6,20},{7,21},{8,26},{9,... | collective-permute-start | bytes 786440 | tf_op jit(solution)/shard_map/ppermute | solution.py:29
  44.4 1.7 %collective-permute-start.13 = (bf16[64,1024]{1,0:T(8,128)(2,1)S(1)}, bf16[64,1024]{1,0:T(8,128)(2,1)S(1)}, u32[]{:S(2)}, u32[]{:S(2)}) collective-permute-start(bf16[64,1024]{1,0:T(8,128)(2,1)S(1)} %get-tuple-element.28), channel_id=1, source_target_pairs={{0,1},{1,0},{2,3},{3,2},{4,5},{5,4},{6,7},{7,6},{8,9},{9,8},{10,11... | collective-permute-start | bytes 393224 | tf_op jit(solution)/shard_map/ppermute | solution.py:29
  45.1 1.3 %collective-permute-start.14 = (bf16[64,1024]{1,0:T(8,128)(2,1)S(1)}, bf16[64,1024]{1,0:T(8,128)(2,1)S(1)}, u32[]{:S(2)}, u32[]{:S(2)}) collective-permute-start(bf16[64,1024]{1,0:T(8,128)(2,1)S(1)} %get-tuple-element.29), channel_id=1, source_target_pairs={{0,1},{1,0},{2,3},{3,2},{4,5},{5,4},{6,7},{7,6},{8,9},{9,8},{10,11... | collective-permute-start | bytes 393224 | tf_op jit(solution)/shard_map/ppermute | solution.py:29
  47.2 8.2 %collective-permute-start.16 = (bf16[64,2048]{1,0:T(8,128)(2,1)S(1)}, bf16[64,2048]{1,0:T(8,128)(2,1)S(1)}, u32[]{:S(2)}, u32[]{:S(2)}) collective-permute-start(bf16[64,2048]{1,0:T(8,128)(2,1)S(1)} %add_convert_fusion.refs_0_), channel_id=1, source_target_pairs={{0,2},{1,3},{2,0},{3,1},{4,6},{5,7},{6,4},{7,5},{8,10},{9,11},{10,... | collective-permute-start | bytes 786440 | tf_op jit(solution)/shard_map/ppermute | solution.py:29
  48.8 8.7 %collective-permute-start.17 = (bf16[64,2048]{1,0:T(8,128)(2,1)S(1)}, bf16[64,2048]{1,0:T(8,128)(2,1)S(1)}, u32[]{:S(2)}, u32[]{:S(2)}) collective-permute-start(bf16[64,2048]{1,0:T(8,128)(2,1)S(1)} %add_convert_fusion.refs_0_), channel_id=1, source_target_pairs={{0,1},{1,0},{2,3},{3,2},{4,5},{5,4},{6,7},{7,6},{8,9},{9,8},{10,11... | collective-permute-start | bytes 786440 | tf_op jit(solution)/shard_map/ppermute | solution.py:29
  55.4 3.3 %collective-permute-start.18 = (bf16[64,2048]{1,0:T(8,128)(2,1)S(1)}, bf16[64,2048]{1,0:T(8,128)(2,1)S(1)}, u32[]{:S(2)}, u32[]{:S(2)}) collective-permute-start(bf16[64,2048]{1,0:T(8,128)(2,1)S(1)} %collective-permute-done.16.refs_1_), channel_id=1, source_target_pairs={{0,1},{1,0},{2,3},{3,2},{4,5},{5,4},{6,7},{7,6},{8,9},{9,8},{10,11... | collective-permute-start | bytes 786440 | tf_op jit(solution)/shard_map/ppermute | solution.py:29

commit v9 on v8

--- a/solution.py
+++ b/solution.py
@@ -204,7 +204,8 @@
     mine, theirs = lax.optimization_barrier((pick(pair, batch), pick(pair, 1 - batch)))
     theirs = swap_x(theirs)
     unit = jnp.concatenate([jnp.where(x == 0, mine, theirs), jnp.where(x == 0, theirs, mine)], axis=1)
-    back = [unit] + [shift_z(unit, by) for by in (1, 2, 3, 4)]
+    moved = {by: shift_z(unit, by) for by in (3, 4, 2, 1)}
+    back = [unit] + [moved[by] for by in (1, 2, 3, 4)]
     near = jnp.concatenate(back[:3], axis=1)
     near_sent = jnp.concatenate([back[0][:, :block], back[1], back[2]], axis=1)
     near_all = [near] + [shift_y(near_sent, by) for by in COLUMNS_BACK[1:]]

time: 60 us -> 60 us (level)
  no operation moved by 1% of the time
where the time goes in v9:
time: 60 us; the launch traced here: 59.8 us
  starting transfers between devices  33.2 us (55%)
  waiting for transfers between devices  13 us (22%)
  Pallas kernels  10.9 us (18%)
  other arithmetic  1.2 us (2%)
  local copies, waits for them, and re-layouts  1.09 us (2%)
    ppermute x19, starting transfers between devices, shift(): lax.ppermute(array, AXES, [(flat(*d), flat(*move(*d))) for d in devices])  33.2 us
    ppermute x19, waiting for transfers between devices, shift(): lax.ppermute(array, AXES, [(flat(*d), flat(*move(*d))) for d in devices])  13 us
    pallas_call x1, Pallas kernels, body(): pl.pallas_call(functools.partial(far_project_kernel, heads, size, block),...  3.55 us
    pallas_call x1, Pallas kernels, body(): pl.pallas_call(functools.partial(near_kernel, heads, size, block), out_sh...  3.28 us
    pallas_call x2, Pallas kernels, projected(): pl.pallas_call(functools.partial(project_kernel, own_half), out_shape=jax...  1.68 us
    pallas_call x1, Pallas kernels, body(): pl.pallas_call(functools.partial(far_kernel, heads, size, block), out_sha...  1.31 us
  transfers between devices with their start and end apart: 19, of which 9 were waited for; matrix products, arithmetic and copies ran while one was open for 2% of the time, Pallas kernels for 13%

profile of v9, /device:TPU:1, one launch (start us, length us, event | category | flops | bytes accessed | tf_op | source)
XLA Modules:
  0.0 59.8 jit_solution(8368890354747873323)
XLA Ops:
  0.0 0.8 %fusion.1 = (bf16[2,64,128]{2,1,0:T(8,128)(2,1)S(1)}, bf16[2,64,128]{2,1,0:T(8,128)(2,1)S(1)}) fusion(s32[]{:T(128)S(6)} %select_n.65, bf16[2,1,64,128]{3,2,0,1:T(8,128)(2,1)} %bitcast.16, bf16[2,1,64,128]{3,2,0,1:T(8,128)(2,1)} %bitcast.17, s32[]{:T(128)S(6)} %select_n.61), kind=kLoop, calls=%fused_computation.14 | loop fusion | flops 32768 | bytes 131080 | tf_op jit(solution)/shard_map/jit(dynamic_index_in_dim)/squeeze | solution.py:201
  0.8 2.1 %collective-permute-start.1 = (bf16[2,64,128]{2,1,0:T(8,128)(2,1)S(1)}, bf16[2,64,128]{2,1,0:T(8,128)(2,1)S(1)}, u32[]{:S(2)}, u32[]{:S(2)}) collective-permute-start(bf16[2,64,128]{2,1,0:T(8,128)(2,1)S(1)} %get-tuple-element.19), channel_id=1, source_target_pairs={{0,16},{1,17},{2,18},{3,19},{4,20},{5,21},{6,22},{7,23},{8,24},{9,... | collective-permute-start | bytes 98312 | tf_op jit(solution)/shard_map/ppermute | solution.py:29
  2.9 1.0 %dynamic-slice_bitcast_fusion = (bf16[64,1024]{1,0:T(8,128)(2,1)S(1)}, bf16[64,1024]{1,0:T(8,128)(2,1)S(1)}) fusion(bf16[2,64,1024]{2,1,0:T(8,128)(2,1)} %param.5, s32[]{:T(128)S(6)} %select_n.61, s32[]{:T(128)S(6)} %select_n.65), kind=kLoop, calls=%fused_computation.4 | loop fusion | bytes 524296 | tf_op jit(solution)/shard_map/jit(dynamic_index_in_dim)/squeeze | solution.py:201
  3.9 0.1 collective-permute-start
  4.1 0.1 convert_reduce_fusion
  4.2 0.0 collective-permute-done.1
  4.3 3.3 %collective-permute-start.8 = (bf16[2,128,128]{2,1,0:T(8,128)(2,1)S(1)}, bf16[2,128,128]{2,1,0:T(8,128)(2,1)S(1)}, u32[]{:S(2)}, u32[]{:S(2)}) collective-permute-start(bf16[2,128,128]{2,1,0:T(8,128)(2,1)S(1)} %pad_maximum_fusion.2.unit_ref), channel_id=1, source_target_pairs={{0,64},{1,65},{2,66},{3,67},{4,68},{5,69},{6,70},{7,71},{8,72},{9,... | collective-permute-start | bytes 196616 | tf_op jit(solution)/shard_map/ppermute | solution.py:29
  7.6 1.6 %collective-permute-start.7 = (bf16[2,128,128]{2,1,0:T(8,128)(2,1)S(1)}, bf16[2,128,128]{2,1,0:T(8,128)(2,1)S(1)}, u32[]{:S(2)}, u32[]{:S(2)}) collective-permute-start(bf16[2,128,128]{2,1,0:T(8,128)(2,1)S(1)} %pad_maximum_fusion.2.unit_ref), channel_id=1, source_target_pairs={{0,32},{1,33},{2,34},{3,35},{4,36},{5,37},{6,38},{7,39},{8,40},{9,... | collective-permute-start | bytes 196616 | tf_op jit(solution)/shard_map/ppermute | solution.py:29
  9.2 4.2 %collective-permute-start.3 = (bf16[2,128,128]{2,1,0:T(8,128)(2,1)S(1)}, bf16[2,128,128]{2,1,0:T(8,128)(2,1)S(1)}, u32[]{:S(2)}, u32[]{:S(2)}) collective-permute-start(bf16[2,128,128]{2,1,0:T(8,128)(2,1)S(1)} %pad_maximum_fusion.2.unit_ref), channel_id=1, source_target_pairs={{0,128},{1,129},{2,130},{3,131},{4,132},{5,133},{6,134},{7,135},{8... | collective-permute-start | bytes 196616 | tf_op jit(solution)/shard_map/ppermute | solution.py:29
  13.4 0.0 collective-permute-start.2
  13.4 0.0 collective-permute-done.8
  13.4 0.0 slice-start
  13.5 3.0 %collective-permute-start.11 = (bf16[2,320,128]{2,1,0:T(8,128)(2,1)S(1)}, bf16[2,320,128]{2,1,0:T(8,128)(2,1)S(1)}, u32[]{:S(2)}, u32[]{:S(2)}) collective-permute-start(bf16[2,320,128]{2,1,0:T(8,128)(2,1)S(1)} %pad_maximum_fusion.1), channel_id=1, source_target_pairs={{0,8},{1,9},{2,10},{3,11},{4,12},{5,13},{6,14},{7,15},{8,0},{9,1},... | collective-permute-start | bytes 491528 | tf_op jit(solution)/shard_map/ppermute | solution.py:29
  16.5 0.8 %collective-permute-start.10 = (bf16[2,320,128]{2,1,0:T(8,128)(2,1)S(1)}, bf16[2,320,128]{2,1,0:T(8,128)(2,1)S(1)}, u32[]{:S(2)}, u32[]{:S(2)}) collective-permute-start(bf16[2,320,128]{2,1,0:T(8,128)(2,1)S(1)} %pad_maximum_fusion.1), channel_id=1, source_target_pairs={{0,12},{1,13},{2,14},{3,15},{4,0},{5,1},{6,2},{7,3},{8,4},{9,5},{1... | collective-permute-start | bytes 491528 | tf_op jit(solution)/shard_map/ppermute | solution.py:29
  17.2 0.1 collective-permute-done.3.fourth_ref
  17.3 1.3 %collective-permute-start.9 = (bf16[2,320,128]{2,1,0:T(8,128)(2,1)S(1)}, bf16[2,320,128]{2,1,0:T(8,128)(2,1)S(1)}, u32[]{:S(2)}, u32[]{:S(2)}) collective-permute-start(bf16[2,320,128]{2,1,0:T(8,128)(2,1)S(1)} %pad_maximum_fusion.1), channel_id=1, source_target_pairs={{0,4},{1,5},{2,6},{3,7},{4,8},{5,9},{6,10},{7,11},{8,12},{9,13},{1... | collective-permute-start | bytes 491528 | tf_op jit(solution)/shard_map/ppermute | solution.py:29
  18.6 0.1 select_reduce_fusion
  18.7 2.4 %collective-permute-done.2.third_ref = bf16[2,128,128]{2,1,0:T(8,128)(2,1)S(1)} collective-permute-done((bf16[2,128,128]{2,1,0:T(8,128)(2,1)S(1)}, bf16[2,128,128]{2,1,0:T(8,128)(2,1)S(1)}, u32[]{:S(2)}, u32[]{:S(2)}) %collective-permute-start.2) | collective-permute-done | bytes 65568 | tf_op jit(solution)/shard_map/ppermute | solution.py:29
  21.2 0.1 shard_map.55
  21.2 1.4 %collective-permute-start.4 = (bf16[2,256,128]{2,1,0:T(8,128)(2,1)S(1)}, bf16[2,256,128]{2,1,0:T(8,128)(2,1)S(1)}, u32[]{:S(2)}, u32[]{:S(2)}) collective-permute-start(bf16[2,256,128]{2,1,0:T(8,128)(2,1)S(1)} %get-tuple-element.20), channel_id=1, source_target_pairs={{0,4},{1,5},{2,6},{3,7},{4,8},{5,9},{6,10},{7,11},{8,12},{9,13},{1... | collective-permute-start | bytes 393224 | tf_op jit(solution)/shard_map/ppermute | solution.py:29
  22.6 1.5 %collective-permute-start.5 = (bf16[2,256,128]{2,1,0:T(8,128)(2,1)S(1)}, bf16[2,256,128]{2,1,0:T(8,128)(2,1)S(1)}, u32[]{:S(2)}, u32[]{:S(2)}) collective-permute-start(bf16[2,256,128]{2,1,0:T(8,128)(2,1)S(1)} %get-tuple-element.21), channel_id=1, source_target_pairs={{0,12},{1,13},{2,14},{3,15},{4,0},{5,1},{6,2},{7,3},{8,4},{9,5},{1... | collective-permute-start | bytes 393224 | tf_op jit(solution)/shard_map/ppermute | solution.py:29
  24.2 0.0 collective-permute-done.11.k3
  24.2 1.6 %collective-permute-start.6 = (bf16[2,256,128]{2,1,0:T(8,128)(2,1)S(1)}, bf16[2,256,128]{2,1,0:T(8,128)(2,1)S(1)}, u32[]{:S(2)}, u32[]{:S(2)}) collective-permute-start(bf16[2,256,128]{2,1,0:T(8,128)(2,1)S(1)} %get-tuple-element.22), channel_id=1, source_target_pairs={{0,8},{1,9},{2,10},{3,11},{4,12},{5,13},{6,14},{7,15},{8,0},{9,1},... | collective-permute-start | bytes 393224 | tf_op jit(solution)/shard_map/ppermute | solution.py:29
  25.8 0.1 broadcast_in_dim.9.first_ref
  25.9 0.0 slice-start.1
  25.9 3.3 %shard_map.56 = (f32[2,64,1024]{2,1,0:T(8,128)S(1)}, f32[2,64,128]{2,1,0:T(8,128)S(1)}) custom-call(s32[2,64,128]{2,1,0:T(8,128)S(1)} %broadcast_in_dim.9.first_ref, bf16[64,1024]{1,0:T(8,128)(2,1)S(1)} %get-tuple-element.26.own_ref.query_ref, bf16[64,1024]{1,0:T(8,128)(2,1)S(1)} %collective-permute-done.other_ref.query_ref, ...), custom_call_target="tpu_custom_call" | custom-call | flops 17179869184 | bytes 16777216 | tf_op jit(solution)/shard_map/pallas_call | solution.py:229
  29.2 0.0 collective-permute-done.4.k1
  29.2 0.0 collective-permute-done.5.k2
  29.2 2.0 %collective-permute-done.6.k3 = bf16[2,256,128]{2,1,0:T(8,128)(2,1)S(1)} collective-permute-done((bf16[2,256,128]{2,1,0:T(8,128)(2,1)S(1)}, bf16[2,256,128]{2,1,0:T(8,128)(2,1)S(1)}, u32[]{:S(2)}, u32[]{:S(2)}) %collective-permute-start.6) | collective-permute-done | bytes 131104 | tf_op jit(solution)/shard_map/ppermute | solution.py:29
  31.2 1.3 %shard_map.57.context_ref = bf16[64,1024]{1,0:T(8,128)(2,1)S(1)} custom-call(s32[2,64,128]{2,1,0:T(8,128)S(1)} %broadcast_in_dim.9.first_ref, bf16[64,1024]{1,0:T(8,128)(2,1)S(1)} %collective-permute-done.other_ref.query_ref, bf16[2,256,128]{2,1,0:T(8,128)(2,1)S(1)} %collective-permute-done.4.k1, bf16[2,256,128]{2,1,0:T(8,128)(2,1)S(1)} %collective-permute-done.5.k2, ...), custom_call_target="tpu_custom_call" | custom-call | tf_op jit(solution)/shard_map/pallas_call | solution.py:241
  32.6 0.8 %shard_map.59 = bf16[64,2048]{1,0:T(8,128)(2,1)S(1)} custom-call(bf16[64,1024]{1,0:T(8,128)(2,1)S(1)} %shard_map.57.context_ref, bf16[1024,4096]{1,0:T(8,128)(2,1)S(1)} %bitcast.14), custom_call_target="tpu_custom_call" | custom-call | tf_op jit(solution)/shard_map/pallas_call | solution.py:250
  33.4 3.6 %collective-permute-start.12 = (bf16[64,2048]{1,0:T(8,128)(2,1)S(1)}, bf16[64,2048]{1,0:T(8,128)(2,1)S(1)}, u32[]{:S(2)}, u32[]{:S(2)}) collective-permute-start(bf16[64,2048]{1,0:T(8,128)(2,1)S(1)} %shard_map.59), channel_id=1, source_target_pairs={{0,1},{1,0},{2,3},{3,2},{4,5},{5,4},{6,7},{7,6},{8,9},{9,8},{10,11... | collective-permute-start | bytes 786440 | tf_op jit(solution)/shard_map/ppermute | solution.py:29
  37.0 0.8 %shard_map.58 = f32[64,2048]{1,0:T(8,128)S(1)} custom-call(bf16[64,1024]{1,0:T(8,128)(2,1)S(1)} %shard_map.57.context_ref, bf16[1024,4096]{1,0:T(8,128)(2,1)S(1)} %bitcast.14), custom_call_target="tpu_custom_call" | custom-call | tf_op jit(solution)/shard_map/pallas_call | solution.py:250
  37.9 0.3 collective-permute-done.12
  38.3 2.6 %collective-permute-start.15 = (bf16[64,2048]{1,0:T(8,128)(2,1)S(1)}, bf16[64,2048]{1,0:T(8,128)(2,1)S(1)}, u32[]{:S(2)}, u32[]{:S(2)}) collective-permute-start(bf16[64,2048]{1,0:T(8,128)(2,1)S(1)} %add_convert_fusion.1), channel_id=1, source_target_pairs={{0,18},{1,19},{2,16},{3,17},{4,22},{5,23},{6,20},{7,21},{8,26},{9,... | collective-permute-start | bytes 786440 | tf_op jit(solution)/shard_map/ppermute | solution.py:29
  40.8 3.5 %shard_map.60 = (bf16[64,1024]{1,0:T(8,128)(2,1)S(1)}, bf16[64,1024]{1,0:T(8,128)(2,1)S(1)}, f32[64,2048]{1,0:T(8,128)S(1)}) custom-call(s32[2,64,128]{2,1,0:T(8,128)S(1)} %broadcast_in_dim.9.first_ref, bf16[64,1024]{1,0:T(8,128)(2,1)S(1)} %get-tuple-element.26.own_ref.query_ref, bf16[2,256,128]{2,1,0:T(8,128)(2,1)S(1)} %collective-permute-done.4.k1, ...), custom_call_target="tpu_custom_call" | custom-call | tf_op jit(solution)/shard_map/pallas_call | solution.py:265
  44.4 0.7 %collective-permute-start.13 = (bf16[64,1024]{1,0:T(8,128)(2,1)S(1)}, bf16[64,1024]{1,0:T(8,128)(2,1)S(1)}, u32[]{:S(2)}, u32[]{:S(2)}) collective-permute-start(bf16[64,1024]{1,0:T(8,128)(2,1)S(1)} %get-tuple-element.28), channel_id=1, source_target_pairs={{0,1},{1,0},{2,3},{3,2},{4,5},{5,4},{6,7},{7,6},{8,9},{9,8},{10,11... | collective-permute-start | bytes 393224 | tf_op jit(solution)/shard_map/ppermute | solution.py:29
  45.1 0.1 collective-permute-start.14
  45.2 0.9 %collective-permute-done.13 = bf16[64,1024]{1,0:T(8,128)(2,1)S(1)} collective-permute-done((bf16[64,1024]{1,0:T(8,128)(2,1)S(1)}, bf16[64,1024]{1,0:T(8,128)(2,1)S(1)}, u32[]{:S(2)}, u32[]{:S(2)}) %collective-permute-start.13) | collective-permute-done | bytes 131104 | tf_op jit(solution)/shard_map/ppermute | solution.py:29
  46.1 0.4 collective-permute-done.14
  46.5 0.6 %collective-permute-done.15 = bf16[64,2048]{1,0:T(8,128)(2,1)S(1)} collective-permute-done((bf16[64,2048]{1,0:T(8,128)(2,1)S(1)}, bf16[64,2048]{1,0:T(8,128)(2,1)S(1)}, u32[]{:S(2)}, u32[]{:S(2)}) %collective-permute-start.15) | collective-permute-done | bytes 262176 | tf_op jit(solution)/shard_map/ppermute | solution.py:29
  47.1 0.1 add_convert_fusion.refs_0_
  47.2 1.6 %collective-permute-start.16 = (bf16[64,2048]{1,0:T(8,128)(2,1)S(1)}, bf16[64,2048]{1,0:T(8,128)(2,1)S(1)}, u32[]{:S(2)}, u32[]{:S(2)}) collective-permute-start(bf16[64,2048]{1,0:T(8,128)(2,1)S(1)} %add_convert_fusion.refs_0_), channel_id=1, source_target_pairs={{0,2},{1,3},{2,0},{3,1},{4,6},{5,7},{6,4},{7,5},{8,10},{9,11},{10,... | collective-permute-start | bytes 786440 | tf_op jit(solution)/shard_map/ppermute | solution.py:29
  48.8 1.5 %collective-permute-start.17 = (bf16[64,2048]{1,0:T(8,128)(2,1)S(1)}, bf16[64,2048]{1,0:T(8,128)(2,1)S(1)}, u32[]{:S(2)}, u32[]{:S(2)}) collective-permute-start(bf16[64,2048]{1,0:T(8,128)(2,1)S(1)} %add_convert_fusion.refs_0_), channel_id=1, source_target_pairs={{0,1},{1,0},{2,3},{3,2},{4,5},{5,4},{6,7},{7,6},{8,9},{9,8},{10,11... | collective-permute-start | bytes 786440 | tf_op jit(solution)/shard_map/ppermute | solution.py:29
  50.3 5.1 %collective-permute-done.16.refs_1_ = bf16[64,2048]{1,0:T(8,128)(2,1)S(1)} collective-permute-done((bf16[64,2048]{1,0:T(8,128)(2,1)S(1)}, bf16[64,2048]{1,0:T(8,128)(2,1)S(1)}, u32[]{:S(2)}, u32[]{:S(2)}) %collective-permute-start.16) | collective-permute-done | bytes 262176 | tf_op jit(solution)/shard_map/ppermute | solution.py:29
  55.4 2.1 %collective-permute-start.18 = (bf16[64,2048]{1,0:T(8,128)(2,1)S(1)}, bf16[64,2048]{1,0:T(8,128)(2,1)S(1)}, u32[]{:S(2)}, u32[]{:S(2)}) collective-permute-start(bf16[64,2048]{1,0:T(8,128)(2,1)S(1)} %collective-permute-done.16.refs_1_), channel_id=1, source_target_pairs={{0,1},{1,0},{2,3},{3,2},{4,5},{5,4},{6,7},{7,6},{8,9},{9,8},{10,11... | collective-permute-start | bytes 786440 | tf_op jit(solution)/shard_map/ppermute | solution.py:29
  57.5 1.2 %collective-permute-done.18.refs_3_ = bf16[64,2048]{1,0:T(8,128)(2,1)S(1)} collective-permute-done((bf16[64,2048]{1,0:T(8,128)(2,1)S(1)}, bf16[64,2048]{1,0:T(8,128)(2,1)S(1)}, u32[]{:S(2)}, u32[]{:S(2)}) %collective-permute-start.18) | collective-permute-done | bytes 262176 | tf_op jit(solution)/shard_map/ppermute | solution.py:29
  58.6 1.0 %shard_map.61 = bf16[2,64,4096]{2,1,0:T(8,128)(2,1)} custom-call(bf16[64,2048]{1,0:T(8,128)(2,1)S(1)} %add_convert_fusion.refs_0_, bf16[64,2048]{1,0:T(8,128)(2,1)S(1)} %collective-permute-done.16.refs_1_, bf16[64,2048]{1,0:T(8,128)(2,1)S(1)} %collective-permute-done.17.refs_2_, bf16[64,2048]{1,0:T(8,128)(2,1)S(1)} %collective-permute-done.18.refs_3_), custom_call_target="tpu_custom_call" | custom-call | tf_op jit(solution)/shard_map/pallas_call | solution.py:284
  (18 shorter events, 0.1 us)
Async XLA Ops:
  0.0 4.0 %copy-start = (s32[2,4096]{1,0:T(2,128)S(1)}, s32[2,4096]{1,0:T(2,128)}, u32[]{:S(2)}) copy-start(s32[2,4096]{1,0:T(2,128)} %param.8) | copy-start | bytes 98308
  0.8 3.4 %collective-permute-start.1 = (bf16[2,64,128]{2,1,0:T(8,128)(2,1)S(1)}, bf16[2,64,128]{2,1,0:T(8,128)(2,1)S(1)}, u32[]{:S(2)}, u32[]{:S(2)}) collective-permute-start(bf16[2,64,128]{2,1,0:T(8,128)(2,1)S(1)} %get-tuple-element.19), channel_id=1, source_target_pairs={{0,16},{1,17},{2,18},{3,19},{4,20},{5,21},{6,22},{7,23},{8,24},{9,... | collective-permute-start | bytes 98312 | tf_op jit(solution)/shard_map/ppermute | solution.py:29
  3.9 18.7 %collective-permute-start = (bf16[64,1024]{1,0:T(8,128)(2,1)S(1)}, bf16[64,1024]{1,0:T(8,128)(2,1)S(1)}, u32[]{:S(2)}, u32[]{:S(2)}) collective-permute-start(bf16[64,1024]{1,0:T(8,128)(2,1)S(1)} %get-tuple-element.32), channel_id=1, source_target_pairs={{0,16},{1,17},{2,18},{3,19},{4,20},{5,21},{6,22},{7,23},{8,24},{9,... | collective-permute-start | bytes 393224 | tf_op jit(solution)/shard_map/ppermute | solution.py:29
  4.3 9.2 %collective-permute-start.8 = (bf16[2,128,128]{2,1,0:T(8,128)(2,1)S(1)}, bf16[2,128,128]{2,1,0:T(8,128)(2,1)S(1)}, u32[]{:S(2)}, u32[]{:S(2)}) collective-permute-start(bf16[2,128,128]{2,1,0:T(8,128)(2,1)S(1)} %pad_maximum_fusion.2.unit_ref), channel_id=1, source_target_pairs={{0,64},{1,65},{2,66},{3,67},{4,68},{5,69},{6,70},{7,71},{8,72},{9,... | collective-permute-start | bytes 196616 | tf_op jit(solution)/shard_map/ppermute | solution.py:29
  7.6 5.9 %collective-permute-start.7 = (bf16[2,128,128]{2,1,0:T(8,128)(2,1)S(1)}, bf16[2,128,128]{2,1,0:T(8,128)(2,1)S(1)}, u32[]{:S(2)}, u32[]{:S(2)}) collective-permute-start(bf16[2,128,128]{2,1,0:T(8,128)(2,1)S(1)} %pad_maximum_fusion.2.unit_ref), channel_id=1, source_target_pairs={{0,32},{1,33},{2,34},{3,35},{4,36},{5,37},{6,38},{7,39},{8,40},{9,... | collective-permute-start | bytes 196616 | tf_op jit(solution)/shard_map/ppermute | solution.py:29
  9.2 8.1 %collective-permute-start.3 = (bf16[2,128,128]{2,1,0:T(8,128)(2,1)S(1)}, bf16[2,128,128]{2,1,0:T(8,128)(2,1)S(1)}, u32[]{:S(2)}, u32[]{:S(2)}) collective-permute-start(bf16[2,128,128]{2,1,0:T(8,128)(2,1)S(1)} %pad_maximum_fusion.2.unit_ref), channel_id=1, source_target_pairs={{0,128},{1,129},{2,130},{3,131},{4,132},{5,133},{6,134},{7,135},{8... | collective-permute-start | bytes 196616 | tf_op jit(solution)/shard_map/ppermute | solution.py:29
  13.4 7.8 %collective-permute-start.2 = (bf16[2,128,128]{2,1,0:T(8,128)(2,1)S(1)}, bf16[2,128,128]{2,1,0:T(8,128)(2,1)S(1)}, u32[]{:S(2)}, u32[]{:S(2)}) collective-permute-start(bf16[2,128,128]{2,1,0:T(8,128)(2,1)S(1)} %pad_maximum_fusion.2.unit_ref), channel_id=1, source_target_pairs={{0,96},{1,97},{2,98},{3,99},{4,100},{5,101},{6,102},{7,103},{8,104... | collective-permute-start | bytes 196616 | tf_op jit(solution)/shard_map/ppermute | solution.py:29
  13.4 19.1 %slice-start = ((s8[8388608]{0:T(1024)(128)(4,1)}), s8[4194304]{0:T(1024)(128)(4,1)S(1)}, s32[]{:S(2)}) async-start(s8[8388608]{0:T(1024)(128)(4,1)} %bitcast.13), calls=%async_computation | async-start | bytes 8388608
  13.5 10.7 %collective-permute-start.11 = (bf16[2,320,128]{2,1,0:T(8,128)(2,1)S(1)}, bf16[2,320,128]{2,1,0:T(8,128)(2,1)S(1)}, u32[]{:S(2)}, u32[]{:S(2)}) collective-permute-start(bf16[2,320,128]{2,1,0:T(8,128)(2,1)S(1)} %pad_maximum_fusion.1), channel_id=1, source_target_pairs={{0,8},{1,9},{2,10},{3,11},{4,12},{5,13},{6,14},{7,15},{8,0},{9,1},... | collective-permute-start | bytes 491528 | tf_op jit(solution)/shard_map/ppermute | solution.py:29
  16.5 9.4 %collective-permute-start.10 = (bf16[2,320,128]{2,1,0:T(8,128)(2,1)S(1)}, bf16[2,320,128]{2,1,0:T(8,128)(2,1)S(1)}, u32[]{:S(2)}, u32[]{:S(2)}) collective-permute-start(bf16[2,320,128]{2,1,0:T(8,128)(2,1)S(1)} %pad_maximum_fusion.1), channel_id=1, source_target_pairs={{0,12},{1,13},{2,14},{3,15},{4,0},{5,1},{6,2},{7,3},{8,4},{9,5},{1... | collective-permute-start | bytes 491528 | tf_op jit(solution)/shard_map/ppermute | solution.py:29
  17.3 8.5 %collective-permute-start.9 = (bf16[2,320,128]{2,1,0:T(8,128)(2,1)S(1)}, bf16[2,320,128]{2,1,0:T(8,128)(2,1)S(1)}, u32[]{:S(2)}, u32[]{:S(2)}) collective-permute-start(bf16[2,320,128]{2,1,0:T(8,128)(2,1)S(1)} %pad_maximum_fusion.1), channel_id=1, source_target_pairs={{0,4},{1,5},{2,6},{3,7},{4,8},{5,9},{6,10},{7,11},{8,12},{9,13},{1... | collective-permute-start | bytes 491528 | tf_op jit(solution)/shard_map/ppermute | solution.py:29
  21.2 7.9 %collective-permute-start.4 = (bf16[2,256,128]{2,1,0:T(8,128)(2,1)S(1)}, bf16[2,256,128]{2,1,0:T(8,128)(2,1)S(1)}, u32[]{:S(2)}, u32[]{:S(2)}) collective-permute-start(bf16[2,256,128]{2,1,0:T(8,128)(2,1)S(1)} %get-tuple-element.20), channel_id=1, source_target_pairs={{0,4},{1,5},{2,6},{3,7},{4,8},{5,9},{6,10},{7,11},{8,12},{9,13},{1... | collective-permute-start | bytes 393224 | tf_op jit(solution)/shard_map/ppermute | solution.py:29
  22.6 6.6 %collective-permute-start.5 = (bf16[2,256,128]{2,1,0:T(8,128)(2,1)S(1)}, bf16[2,256,128]{2,1,0:T(8,128)(2,1)S(1)}, u32[]{:S(2)}, u32[]{:S(2)}) collective-permute-start(bf16[2,256,128]{2,1,0:T(8,128)(2,1)S(1)} %get-tuple-element.21), channel_id=1, source_target_pairs={{0,12},{1,13},{2,14},{3,15},{4,0},{5,1},{6,2},{7,3},{8,4},{9,5},{1... | collective-permute-start | bytes 393224 | tf_op jit(solution)/shard_map/ppermute | solution.py:29
  24.2 7.1 %collective-permute-start.6 = (bf16[2,256,128]{2,1,0:T(8,128)(2,1)S(1)}, bf16[2,256,128]{2,1,0:T(8,128)(2,1)S(1)}, u32[]{:S(2)}, u32[]{:S(2)}) collective-permute-start(bf16[2,256,128]{2,1,0:T(8,128)(2,1)S(1)} %get-tuple-element.22), channel_id=1, source_target_pairs={{0,8},{1,9},{2,10},{3,11},{4,12},{5,13},{6,14},{7,15},{8,0},{9,1},... | collective-permute-start | bytes 393224 | tf_op jit(solution)/shard_map/ppermute | solution.py:29
  25.9 6.7 %slice-start.1 = ((s8[8388608]{0:T(1024)(128)(4,1)}), s8[4194304]{0:T(1024)(128)(4,1)S(1)}, s32[]{:S(2)}) async-start(s8[8388608]{0:T(1024)(128)(4,1)} %bitcast.13), calls=%async_computation.1 | async-start | bytes 8388608
  33.4 4.8 %collective-permute-start.12 = (bf16[64,2048]{1,0:T(8,128)(2,1)S(1)}, bf16[64,2048]{1,0:T(8,128)(2,1)S(1)}, u32[]{:S(2)}, u32[]{:S(2)}) collective-permute-start(bf16[64,2048]{1,0:T(8,128)(2,1)S(1)} %shard_map.59), channel_id=1, source_target_pairs={{0,1},{1,0},{2,3},{3,2},{4,5},{5,4},{6,7},{7,6},{8,9},{9,8},{10,11... | collective-permute-start | bytes 786440 | tf_op jit(solution)/shard_map/ppermute | solution.py:29
  38.3 8.8 %collective-permute-start.15 = (bf16[64,2048]{1,0:T(8,128)(2,1)S(1)}, bf16[64,2048]{1,0:T(8,128)(2,1)S(1)}, u32[]{:S(2)}, u32[]{:S(2)}) collective-permute-start(bf16[64,2048]{1,0:T(8,128)(2,1)S(1)} %add_convert_fusion.1), channel_id=1, source_target_pairs={{0,18},{1,19},{2,16},{3,17},{4,22},{5,23},{6,20},{7,21},{8,26},{9,... | collective-permute-start | bytes 786440 | tf_op jit(solution)/shard_map/ppermute | solution.py:29
  44.4 1.7 %collective-permute-start.13 = (bf16[64,1024]{1,0:T(8,128)(2,1)S(1)}, bf16[64,1024]{1,0:T(8,128)(2,1)S(1)}, u32[]{:S(2)}, u32[]{:S(2)}) collective-permute-start(bf16[64,1024]{1,0:T(8,128)(2,1)S(1)} %get-tuple-element.28), channel_id=1, source_target_pairs={{0,1},{1,0},{2,3},{3,2},{4,5},{5,4},{6,7},{7,6},{8,9},{9,8},{10,11... | collective-permute-start | bytes 393224 | tf_op jit(solution)/shard_map/ppermute | solution.py:29
  45.1 1.3 %collective-permute-start.14 = (bf16[64,1024]{1,0:T(8,128)(2,1)S(1)}, bf16[64,1024]{1,0:T(8,128)(2,1)S(1)}, u32[]{:S(2)}, u32[]{:S(2)}) collective-permute-start(bf16[64,1024]{1,0:T(8,128)(2,1)S(1)} %get-tuple-element.29), channel_id=1, source_target_pairs={{0,1},{1,0},{2,3},{3,2},{4,5},{5,4},{6,7},{7,6},{8,9},{9,8},{10,11... | collective-permute-start | bytes 393224 | tf_op jit(solution)/shard_map/ppermute | solution.py:29
  47.2 8.2 %collective-permute-start.16 = (bf16[64,2048]{1,0:T(8,128)(2,1)S(1)}, bf16[64,2048]{1,0:T(8,128)(2,1)S(1)}, u32[]{:S(2)}, u32[]{:S(2)}) collective-permute-start(bf16[64,2048]{1,0:T(8,128)(2,1)S(1)} %add_convert_fusion.refs_0_), channel_id=1, source_target_pairs={{0,2},{1,3},{2,0},{3,1},{4,6},{5,7},{6,4},{7,5},{8,10},{9,11},{10,... | collective-permute-start | bytes 786440 | tf_op jit(solution)/shard_map/ppermute | solution.py:29
  48.8 8.7 %collective-permute-start.17 = (bf16[64,2048]{1,0:T(8,128)(2,1)S(1)}, bf16[64,2048]{1,0:T(8,128)(2,1)S(1)}, u32[]{:S(2)}, u32[]{:S(2)}) collective-permute-start(bf16[64,2048]{1,0:T(8,128)(2,1)S(1)} %add_convert_fusion.refs_0_), channel_id=1, source_target_pairs={{0,1},{1,0},{2,3},{3,2},{4,5},{5,4},{6,7},{7,6},{8,9},{9,8},{10,11... | collective-permute-start | bytes 786440 | tf_op jit(solution)/shard_map/ppermute | solution.py:29
  55.4 3.3 %collective-permute-start.18 = (bf16[64,2048]{1,0:T(8,128)(2,1)S(1)}, bf16[64,2048]{1,0:T(8,128)(2,1)S(1)}, u32[]{:S(2)}, u32[]{:S(2)}) collective-permute-start(bf16[64,2048]{1,0:T(8,128)(2,1)S(1)} %collective-permute-done.16.refs_1_), channel_id=1, source_target_pairs={{0,1},{1,0},{2,3},{3,2},{4,5},{5,4},{6,7},{7,6},{8,9},{9,8},{10,11... | collective-permute-start | bytes 786440 | tf_op jit(solution)/shard_map/ppermute | solution.py:29
